TPU v7x, 256 devices: a whole 4x4x8 slice. The times are simulated.
256 devices in a mesh: dp: 32 (over z, x), tensor: 8 (over y, core).
Axes of the slice: x: 4, y: 4, z: 8, core: 2. Of those that a mesh axis runs over, the one named last changes fastest.
Arguments:
- hidden: bfloat16 [1024, 53248], P('dp', 'tensor'), may hold values from -6 to 6
- down_matrix: bfloat16 [53248, 16384], P('tensor', 'dp'), may hold values from -0.02734375 to 0.02734375
- down_factor_levels: bfloat16 [32, 64, 53248], P('dp', None, 'tensor'), may hold values from -127 to 127
- hidden_level_scale: float32 [32, 53248], P('dp', 'tensor'), as said below
- adapter_up_factors: bfloat16 [32, 64, 16384], P(None, None, 'dp'), may hold values from -0.75 to 0.75
- adapter_per_row: int32 [1024, 1], replicated, may hold values from 0 to 31; in each aligned block of 32 rows (0 to 31, 32 to 63, ...) at most 2 rows name the same one
Outputs:
- mixed: bfloat16 [1024, 16384], P('tensor', 'dp')
Inputs may be any that keep to these rules, and one draw needn't show every extreme that they name: `adapter_per_row`: in each aligned block of 32 rows (the rows of one index of dp) no adapter is named by more than 2 rows, a bound that some block reaches. `hidden_level_scale`: Positive.
All inputs are finite; a program needn't handle non-finite values.
Results may differ from a plain program's by a relative error of at most 0.0053.
Values may be sent and summed in bfloat16 or wider, within the bound.
No kernel may reach another device: no remote copies, remote signals or barrier semaphores. Data moves between devices by JAX's collectives and lax.ppermute only.
A program may use at most 64 MiB of HBM per device.

v0:
```python
import jax
import jax.numpy as jnp
from jax import lax
from jax.sharding import PartitionSpec as P


def project_rows(weight, piece):
    return jnp.dot(piece, weight, preferred_element_type=jnp.float32)


def shards(
    hidden, down_matrix, down_factor_levels, hidden_level_scale, adapter_up_factors, adapter_per_row
):
    rows_dev = hidden.shape[0]
    n_groups = lax.axis_size("dp")
    per_owner = max(2, 2 * rows_dev // n_groups)
    group_index = lax.axis_index("dp")
    adapters_all = adapter_per_row[:, 0]
    every_row_output = adapters_all.shape[0]
    rank_activations = down_factor_levels.shape[1]
    local_dense = (
        down_factor_levels[0].astype(jnp.float32) * hidden_level_scale[0][None, :]
    ).astype(jnp.bfloat16)
    base_projection = project_rows(down_matrix, lax.all_gather(hidden, "dp", axis=0, tiled=True))
    mine = lax.dynamic_slice_in_dim(adapters_all, group_index * rows_dev, rows_dev)
    row_order = jnp.arange(rows_dev, dtype=jnp.int32)
    earlier = (mine[:, None] == mine[None, :]) & (row_order[None, :] < row_order[:, None])
    position = jnp.sum(earlier.astype(jnp.int32), axis=1)
    slot_of = mine * per_owner + position
    slot_ids = jnp.arange(n_groups * per_owner, dtype=jnp.int32)
    select = (slot_ids[:, None] == slot_of[None, :]).astype(jnp.bfloat16)
    outgoing = jnp.dot(select, hidden, preferred_element_type=jnp.float32).astype(jnp.bfloat16)
    outgoing = outgoing.reshape(n_groups, per_owner, hidden.shape[1])
    shrunk = jnp.einsum(
        "smf,rf->smr",
        lax.all_to_all(outgoing, "dp", split_axis=0, concat_axis=0, tiled=True),
        local_dense,
        preferred_element_type=jnp.float32,
    ).astype(jnp.bfloat16)
    flat = shrunk.reshape(shrunk.shape[0], shrunk.shape[1] * shrunk.shape[2])
    returned = lax.all_to_all(flat, "dp", split_axis=0, concat_axis=0, tiled=True)
    returned = returned.reshape(n_groups * per_owner, rank_activations)
    own_rows = lax.dot_general(
        select, returned, (((0,), (0,)), ((), ())), preferred_element_type=jnp.float32
    ).astype(jnp.bfloat16)
    shrink_all = lax.all_gather(
        own_rows.reshape(rows_dev * rank_activations), "dp", axis=0, tiled=True
    ).reshape(every_row_output, rank_activations)
    adapter_index_list = jnp.arange(adapter_up_factors.shape[0], dtype=jnp.int32)
    chosen = adapters_all[:, None] == adapter_index_list[None, :]
    spread_rows = jnp.where(chosen[:, :, None], shrink_all[:, None, :], jnp.zeros((), jnp.bfloat16))
    spread_rows = spread_rows.reshape(
        every_row_output, adapter_up_factors.shape[0] * rank_activations
    )
    adapter_delta = jnp.dot(
        spread_rows,
        adapter_up_factors.reshape(
            adapter_up_factors.shape[0] * rank_activations, adapter_up_factors.shape[2]
        ),
        preferred_element_type=jnp.float32,
    )
    total_output = lax.psum_scatter(
        base_projection + adapter_delta, "tensor", scatter_dimension=0, tiled=True
    )
    return total_output.astype(jnp.bfloat16)


def solution(mesh):
    return jax.shard_map(
        shards,
        mesh=mesh,
        in_specs=(
            P("dp", "tensor"),
            P("tensor", "dp"),
            P("dp", None, "tensor"),
            P("dp", "tensor"),
            P(None, None, "dp"),
            P(),
        ),
        out_specs=P("tensor", "dp"),
        check_vma=False,
    )
```

profile of v0, /device:TPU:2, one launch (start us, length us, event | category | flops | bytes accessed | tf_op | source)
XLA Modules:
  0.0 204.0 jit_solution(7147101190510910882)
XLA Ops:
  6.5 0.0 copy-start
  6.5 0.0 all-gather.2.cloned.1.call-start
  6.5 0.7 all-gather.2.cloned.1.call-update
  7.3 0.7 dynamic-slice_bitcast_fusion
  8.0 0.2 convert_reduce_fusion
  8.2 0.7 multiply_add_fusion
  8.9 0.0 copy-start.1
  8.9 1.4 convolution_convert_fusion
  10.3 1.2 reshape.53
  11.5 0.0 copy-start.2
  11.5 11.8 %all-to-all-start = ((bf16[32,2,6656]{2,1,0:T(2,128)(2,1)}), bf16[32,2,6656]{2,1,0:T(2,128)(2,1)S(1)}, u32[]{:S(2)}, u32[]{:S(2)}) async-start(bf16[32,2,6656]{2,1,0:T(2,128)(2,1)} %reshape.53), calls=%async_computation | async-start | bytes 1703936 | tf_op jit(solution)/shard_map/all_to_all | solution.py:36
  23.3 0.0 copy-done.1
  23.3 0.1 reduce
  23.4 31.3 %all-to-all-done = bf16[32,2,6656]{2,1,0:T(2,128)(2,1)S(1)} async-done(((bf16[32,2,6656]{2,1,0:T(2,128)(2,1)}), bf16[32,2,6656]{2,1,0:T(2,128)(2,1)S(1)}, u32[]{:S(2)}, u32[]{:S(2)}) %all-to-all-start) | async-done | bytes 852000 | tf_op jit(solution)/shard_map/all_to_all | solution.py:36
  54.7 1.5 convolution_convert_fusion.1
  56.3 0.7 all_to_all.12
  56.9 5.8 %all-to-all-start.1 = ((bf16[32,1,128]{2,1,0:T(2,128)(2,1)}), bf16[32,1,128]{2,1,0:T(2,128)(2,1)S(1)}, u32[]{:S(2)}, u32[]{:S(2)}) async-start(bf16[32,1,128]{2,1,0:T(2,128)(2,1)} %all_to_all.12), calls=%async_computation.1 | async-start | bytes 32768 | tf_op jit(solution)/shard_map/all_to_all | solution.py:41
  62.8 0.0 reduce-scatter.2.cloned.1.call-start
  62.8 0.0 copy-done.2
  62.9 8.4 %all-to-all-done.1 = bf16[32,1,128]{2,1,0:T(2,128)(2,1)S(1)} async-done(((bf16[32,1,128]{2,1,0:T(2,128)(2,1)}), bf16[32,1,128]{2,1,0:T(2,128)(2,1)S(1)}, u32[]{:S(2)}, u32[]{:S(2)}) %all-to-all-start.1) | async-done | bytes 8224 | tf_op jit(solution)/shard_map/all_to_all | solution.py:41
  71.2 0.1 reduce.1
  71.3 0.1 reshape.54
  71.3 0.2 convolution_convert_fusion.2
  71.5 0.1 reshape.55
  71.6 41.6 %all_gather.7 = bf16[65536]{0:T(1024)(128)(2,1)S(1)} all-gather(bf16[2048]{0:T(1024)(128)(2,1)S(1)} %reshape.55), channel_id=1, replica_groups=mesh['dp'=32,'tensor'=8] {'dp'}, dimensions={0}, use_global_device_ids=true | all-gather | bytes 135168 | tf_op jit(solution)/shard_map/all_gather | solution.py:46
  113.2 0.1 broadcast_in_dim.31
  113.4 0.1 copy.18
  113.5 0.0 copy-done
  113.5 3.7 %fusion = f32[1024,512,1]{1,0,2:T(8,128)} fusion(bf16[32,64,512]{2,1,0:T(8,128)(2,1)S(1)} %copy-done, pred[1024,32]{0,1:T(8,128)(4,1)S(1)} %iota_compare_fusion, bf16[1024,64]{0,1:T(8,128)(2,1)S(1)} %copy.18), kind=kOutput, calls=%fused_computation.1 | convolution fusion | flops 2149580800 | bytes 4358144 | tf_op jit(solution)/shard_map/dot_general | solution.py:55
  117.2 30.3 %all-gather.2.cloned.1.call-done = bf16[1024,6656]{1,0:T(8,128)(2,1)} async-done(((bf16[32,6656]{1,0:T(8,128)(2,1)}), bf16[1024,6656]{1,0:T(8,128)(2,1)}) %all-gather.2.cloned.1.call-update) | async-done | bytes 13631504 | tf_op jit(solution)/shard_map/all_gather | solution.py:24
  147.4 13.5 %bitcast_add_fusion = f32[1024,512]{1,0:T(8,128)} fusion(f32[1024,512,1]{1,0,2:T(8,128)} %fusion, bf16[1024,6656]{1,0:T(8,128)(2,1)} %all-gather.2.cloned.1.call-done, bf16[6656,512]{1,0:T(8,128)(2,1)} %param.7), kind=kOutput, calls=%fused_computation.4 | convolution fusion | flops 6979846144 | bytes 24641536 | tf_op jit(solution)/shard_map/dot_general | solution.py:8
  161.0 0.0 reduce-scatter.2.cloned.1.call-update
  161.0 34.6 %reduce-scatter.2.cloned.1.call-done = f32[128,512]{1,0:T(8,128)} async-done(((f32[1024,512]{1,0:T(8,128)}), f32[128,512]{1,0:T(8,128)}) %reduce-scatter.2.cloned.1.call-update) | async-done | bytes 262160 | tf_op jit(solution)/shard_map/reduce_scatter | solution.py:62
  195.6 1.6 convert_element_type.32
  (2 shorter events, 0.0 us)
Async XLA Ops:
  6.5 107.0 %copy-start = (bf16[32,64,512]{2,1,0:T(8,128)(2,1)S(1)}, bf16[32,64,512]{2,1,0:T(8,128)(2,1)}, u32[]{:S(2)}) copy-start(bf16[32,64,512]{2,1,0:T(8,128)(2,1)} %param.10) | copy-start | bytes 6291460
  6.5 140.9 %all-gather.2.cloned.1.call-start = ((), (), s32[]{:S(2)}) async-start(), calls=%async_computation.3 | async-start | bytes 14057472 | tf_op jit(solution)/shard_map/all_gather | solution.py:24
  8.9 14.4 %copy-start.1 = (f32[1,6656]{1,0:T(1,128)S(1)}, f32[1,6656]{1,0:T(1,128)}, u32[]{:S(2)}) copy-start(f32[1,6656]{1,0:T(1,128)} %param.9) | copy-start | bytes 79876
  11.5 51.3 %copy-start.2 = (s32[1024,1]{0,1:T(1,128)S(1)}, s32[1024,1]{0,1:T(1,128)}, u32[]{:S(2)}) copy-start(s32[1024,1]{0,1:T(1,128)} %param.11) | copy-start | bytes 12292
  11.5 43.2 %all-to-all-start = ((bf16[32,2,6656]{2,1,0:T(2,128)(2,1)}), bf16[32,2,6656]{2,1,0:T(2,128)(2,1)S(1)}, u32[]{:S(2)}, u32[]{:S(2)}) async-start(bf16[32,2,6656]{2,1,0:T(2,128)(2,1)} %reshape.53), calls=%async_computation | async-start | bytes 1703936 | tf_op jit(solution)/shard_map/all_to_all | solution.py:36
  56.9 14.3 %all-to-all-start.1 = ((bf16[32,1,128]{2,1,0:T(2,128)(2,1)}), bf16[32,1,128]{2,1,0:T(2,128)(2,1)S(1)}, u32[]{:S(2)}, u32[]{:S(2)}) async-start(bf16[32,1,128]{2,1,0:T(2,128)(2,1)} %all_to_all.12), calls=%async_computation.1 | async-start | bytes 32768 | tf_op jit(solution)/shard_map/all_to_all | solution.py:41
  62.8 132.8 %reduce-scatter.2.cloned.1.call-start = ((), (), s32[]{:S(2)}) async-start(), calls=%async_computation.4 | async-start | bytes 2359296 | tf_op jit(solution)/shard_map/reduce_scatter | solution.py:62
Sparse Core Ops, SparseCore 0:
  9.9 137.4 all-gather.1
  161.1 34.3 reduce-scatter.1
where the time goes:
time: 204 us
  waiting for transfers between devices  105 us (51%)
  blocking collectives  41.6 us (20%)
  matrix products  20.3 us (10%)
  starting transfers between devices  17.6 us (9%)
  between operations  13.5 us (7%)
  local copies, waits for them, and re-layouts  3.12 us (2%)
  other arithmetic  2.67 us (1%)
    all_gather x1, blocking collectives, shards(): lax.all_gather(own_rows.reshape(rows_dev * rank_activations), 'dp', axis=...  41.6 us
    reduce_scatter x1, waiting for transfers between devices, shards(): lax.psum_scatter(base_projection + adapter_delta, 'tensor', scatter_dimen...  34.6 us
    all_to_all x1, waiting for transfers between devices, shards(): lax.all_to_all(outgoing, 'dp', split_axis=0, concat_axis=0, tiled=True)  31.3 us
    all_gather x1, waiting for transfers between devices, shards(): lax.all_gather(hidden, 'dp', axis=0, tiled=True)  30.3 us
    dot_general x1, matrix products, project_rows(): return jnp.dot(piece, weight, preferred_element_type=jnp.float32)  13.5 us
    all_to_all x1, starting transfers between devices, shards(): lax.all_to_all(outgoing, 'dp', split_axis=0, concat_axis=0, tiled=True)  11.8 us
    all_to_all x1, waiting for transfers between devices, shards(): lax.all_to_all(flat, 'dp', split_axis=0, concat_axis=0, tiled=True)  8.36 us
    all_to_all x1, starting transfers between devices, shards(): lax.all_to_all(flat, 'dp', split_axis=0, concat_axis=0, tiled=True)  5.81 us
  transfers between devices with their start and end apart: 4, of which 4 were waited for; matrix products, arithmetic and copies ran while one was open for 5% of the time, Pallas kernels for 0%

commit v1 on v0

v1 whole, which is shorter than its diff:
```python
import functools

import jax
import jax.numpy as jnp
from jax import lax
from jax.experimental import pallas as pl
from jax.experimental.pallas import tpu as pltpu
from jax.sharding import Mesh, PartitionSpec as P

SIZES = {"z": 8, "x": 4}
BF16 = jnp.bfloat16
F32 = jnp.float32
I32 = jnp.int32
LANES = 128
NEAR, FAR = (1, 7, 2, 6), (3, 5, 4)
VMEM_LIMIT = 56 << 20


def turn(value, axis, by):
    size = SIZES[axis]
    pairs = [
        (i * 2 + c, (i + (by if c == 0 else -by)) % size * 2 + c)
        for i in range(size)
        for c in range(2)
    ]
    return lax.ppermute(value, (axis, "core"), pairs)


def after(value, *others):
    return lax.optimization_barrier((value, *others))[0]


def stack(*blocks):
    return jnp.concatenate(blocks, axis=0)


def dot(a, b, over=((1,), (0,))):
    return lax.dot_general(a, b, (over, ((), ())), preferred_element_type=F32)


def iota(shape, dim):
    return lax.broadcasted_iota(I32, shape, dim)


def plan_kernel(info, ids_ref, levels, scale, fill, pick, mask, dense, slot_of, slot_all):
    z, x, sign, t, me = (info[k] for k in range(5))
    rows = ids_ref.shape[1]
    rank = levels.shape[0]
    dense[...] = (levels[...].astype(F32) * scale[...]).astype(BF16)
    ids = ids_ref[...]
    lane, sub = iota(ids.shape, 1), iota(ids.shape, 0)
    place = jnp.zeros(ids.shape, I32)
    for q in range(rows):
        place += jnp.where((ids == ids[:, q : q + 1]) & (lane > q), 1, 0)
    slot_of[...] = jnp.where(ids == me, (sub >> 2) * 8 + (sub & 3) * 2 + place, -1)
    slot_all[...] = ids * 8 + (sub & 3) * 2 + place
    eye = iota((rows, rows), 0) == iota((rows, rows), 1)

    def column(row):
        return jnp.sum(jnp.where(eye, row, 0), axis=1, keepdims=True)

    def ones(where):
        return jnp.where(where, 1.0, 0.0).astype(BF16)

    for i in range(8):
        for j in range(4):
            source = ((z - sign * i) & 7) * 4 + ((x - sign * j) & 3)
            col = column(slot_of[pl.ds(source, 1), :])
            at = (i * 4 + j) * rows
            fill[at : at + rows, :] = ones(col == iota((rows, fill.shape[1]), 1))
    rank_bits = rank.bit_length() - 1
    for j in range(4):
        at = slice(j * rows, (j + 1) * rows)
        col = column(slot_all[pl.ds(t * 4 + j, 1), :])
        pick[at, :] = ones(col == iota((rows, pick.shape[1]), 1))
        col = column(ids_ref[pl.ds(t * 4 + j, 1), :])
        mask[at, :] = ones(col == (iota((rows, mask.shape[1]), 1) >> rank_bits))


def start(pairs, sems):
    copies = [pltpu.make_async_copy(src, dst, sems.at[k]) for k, (src, dst) in enumerate(pairs)]
    for copy in copies:
        copy.start()
    return copies


def wait(copies):
    for copy in copies:
        copy.wait()


def multiply(lhs, w, dense, acc):
    depth, n = w.shape
    half = depth // 2 if depth % 256 == 0 else depth
    for at in range(0, depth, half):
        at = slice(at, at + half)
        rows = lhs[:, at]
        base, shrink = dot(rows, w[at, :]), dot(rows, dense[:, at], ((1,), (1,)))
        if at.start:
            acc[:, :n] += base
            acc[:, n:] += shrink
        else:
            acc[:, :n], acc[:, n:] = base, shrink


def weight_copies(cut, weights, dense, w, d):
    first = [(weights.at[:cut], w.at[:cut]), (dense.at[:, :cut], d.at[:, :cut])]
    second = [(weights.at[cut:], w.at[cut:]), (dense.at[:, cut:], d.at[:, cut:])]
    return first, second


def both_products(cut, first, second, w, d, rows_a, rows_b, acc_a, acc_b, sems):
    copies = start(first + second, sems)
    wait(copies[: len(first)])
    multiply(rows_a, w.at[:cut], d.at[:, :cut], acc_a)
    wait(copies[len(first) :])
    multiply(rows_b, w.at[cut:], d.at[:, cut:], acc_b)


def finish(base, at, fill, block, parts):
    n = base.shape[1]
    both = stack(*parts)
    rows = both.shape[0]
    base[at : at + rows, :] = both[:, :n].astype(BF16)
    return dot(fill[block * rows : (block + 1) * rows, :], both[:, n:].astype(BF16), ((0,), (0,)))


def own_kernel(cut, *refs):
    own, (weights, dense, fill, base, slots), (w, d, rows_a, rows_b, acc_a, acc_b, sems) = (
        refs[:4], refs[4:9], refs[9:],
    )
    first, second = weight_copies(cut, weights, dense, w, d)
    rows = own[0].shape[0]
    for j in range(4):
        at = pl.ds(j * rows, rows)
        first.append((own[j].at[:, :cut], rows_a.at[at]))
        second.append((own[j].at[:, cut:], rows_b.at[at]))
    both_products(cut, first, second, w, d, rows_a, rows_b, acc_a, acc_b, sems)
    slots[...] = finish(base, 0, fill, 0, [acc_a[...] + acc_b[...]])


def near_kernel(cut, *refs):
    a, near, (weights, dense, acc_a, acc_b), (w, d, rows_a, rows_b, sems) = (
        refs[:4], refs[4:7], refs[7:11], refs[11:],
    )
    first, second = weight_copies(cut, weights, dense, w, d)
    for k in range(4):
        n = a[k].shape[0]
        first.append((a[k], rows_a.at[pl.ds(k * n, n)]))
        if k < 3:
            second.append((near[k], rows_b.at[pl.ds(k * n, n)]))
    both_products(cut, first, second, w, d, rows_a, rows_b, acc_a, acc_b, sems)


def far_kernel(cut, *refs):
    a, b, (weights, dense), (fill, near_a, near_b, earlier) = (
        refs[:2], refs[2:6], refs[6:8], refs[8:12],
    )
    base, acc_a, far_b, slots = refs[12:16]
    w, d, rows_a, rows_b, acc_b, sems = refs[16:]
    first, second = weight_copies(cut, weights, dense, w, d)
    at_b = 0
    for k in range(4):
        n, n_b = a[0].shape[0], b[k].shape[0]
        if k < 2:
            first.append((a[k], rows_a.at[pl.ds(k * n, n)]))
        second.append((b[k], rows_b.at[pl.ds(at_b, n_b)]))
        at_b += n_b
    both_products(cut, first, second, w, d, rows_a, rows_b, acc_a, acc_b, sems)
    rows = n // 4
    total = earlier[...]
    for k, i in enumerate(NEAR):
        parts = []
        for j in range(4):
            row = n * k + j * rows
            if j == 2:
                of_b = acc_b[k * rows : (k + 1) * rows, :]
            else:
                row_b = (j if j < 2 else 2) * n + k * rows
                of_b = near_b[row_b : row_b + rows, :]
            parts.append(near_a[row : row + rows, :] + of_b)
        total += finish(base, k * n, fill, i, parts)
    far_b[...] = acc_b[n:, :]
    slots[...] = total


def last_kernel(cut, info, a, far, weights, dense, fill, far_a, far_b, base_own, base_near, earlier, *refs):
    slots, out, (w, d, acc_a, acc_b, base, sems) = refs[0], refs[1:9], refs[9:]
    first, second = weight_copies(cut, weights, dense, w, d)
    both_products(cut, first, second, w, d, a, far, acc_a, acc_b, sems)
    n = a.shape[0]
    rows = n // 4
    total = earlier[...]
    base[:n, :] = base_own[...]
    for k, i in enumerate(NEAR):
        base[i * n : (i + 1) * n, :] = base_near[k * n : (k + 1) * n, :]
    for k, i in enumerate(FAR):
        parts = []
        for j in range(4):
            of_a = acc_a[j * rows : (j + 1) * rows, :] if k == 2 else None
            if k < 2:
                of_a = far_a[k * n + j * rows : k * n + (j + 1) * rows, :]
            if j == 2:
                of_b = acc_b[k * rows : (k + 1) * rows, :]
            else:
                row_b = ((j if j < 2 else 2) * 3 + k) * rows
                of_b = far_b[row_b : row_b + rows, :]
            parts.append(of_a + of_b)
        total += finish(base, i * n, fill, i, parts)
    rank = total.shape[1]
    slots[:, :rank], slots[:, rank:] = total, total
    z, _, sign, t, _ = (info[k] for k in range(5))
    for by, ref in enumerate(out):
        i = (sign * (z - t - by)) & 7
        ref[...] = base[pl.ds(pl.multiple_of(i * n, n), n), :]


def delta_kernel(slots, pick, mask, up, delta):
    mine = dot(pick[...], slots[...]).astype(BF16)
    spread = jnp.concatenate([mine] * (mask.shape[1] // LANES), axis=1) * mask[...]
    delta[...] = dot(spread, up[...])


def sum_kernel(info, delta, *refs):
    got, out, total = refs[:8], refs[8], refs[9]
    x, sign = info[1], info[2]
    rows = out.shape[0] // 4
    for j in range(4):
        at = slice(j * rows, (j + 1) * rows)
        other = slice((-j) % 4 * rows, ((-j) % 4 + 1) * rows)
        total[at, :] = sum(ref[other if by % 2 else at, :].astype(F32) for by, ref in enumerate(got))
    for k in range(4):
        j = (sign * (x - k)) & 3
        at = slice(k * rows, (k + 1) * rows)
        part = total[pl.ds(pl.multiple_of(j * rows, rows), rows), :]
        out[at, :] = (part + delta[at, :]).astype(BF16)


def local(kernel, out_shape, places, scratch=(), flops=1 << 20, name=None):
    vmem = pl.BlockSpec(memory_space=pltpu.VMEM)
    specs = {"s": pl.BlockSpec(memory_space=pltpu.SMEM), "v": vmem, "h": pl.BlockSpec(memory_space=pl.ANY)}
    return pl.pallas_call(
        kernel,
        out_shape=out_shape,
        in_specs=[specs[place] for place in places],
        out_specs=jax.tree.map(lambda _: vmem, out_shape),
        scratch_shapes=scratch,
        compiler_params=pltpu.CompilerParams(vmem_limit_bytes=VMEM_LIMIT),
        cost_estimate=pl.CostEstimate(flops=flops, bytes_accessed=4 << 20, transcendentals=0),
        name=name,
    )


def shards(hidden, down_matrix, levels, scale, up_factors, adapter_per_row):
    rows, width = hidden.shape
    rank = levels.shape[1]
    adapters = up_factors.shape[0]
    out_width = down_matrix.shape[1]
    z, x = lax.axis_index("z"), lax.axis_index("x")
    y, core = lax.axis_index("y"), lax.axis_index("core")
    me, t = z * 4 + x, y * 2 + core
    sign = 1 - 2 * core
    cut = width * 20 // 52 // 128 * 128
    levels = levels.reshape(rank, width)

    info = jnp.stack([z, x, sign, t, me]).astype(I32)
    fill, pick, mask, dense = local(
        plan_kernel,
        (
            jax.ShapeDtypeStruct((32 * rows, 64), BF16),
            jax.ShapeDtypeStruct((4 * rows, 8 * adapters), BF16),
            jax.ShapeDtypeStruct((4 * rows, adapters * rank), BF16),
            jax.ShapeDtypeStruct((rank, width), BF16),
        ),
        "svvv",
        [pltpu.VMEM((32, rows), I32), pltpu.VMEM((32, rows), I32)],
        name="plan",
    )(info, adapter_per_row.reshape(32, rows), levels, scale)

    n, wide = 4 * rows, out_width + rank
    block = jax.ShapeDtypeStruct((n, out_width), BF16)

    def sums(count):
        return jax.ShapeDtypeStruct((count * rows, wide), F32)

    def scratch(rows_a, rows_b, copies):
        rows_of = [((rows_a * rows, cut), BF16), ((rows_b * rows, width - cut), BF16)]
        return [
            pltpu.VMEM((width, out_width), BF16),
            pltpu.VMEM((rank, width), BF16),
            *(pltpu.VMEM(*shape) for shape in rows_of if shape[0][0]),
        ], [pltpu.SemaphoreType.DMA((copies,))]

    def acc(count):
        return pltpu.VMEM((count * rows, wide), F32)

    def cost(count):
        return 2 * count * rows * width * wide

    part_a, part_b = hidden[:, :cut], hidden[:, cut:]
    b = {0: part_b}
    b[1], b[7] = turn(part_b, "z", 1), turn(part_b, "z", -1)
    own_1, own_3 = turn(hidden, "x", 1), turn(hidden, "x", -1)
    b[2], b[6] = turn(b[1], "z", 1), turn(b[7], "z", -1)
    own_2 = turn(own_1, "x", 1)
    near_0 = stack(*(b[i] for i in NEAR))
    near_1, near_3 = turn(near_0, "x", 1), turn(near_0, "x", -1)
    b[3], b[5] = turn(b[2], "z", 1), turn(b[6], "z", -1)
    b[4] = turn(b[3], "z", 1)
    a = {0: after(stack(part_a, own_1[:, :cut], own_2[:, :cut], own_3[:, :cut]), b[3], b[5])}
    a[1], a[7] = turn(a[0], "z", 1), turn(a[0], "z", -1)
    head, tail = scratch(4, 4, 12)
    base_own, slots = local(
        functools.partial(own_kernel, cut),
        (block, jax.ShapeDtypeStruct((64, rank), F32)),
        "hhhhhhv",
        [*head, acc(4), acc(4), *tail],
        cost(4),
        "own",
    )(hidden, own_1, own_2, own_3, down_matrix, dense, fill)
    far_0 = after(stack(*(b[i] for i in FAR)), pick, mask)
    near_2 = turn(near_1, "x", 1)
    far_1, far_3 = turn(far_0, "x", 1), turn(far_0, "x", -1)
    a[2], a[6] = turn(after(a[1], base_own), "z", 1), turn(a[7], "z", -1)
    head, tail = scratch(16, 12, 11)
    near_a, near_b = local(
        functools.partial(near_kernel, cut),
        (sums(16), sums(12)),
        "hhhhhhhhh",
        [*head, *tail],
        cost(14),
        "near",
    )(*(a[i] for i in NEAR), near_0, near_1, near_3, down_matrix, dense)
    far_2 = turn(after(far_1, near_a, near_b), "x", 1)
    a[3], a[5] = turn(a[2], "z", 1), turn(a[6], "z", -1)
    a[4] = turn(a[3], "z", 1)
    head, tail = scratch(8, 13, 10)
    base_near, far_a, far_b, slots = local(
        functools.partial(far_kernel, cut),
        (
            jax.ShapeDtypeStruct((4 * n, out_width), BF16),
            sums(8),
            sums(9),
            jax.ShapeDtypeStruct((64, rank), F32),
        ),
        "hhhhhhhhvvvv",
        [*head, acc(13), *tail],
        cost(11),
        "far",
    )(a[3], a[5], near_2, far_0, far_1, far_3, down_matrix, dense, fill, near_a, near_b, slots)
    head, tail = scratch(0, 0, 4)
    slots, *blocks = local(
        functools.partial(last_kernel, cut),
        (jax.ShapeDtypeStruct((64, LANES), F32),) + (block,) * 8,
        "svvhhvvvvvv",
        [*head, acc(4), acc(3), pltpu.VMEM((8 * n, out_width), BF16), *tail],
        cost(4),
        "last",
    )(info, a[4], far_2, down_matrix, dense, fill, far_a, far_b, base_own, base_near, slots)

    slots = lax.all_to_all(slots, ("y", "core"), 0, 0, tiled=True)
    slots = jnp.sum(slots.reshape(8, 8, LANES), axis=0)
    slots = jnp.broadcast_to(slots[None], (adapters, 8, LANES)).reshape(adapters * 8, LANES)
    slots = lax.all_to_all(slots, ("z", "x"), 0, 0, tiled=True).astype(BF16)
    delta = local(
        delta_kernel,
        jax.ShapeDtypeStruct((n, out_width), F32),
        "vvvv",
        flops=2 * n * adapters * rank * out_width,
        name="delta",
    )(slots, pick, mask, up_factors.reshape(adapters * rank, out_width))

    got = [blocks[0]]
    for by in range(1, 8):
        pairs = [(i, (i + by) % 8) for i in range(8)]
        got.append(lax.ppermute(blocks[by], ("y", "core"), pairs))
    return local(
        sum_kernel, block, "s" + "v" * 9, [pltpu.VMEM((n, out_width), F32)], name="sum"
    )(info, delta, *got)


def solution(mesh):
    torus = Mesh(mesh.devices.reshape(8, 4, 4, 2), ("z", "x", "y", "core"))
    dp, tensor = ("z", "x"), ("y", "core")
    return jax.shard_map(
        shards,
        mesh=torus,
        in_specs=(
            P(dp, tensor),
            P(tensor, dp),
            P(dp, None, tensor),
            P(dp, tensor),
            P(None, None, dp),
            P(),
        ),
        out_specs=P(tensor, dp),
        check_vma=False,
    )
```

time: 204 us -> 150 us (0.74); the launches traced: 204 us -> 148 us
  waiting for transfers between devices: 105 us -> 29.5 us
  Pallas kernels: 0 us -> 40.9 us
  starting transfers between devices: 17.6 us -> 55.6 us
  blocking collectives: 41.6 us -> 9.62 us
  matrix products: 20.3 us -> 0 us
  between operations: 13.5 us -> 0.36 us
  local copies, waits for them, and re-layouts: 3.12 us -> 9.15 us
    ppermute x0 -> x30, starting transfers between devices: none -> 46.9 us  [the longest x23 38.9 us: turn(): return lax.ppermute(value, (axis, 'core'), pairs)]
    all_gather x1 -> x0, blocking collectives: 41.6 us -> none  [shards(): lax.all_gather(own_rows.reshape(rows_dev * rank_activations), 'dp', axis=...]
    pallas_call x0 -> x7, Pallas kernels: none -> 40.9 us  [the longest x1 10.2 us: shards(): local(functools.partial(far_kernel, cut), (jax.ShapeDtypeStruct((4 * n, o...]
    all_to_all x2 -> x1, waiting for transfers between devices: 39.7 us -> 2.38 us  [shards(): slots = lax.all_to_all(slots, ('z', 'x'), 0, 0, tiled=True).astype(BF16)]
    reduce_scatter x1 -> x0, waiting for transfers between devices: 34.6 us -> none  [shards(): lax.psum_scatter(base_projection + adapter_delta, 'tensor', scatter_dimen...]
    all_gather x1 -> x0, waiting for transfers between devices: 30.3 us -> none  [shards(): lax.all_gather(hidden, 'dp', axis=0, tiled=True)]
    ppermute x0 -> x30, waiting for transfers between devices: none -> 27.1 us  [the longest x23 25.9 us: turn(): return lax.ppermute(value, (axis, 'core'), pairs)]
    dot_general x5 -> x0, matrix products: 20.3 us -> none  [the longest x1 13.5 us: project_rows(): return jnp.dot(piece, weight, preferred_element_type=jnp.float32)]
  transfers between devices with their start and end apart: 4 -> 31, of which waited for: 4 -> 11; matrix products, arithmetic and copies ran while one was open for 5% -> 4% of each run, Pallas kernels for 0% -> 21%
where the time goes in v1:
time: 150 us; the launch traced here: 148 us
  starting transfers between devices  55.6 us (37%)
  Pallas kernels  40.9 us (27%)
  waiting for transfers between devices  29.5 us (20%)
  blocking collectives  9.62 us (6%)
  local copies, waits for them, and re-layouts  9.15 us (6%)
  other arithmetic  2.56 us (2%)
    ppermute x23, starting transfers between devices, turn(): return lax.ppermute(value, (axis, 'core'), pairs)  38.9 us
    ppermute x23, waiting for transfers between devices, turn(): return lax.ppermute(value, (axis, 'core'), pairs)  25.9 us
    pallas_call x1, Pallas kernels, shards(): local(functools.partial(far_kernel, cut), (jax.ShapeDtypeStruct((4 * n, o...  10.2 us
    all_to_all x1, blocking collectives, shards(): slots = lax.all_to_all(slots, ('y', 'core'), 0, 0, tiled=True)  9.62 us
    all_to_all x1, starting transfers between devices, shards(): slots = lax.all_to_all(slots, ('z', 'x'), 0, 0, tiled=True).astype(BF16)  8.73 us
    pallas_call x1, Pallas kernels, shards(): local(functools.partial(near_kernel, cut), (sums(16), sums(12)), 'hhhhhhh...  8.51 us
    ppermute x7, starting transfers between devices, shards(): got.append(lax.ppermute(blocks[by], ('y', 'core'), pairs))  7.94 us
    pallas_call x1, Pallas kernels, shards(): local(functools.partial(last_kernel, cut), (jax.ShapeDtypeStruct((64, LAN...  7.44 us
  transfers between devices with their start and end apart: 31, of which 11 were waited for; matrix products, arithmetic and copies ran while one was open for 4% of the time, Pallas kernels for 21%

profile of v1, /device:TPU:2, one launch (start us, length us, event | category | flops | bytes accessed | tf_op | source)
XLA Modules:
  0.0 147.7 jit_solution(4403164554974640052)
XLA Ops:
  0.0 1.0 slice.19
  1.0 2.0 %collective-permute-start.3 = (bf16[32,4096]{1,0:T(8,128)(2,1)S(1)}, bf16[32,4096]{1,0:T(8,128)(2,1)S(1)}, u32[]{:S(2)}, u32[]{:S(2)}) collective-permute-start(bf16[32,4096]{1,0:T(8,128)(2,1)S(1)} %slice.19), channel_id=1, source_target_pairs={{0,32},{1,225},{32,64},{33,1},{64,96},{65,33},{96,128},{97,65},{12... | collective-permute-start | bytes 786440 | tf_op jit(solution)/shard_map/ppermute | solution.py:26
  3.0 1.5 %collective-permute-start = (bf16[32,6656]{1,0:T(8,128)(2,1)}, bf16[32,6656]{1,0:T(8,128)(2,1)S(1)}, u32[]{:S(2)}, u32[]{:S(2)}) collective-permute-start(bf16[32,6656]{1,0:T(8,128)(2,1)} %refs_0_.1), channel_id=1, source_target_pairs={{0,8},{1,25},{8,16},{9,1},{16,24},{17,9},{24,0},{25,17},{2,10},{3,... | collective-permute-start | bytes 1277960 | tf_op jit(solution)/shard_map/ppermute | solution.py:26
  4.5 0.5 collective-permute-start.2
  5.0 4.0 %collective-permute-start.6 = (bf16[32,4096]{1,0:T(8,128)(2,1)S(1)}, bf16[32,4096]{1,0:T(8,128)(2,1)S(1)}, u32[]{:S(2)}, u32[]{:S(2)}) collective-permute-start(bf16[32,4096]{1,0:T(8,128)(2,1)S(1)} %slice.19), channel_id=1, source_target_pairs={{0,224},{1,33},{32,0},{33,65},{64,32},{65,97},{96,64},{97,129},{12... | collective-permute-start | bytes 786440 | tf_op jit(solution)/shard_map/ppermute | solution.py:26
  9.0 0.9 slice.15
  10.0 1.3 collective-permute-done.3
  11.3 1.6 %collective-permute-done.6 = bf16[32,4096]{1,0:T(8,128)(2,1)S(1)} collective-permute-done((bf16[32,4096]{1,0:T(8,128)(2,1)S(1)}, bf16[32,4096]{1,0:T(8,128)(2,1)S(1)}, u32[]{:S(2)}, u32[]{:S(2)}) %collective-permute-start.6) | collective-permute-done | bytes 262176 | tf_op jit(solution)/shard_map/ppermute | solution.py:26
  12.9 3.7 %collective-permute-start.7 = (bf16[32,4096]{1,0:T(8,128)(2,1)S(1)}, bf16[32,4096]{1,0:T(8,128)(2,1)S(1)}, u32[]{:S(2)}, u32[]{:S(2)}) collective-permute-start(bf16[32,4096]{1,0:T(8,128)(2,1)S(1)} %collective-permute-done.6), channel_id=1, source_target_pairs={{0,224},{1,33},{32,0},{33,65},{64,32},{65,97},{96,64},{97,129},{12... | collective-permute-start | bytes 786440 | tf_op jit(solution)/shard_map/ppermute | solution.py:26
  16.6 1.6 %collective-permute-start.1 = (bf16[32,6656]{1,0:T(8,128)(2,1)S(1)}, bf16[32,6656]{1,0:T(8,128)(2,1)S(1)}, u32[]{:S(2)}, u32[]{:S(2)}) collective-permute-start(bf16[32,6656]{1,0:T(8,128)(2,1)S(1)} %collective-permute-done.refs_1_), channel_id=1, source_target_pairs={{0,8},{1,25},{8,16},{9,1},{16,24},{17,9},{24,0},{25,17},{2,10},{3,... | collective-permute-start | bytes 1277960 | tf_op jit(solution)/shard_map/ppermute | solution.py:26
  18.3 0.0 copy-start.23
  18.3 2.2 %collective-permute-done.4 = bf16[32,4096]{1,0:T(8,128)(2,1)S(1)} collective-permute-done((bf16[32,4096]{1,0:T(8,128)(2,1)S(1)}, bf16[32,4096]{1,0:T(8,128)(2,1)S(1)}, u32[]{:S(2)}, u32[]{:S(2)}) %collective-permute-start.4) | collective-permute-done | bytes 262176 | tf_op jit(solution)/shard_map/ppermute | solution.py:26
  20.5 0.2 collective-permute-done.7
  20.7 3.7 %collective-permute-start.8 = (bf16[32,4096]{1,0:T(8,128)(2,1)S(1)}, bf16[32,4096]{1,0:T(8,128)(2,1)S(1)}, u32[]{:S(2)}, u32[]{:S(2)}) collective-permute-start(bf16[32,4096]{1,0:T(8,128)(2,1)S(1)} %collective-permute-done.7), channel_id=1, source_target_pairs={{0,224},{1,33},{32,0},{33,65},{64,32},{65,97},{96,64},{97,129},{12... | collective-permute-start | bytes 786440 | tf_op jit(solution)/shard_map/ppermute | solution.py:26
  24.4 0.7 collective-permute-done.1.refs_2_
  25.1 0.8 copy-done.7
  25.9 0.9 pad_maximum_fusion.1
  26.8 4.1 %collective-permute-done.5 = bf16[32,4096]{1,0:T(8,128)(2,1)S(1)} collective-permute-done((bf16[32,4096]{1,0:T(8,128)(2,1)S(1)}, bf16[32,4096]{1,0:T(8,128)(2,1)S(1)}, u32[]{:S(2)}, u32[]{:S(2)}) %collective-permute-start.5) | collective-permute-done | bytes 262176 | tf_op jit(solution)/shard_map/ppermute | solution.py:26
  30.9 2.7 %collective-permute-start.9 = (bf16[128,2560]{1,0:T(8,128)(2,1)}, bf16[128,2560]{1,0:T(8,128)(2,1)}, u32[]{:S(2)}, u32[]{:S(2)}) collective-permute-start(bf16[128,2560]{1,0:T(8,128)(2,1)} %pad_maximum_fusion.1), channel_id=1, source_target_pairs={{0,32},{1,225},{32,64},{33,1},{64,96},{65,33},{96,128},{97,65},{12... | collective-permute-start | bytes 1966088 | tf_op jit(solution)/shard_map/ppermute | solution.py:26
  33.6 0.5 collective-permute-start.15
  34.1 1.6 %collective-permute-start.17 = (bf16[128,4096]{1,0:T(8,128)(2,1)S(1)}, bf16[128,4096]{1,0:T(8,128)(2,1)S(1)}, u32[]{:S(2)}, u32[]{:S(2)}) collective-permute-start(bf16[128,4096]{1,0:T(8,128)(2,1)S(1)} %constant_dynamic-update-slice_fusion.refs_4_), channel_id=1, source_target_pairs={{0,8},{1,25},{8,16},{9,1},{16,24},{17,9},{24,0},{25,17},{2,10},{3,... | collective-permute-start | bytes 3145736 | tf_op jit(solution)/shard_map/ppermute | solution.py:26
  35.7 3.7 %collective-permute-start.13 = (bf16[32,4096]{1,0:T(8,128)(2,1)S(1)}, bf16[32,4096]{1,0:T(8,128)(2,1)}, u32[]{:S(2)}, u32[]{:S(2)}) collective-permute-start(bf16[32,4096]{1,0:T(8,128)(2,1)S(1)} %collective-permute-done.5), channel_id=1, source_target_pairs={{0,32},{1,225},{32,64},{33,1},{64,96},{65,33},{96,128},{97,65},{12... | collective-permute-start | bytes 786440 | tf_op jit(solution)/shard_map/ppermute | solution.py:26
  39.4 0.5 collective-permute-start.18
  39.9 0.5 broadcast.4
  40.4 0.7 reduce.4
  41.1 0.7 reshape.19.ids_ref
  41.8 0.7 stack.23.info
  42.5 3.1 %plan.1 = (bf16[1024,64]{1,0:T(8,128)(2,1)}, bf16[128,256]{1,0:T(8,128)(2,1)}, bf16[128,2048]{1,0:T(8,128)(2,1)}, bf16[64,6656]{1,0:T(8,128)(2,1)}) custom-call(s32[5]{0:T(128)} %stack.23.info, s32[32,32]{1,0:T(8,128)} %reshape.19.ids_ref, bf16[64,6656]{1,0:T(8,128)(2,1)} %bitcast.13, f32[1,6656]{1,0:T(1,128)} %scale.1), custom_call_target="tpu_custom_call" | custom-call | flops 1048576 | bytes 4194304 | tf_op jit(solution)/shard_map/plan/pallas_call | solution.py:267
  45.6 6.4 %own.1 = (bf16[128,512]{1,0:T(8,128)(2,1)}, f32[64,64]{1,0:T(8,128)}) custom-call(bf16[32,6656]{1,0:T(8,128)(2,1)} %refs_0_.1, bf16[32,6656]{1,0:T(8,128)(2,1)} %copy-done.5, bf16[32,6656]{1,0:T(8,128)(2,1)} %copy-done.7, bf16[32,6656]{1,0:T(8,128)(2,1)} %copy-done.6, bf16[6656,512]{1,0:T(8,128)(2,1)} %weights.1, ...), custom_call_target="tpu_custom_call" | custom-call | flops 981467136 | bytes 4194304 | tf_op jit(solution)/shard_map/own/pallas_call | solution.py:313
  52.0 2.8 %collective-permute-start.10 = (bf16[128,2560]{1,0:T(8,128)(2,1)}, bf16[128,2560]{1,0:T(8,128)(2,1)}, u32[]{:S(2)}, u32[]{:S(2)}) collective-permute-start(bf16[128,2560]{1,0:T(8,128)(2,1)} %collective-permute-done.9.refs_0_), channel_id=1, source_target_pairs={{0,32},{1,225},{32,64},{33,1},{64,96},{65,33},{96,128},{97,65},{12... | collective-permute-start | bytes 1966088 | tf_op jit(solution)/shard_map/ppermute | solution.py:26
  54.8 0.5 collective-permute-start.16
  55.3 1.0 pad_maximum_fusion.refs_3_
  56.3 1.6 %collective-permute-start.14 = (bf16[96,4096]{1,0:T(8,128)(2,1)S(1)}, bf16[96,4096]{1,0:T(8,128)(2,1)S(1)}, u32[]{:S(2)}, u32[]{:S(2)}) collective-permute-start(bf16[96,4096]{1,0:T(8,128)(2,1)S(1)} %pad_maximum_fusion.refs_3_), channel_id=1, source_target_pairs={{0,8},{1,25},{8,16},{9,1},{16,24},{17,9},{24,0},{25,17},{2,10},{3,... | collective-permute-start | bytes 2359304 | tf_op jit(solution)/shard_map/ppermute | solution.py:26
  57.9 10.3 %collective-permute-done.10.refs_2_ = bf16[128,2560]{1,0:T(8,128)(2,1)} collective-permute-done((bf16[128,2560]{1,0:T(8,128)(2,1)}, bf16[128,2560]{1,0:T(8,128)(2,1)}, u32[]{:S(2)}, u32[]{:S(2)}) %collective-permute-start.10) | collective-permute-done | bytes 655392 | tf_op jit(solution)/shard_map/ppermute | solution.py:26
  68.2 1.6 %collective-permute-start.21 = (bf16[128,4096]{1,0:T(8,128)(2,1)S(1)}, bf16[128,4096]{1,0:T(8,128)(2,1)S(1)}, u32[]{:S(2)}, u32[]{:S(2)}) collective-permute-start(bf16[128,4096]{1,0:T(8,128)(2,1)S(1)} %collective-permute-done.17.refs_5_), channel_id=1, source_target_pairs={{0,8},{1,25},{8,16},{9,1},{16,24},{17,9},{24,0},{25,17},{2,10},{3,... | collective-permute-start | bytes 3145736 | tf_op jit(solution)/shard_map/ppermute | solution.py:26
  69.8 0.5 collective-permute-start.22
  70.3 3.2 %collective-permute-start.20 = (bf16[128,2560]{1,0:T(8,128)(2,1)}, bf16[128,2560]{1,0:T(8,128)(2,1)S(1)}, u32[]{:S(2)}, u32[]{:S(2)}) collective-permute-start(bf16[128,2560]{1,0:T(8,128)(2,1)} %collective-permute-done.16.refs_3_), channel_id=1, source_target_pairs={{0,224},{1,33},{32,0},{33,65},{64,32},{65,97},{96,64},{97,129},{12... | collective-permute-start | bytes 1966088 | tf_op jit(solution)/shard_map/ppermute | solution.py:26
  73.5 8.5 %near.1 = (f32[512,576]{1,0:T(8,128)}, f32[384,576]{1,0:T(8,128)}) custom-call(bf16[128,2560]{1,0:T(8,128)(2,1)} %collective-permute-done.9.refs_0_, bf16[128,2560]{1,0:T(8,128)(2,1)} %collective-permute-done.15.refs_1_, bf16[128,2560]{1,0:T(8,128)(2,1)} %collective-permute-done.10.refs_2_, bf16[128,2560]{1,0:T(8,128)(2,1)} %collective-permute-done.16.refs_3_, ...), custom_call_target="tpu_custom_call" | custom-call | flops 3435134976 | bytes 4194304 | tf_op jit(solution)/shard_map/near/pallas_call | solution.py:326
  82.0 1.8 %collective-permute-start.19 = (bf16[96,4096]{1,0:T(8,128)(2,1)S(1)}, bf16[96,4096]{1,0:T(8,128)(2,1)S(1)}, u32[]{:S(2)}, u32[]{:S(2)}) collective-permute-start(bf16[96,4096]{1,0:T(8,128)(2,1)S(1)} %collective-permute-done.14.refs_4_), channel_id=1, source_target_pairs={{0,8},{1,25},{8,16},{9,1},{16,24},{17,9},{24,0},{25,17},{2,10},{3,... | collective-permute-start | bytes 2359304 | tf_op jit(solution)/shard_map/ppermute | solution.py:26
  83.8 1.0 collective-permute-start.12
  84.8 5.5 %collective-permute-done.22.refs_5_ = bf16[96,4096]{1,0:T(8,128)(2,1)S(1)} collective-permute-done((bf16[96,4096]{1,0:T(8,128)(2,1)S(1)}, bf16[96,4096]{1,0:T(8,128)(2,1)S(1)}, u32[]{:S(2)}, u32[]{:S(2)}) %collective-permute-start.22) | collective-permute-done | bytes 786464 | tf_op jit(solution)/shard_map/ppermute | solution.py:26
  90.3 0.9 copy-done.9
  91.1 0.4 copy-done.2
  91.5 0.2 copy-done.12
  91.7 10.2 %far.1 = (bf16[512,512]{1,0:T(8,128)(2,1)}, f32[256,576]{1,0:T(8,128)}, f32[288,576]{1,0:T(8,128)}, f32[64,64]{1,0:T(8,128)}) custom-call(bf16[128,2560]{1,0:T(8,128)(2,1)} %collective-permute-done.11.refs_0_, bf16[128,2560]{1,0:T(8,128)(2,1)} %copy-done.12, bf16[128,4096]{1,0:T(8,128)(2,1)} %copy-done.2, bf16[96,4096]{1,0:T(8,128)(2,1)} %copy-done, ...), custom_call_target="tpu_custom_call" | custom-call | flops 2699034624 | bytes 4194304 | tf_op jit(solution)/shard_map/far/pallas_call | solution.py:338
  102.0 0.9 copy-done.10
  102.9 0.3 copy-done.11
  103.1 7.4 %last.1 = (f32[64,128]{1,0:T(8,128)}, bf16[128,512]{1,0:T(8,128)(2,1)}, bf16[128,512]{1,0:T(8,128)(2,1)}, bf16[128,512]{1,0:T(8,128)(2,1)}, bf16[128,512]{1,0:T(...) custom-call(s32[5]{0:T(128)} %stack.23.info, ...), custom_call_target="tpu_custom_call" | custom-call | flops 981467136 | bytes 4194304 | tf_op jit(solution)/shard_map/last/pallas_call | solution.py:352
  110.6 0.0 collective-permute-start.23
  110.6 1.6 %collective-permute-start.24 = (bf16[128,512]{1,0:T(8,128)(2,1)}, bf16[128,512]{1,0:T(8,128)(2,1)S(1)}, u32[]{:S(2)}, u32[]{:S(2)}) collective-permute-start(bf16[128,512]{1,0:T(8,128)(2,1)} %get-tuple-element.49), channel_id=1, source_target_pairs={{0,2},{1,3},{2,4},{3,5},{4,6},{5,7},{6,0},{7,1},{8,10},{9,11},{10,... | collective-permute-start | bytes 393224 | tf_op jit(solution)/shard_map/ppermute | solution.py:376
  112.2 9.6 %all_to_all.15 = f32[8,8,128]{2,1,0:T(8,128)S(1)} all-to-all(f32[8,8,128]{2,1,0:T(8,128)} %bitcast.15), channel_id=1, replica_groups=mesh['z'=8,'x'=4,'y'=4,'core'=2] {'y','core'}, dimensions={0} | all-to-all | bytes 65536 | tf_op jit(solution)/shard_map/all_to_all | solution.py:361
  121.9 0.6 broadcast_in_dim.2
  122.5 8.7 %all-to-all-start.1 = ((bf16[32,8,128]{2,1,0:T(8,128)(2,1)}), bf16[32,8,128]{2,1,0:T(8,128)(2,1)S(1)}, u32[]{:S(2)}, u32[]{:S(2)}) async-start(bf16[32,8,128]{2,1,0:T(8,128)(2,1)} %broadcast_in_dim.2), calls=%async_computation.1 | async-start | bytes 131072 | tf_op jit(solution)/shard_map/all_to_all | solution.py:364
  131.2 0.1 collective-permute-start.25
  131.3 1.4 collective-permute-start.26
  132.8 2.6 %collective-permute-start.27 = (bf16[128,512]{1,0:T(8,128)(2,1)}, bf16[128,512]{1,0:T(8,128)(2,1)S(1)}, u32[]{:S(2)}, u32[]{:S(2)}) collective-permute-start(bf16[128,512]{1,0:T(8,128)(2,1)} %get-tuple-element.52), channel_id=1, source_target_pairs={{0,5},{1,6},{2,7},{3,0},{4,1},{5,2},{6,3},{7,4},{8,13},{9,14},{10,... | collective-permute-start | bytes 393224 | tf_op jit(solution)/shard_map/ppermute | solution.py:376
  135.4 2.2 %collective-permute-start.28 = (bf16[128,512]{1,0:T(8,128)(2,1)}, bf16[128,512]{1,0:T(8,128)(2,1)S(1)}, u32[]{:S(2)}, u32[]{:S(2)}) collective-permute-start(bf16[128,512]{1,0:T(8,128)(2,1)} %get-tuple-element.53), channel_id=1, source_target_pairs={{0,6},{1,7},{2,0},{3,1},{4,2},{5,3},{6,4},{7,5},{8,14},{9,15},{10,... | collective-permute-start | bytes 393224 | tf_op jit(solution)/shard_map/ppermute | solution.py:376
  137.5 2.4 %all-to-all-done.1 = bf16[32,8,128]{2,1,0:T(8,128)(2,1)S(1)} async-done(((bf16[32,8,128]{2,1,0:T(8,128)(2,1)}), bf16[32,8,128]{2,1,0:T(8,128)(2,1)S(1)}, u32[]{:S(2)}, u32[]{:S(2)}) %all-to-all-start.1) | async-done | bytes 65568 | tf_op jit(solution)/shard_map/all_to_all | solution.py:364
  139.9 0.6 copy-done.13
  140.6 3.1 %delta.1 = f32[128,512]{1,0:T(8,128)} custom-call(bf16[256,128]{1,0:T(8,128)(2,1)} %bitcast.14, bf16[128,256]{1,0:T(8,128)(2,1)} %get-tuple-element.35.pick, bf16[128,2048]{1,0:T(8,128)(2,1)} %get-tuple-element.36.mask, bf16[2048,512]{1,0:T(8,128)(2,1)} %bitcast.12), custom_call_target="tpu_custom_call" | custom-call | flops 268435456 | bytes 4194304 | tf_op jit(solution)/shard_map/delta/pallas_call | solution.py:365
  143.7 0.4 collective-permute-done.28.refs_6_
  144.1 0.8 collective-permute-done.29.refs_7_
  144.9 0.6 copy-done.22
  145.5 2.2 %sum.1 = bf16[128,512]{1,0:T(8,128)(2,1)} custom-call(s32[5]{0:T(128)} %stack.23.info, f32[128,512]{1,0:T(8,128)} %delta.1, bf16[128,512]{1,0:T(8,128)(2,1)} %get-tuple-element.47.refs_0_, bf16[128,512]{1,0:T(8,128)(2,1)} %copy-done.16, bf16[128,512]{1,0:T(8,128)(2,1)} %copy-done.17, bf16[128,512]{1,0:T(8,128)(2,1)} %copy-done.18, ...), custom_call_target="tpu_custom_call" | custom-call | flops 1048576 | bytes 4194304 | tf_op jit(solution)/shard_map/sum/pallas_call | solution.py:377
  (71 shorter events, 0.3 us)
Async XLA Ops:
  1.0 10.3 %collective-permute-start.3 = (bf16[32,4096]{1,0:T(8,128)(2,1)S(1)}, bf16[32,4096]{1,0:T(8,128)(2,1)S(1)}, u32[]{:S(2)}, u32[]{:S(2)}) collective-permute-start(bf16[32,4096]{1,0:T(8,128)(2,1)S(1)} %slice.19), channel_id=1, source_target_pairs={{0,32},{1,225},{32,64},{33,1},{64,96},{65,33},{96,128},{97,65},{12... | collective-permute-start | bytes 786440 | tf_op jit(solution)/shard_map/ppermute | solution.py:26
  3.0 13.7 %collective-permute-start = (bf16[32,6656]{1,0:T(8,128)(2,1)}, bf16[32,6656]{1,0:T(8,128)(2,1)S(1)}, u32[]{:S(2)}, u32[]{:S(2)}) collective-permute-start(bf16[32,6656]{1,0:T(8,128)(2,1)} %refs_0_.1), channel_id=1, source_target_pairs={{0,8},{1,25},{8,16},{9,1},{16,24},{17,9},{24,0},{25,17},{2,10},{3,... | collective-permute-start | bytes 1277960 | tf_op jit(solution)/shard_map/ppermute | solution.py:26
  4.5 13.8 %collective-permute-start.2 = (bf16[32,6656]{1,0:T(8,128)(2,1)}, bf16[32,6656]{1,0:T(8,128)(2,1)S(1)}, u32[]{:S(2)}, u32[]{:S(2)}) collective-permute-start(bf16[32,6656]{1,0:T(8,128)(2,1)} %refs_0_.1), channel_id=1, source_target_pairs={{0,24},{1,9},{8,0},{9,17},{16,8},{17,25},{24,16},{25,1},{2,26},{3,... | collective-permute-start | bytes 1277960 | tf_op jit(solution)/shard_map/ppermute | solution.py:26
  5.0 7.9 %collective-permute-start.6 = (bf16[32,4096]{1,0:T(8,128)(2,1)S(1)}, bf16[32,4096]{1,0:T(8,128)(2,1)S(1)}, u32[]{:S(2)}, u32[]{:S(2)}) collective-permute-start(bf16[32,4096]{1,0:T(8,128)(2,1)S(1)} %slice.19), channel_id=1, source_target_pairs={{0,224},{1,33},{32,0},{33,65},{64,32},{65,97},{96,64},{97,129},{12... | collective-permute-start | bytes 786440 | tf_op jit(solution)/shard_map/ppermute | solution.py:26
  11.3 9.2 %collective-permute-start.4 = (bf16[32,4096]{1,0:T(8,128)(2,1)S(1)}, bf16[32,4096]{1,0:T(8,128)(2,1)S(1)}, u32[]{:S(2)}, u32[]{:S(2)}) collective-permute-start(bf16[32,4096]{1,0:T(8,128)(2,1)S(1)} %collective-permute-done.3), channel_id=1, source_target_pairs={{0,32},{1,225},{32,64},{33,1},{64,96},{65,33},{96,128},{97,65},{12... | collective-permute-start | bytes 786440 | tf_op jit(solution)/shard_map/ppermute | solution.py:26
  12.9 7.8 %collective-permute-start.7 = (bf16[32,4096]{1,0:T(8,128)(2,1)S(1)}, bf16[32,4096]{1,0:T(8,128)(2,1)S(1)}, u32[]{:S(2)}, u32[]{:S(2)}) collective-permute-start(bf16[32,4096]{1,0:T(8,128)(2,1)S(1)} %collective-permute-done.6), channel_id=1, source_target_pairs={{0,224},{1,33},{32,0},{33,65},{64,32},{65,97},{96,64},{97,129},{12... | collective-permute-start | bytes 786440 | tf_op jit(solution)/shard_map/ppermute | solution.py:26
  16.6 7.8 %copy-start.5 = (bf16[32,6656]{1,0:T(8,128)(2,1)}, bf16[32,6656]{1,0:T(8,128)(2,1)S(1)}, u32[]{:S(2)}) copy-start(bf16[32,6656]{1,0:T(8,128)(2,1)S(1)} %collective-permute-done.refs_1_) | copy-start | bytes 1277956
  16.6 8.4 %collective-permute-start.1 = (bf16[32,6656]{1,0:T(8,128)(2,1)S(1)}, bf16[32,6656]{1,0:T(8,128)(2,1)S(1)}, u32[]{:S(2)}, u32[]{:S(2)}) collective-permute-start(bf16[32,6656]{1,0:T(8,128)(2,1)S(1)} %collective-permute-done.refs_1_), channel_id=1, source_target_pairs={{0,8},{1,25},{8,16},{9,1},{16,24},{17,9},{24,0},{25,17},{2,10},{3,... | collective-permute-start | bytes 1277960 | tf_op jit(solution)/shard_map/ppermute | solution.py:26
  18.2 6.8 %copy-start.6 = (bf16[32,6656]{1,0:T(8,128)(2,1)}, bf16[32,6656]{1,0:T(8,128)(2,1)S(1)}, u32[]{:S(2)}) copy-start(bf16[32,6656]{1,0:T(8,128)(2,1)S(1)} %collective-permute-done.2.refs_3_) | copy-start | bytes 1277956
  18.3 22.2 %copy-start.23 = (s32[1024,1]{0,1:T(1,128)S(1)}, s32[1024,1]{0,1:T(1,128)}, u32[]{:S(2)}) copy-start(s32[1024,1]{0,1:T(1,128)} %param.11) | copy-start | bytes 12292
  20.5 10.3 %collective-permute-start.5 = (bf16[32,4096]{1,0:T(8,128)(2,1)S(1)}, bf16[32,4096]{1,0:T(8,128)(2,1)S(1)}, u32[]{:S(2)}, u32[]{:S(2)}) collective-permute-start(bf16[32,4096]{1,0:T(8,128)(2,1)S(1)} %collective-permute-done.4), channel_id=1, source_target_pairs={{0,32},{1,225},{32,64},{33,1},{64,96},{65,33},{96,128},{97,65},{12... | collective-permute-start | bytes 786440 | tf_op jit(solution)/shard_map/ppermute | solution.py:26
  20.7 10.2 %collective-permute-start.8 = (bf16[32,4096]{1,0:T(8,128)(2,1)S(1)}, bf16[32,4096]{1,0:T(8,128)(2,1)S(1)}, u32[]{:S(2)}, u32[]{:S(2)}) collective-permute-start(bf16[32,4096]{1,0:T(8,128)(2,1)S(1)} %collective-permute-done.7), channel_id=1, source_target_pairs={{0,224},{1,33},{32,0},{33,65},{64,32},{65,97},{96,64},{97,129},{12... | collective-permute-start | bytes 786440 | tf_op jit(solution)/shard_map/ppermute | solution.py:26
  25.1 0.8 copy-start.7
  30.9 3.2 %copy-start.14 = (bf16[32,4096]{1,0:T(8,128)(2,1)}, bf16[32,4096]{1,0:T(8,128)(2,1)S(1)}, u32[]{:S(2)}) copy-start(bf16[32,4096]{1,0:T(8,128)(2,1)S(1)} %collective-permute-done.8) | copy-start | bytes 786436
  30.9 21.1 %collective-permute-start.9 = (bf16[128,2560]{1,0:T(8,128)(2,1)}, bf16[128,2560]{1,0:T(8,128)(2,1)}, u32[]{:S(2)}, u32[]{:S(2)}) collective-permute-start(bf16[128,2560]{1,0:T(8,128)(2,1)} %pad_maximum_fusion.1), channel_id=1, source_target_pairs={{0,32},{1,225},{32,64},{33,1},{64,96},{65,33},{96,128},{97,65},{12... | collective-permute-start | bytes 1966088 | tf_op jit(solution)/shard_map/ppermute | solution.py:26
  33.6 21.2 %collective-permute-start.15 = (bf16[128,2560]{1,0:T(8,128)(2,1)}, bf16[128,2560]{1,0:T(8,128)(2,1)}, u32[]{:S(2)}, u32[]{:S(2)}) collective-permute-start(bf16[128,2560]{1,0:T(8,128)(2,1)} %pad_maximum_fusion.1), channel_id=1, source_target_pairs={{0,224},{1,33},{32,0},{33,65},{64,32},{65,97},{96,64},{97,129},{12... | collective-permute-start | bytes 1966088 | tf_op jit(solution)/shard_map/ppermute | solution.py:26
  34.1 17.9 %copy-start.1 = (bf16[128,4096]{1,0:T(8,128)(2,1)}, bf16[128,4096]{1,0:T(8,128)(2,1)S(1)}, u32[]{:S(2)}) copy-start(bf16[128,4096]{1,0:T(8,128)(2,1)S(1)} %constant_dynamic-update-slice_fusion.refs_4_) | copy-start | bytes 3145732
  34.1 34.1 %collective-permute-start.17 = (bf16[128,4096]{1,0:T(8,128)(2,1)S(1)}, bf16[128,4096]{1,0:T(8,128)(2,1)S(1)}, u32[]{:S(2)}, u32[]{:S(2)}) collective-permute-start(bf16[128,4096]{1,0:T(8,128)(2,1)S(1)} %constant_dynamic-update-slice_fusion.refs_4_), channel_id=1, source_target_pairs={{0,8},{1,25},{8,16},{9,1},{16,24},{17,9},{24,0},{25,17},{2,10},{3,... | collective-permute-start | bytes 3145736 | tf_op jit(solution)/shard_map/ppermute | solution.py:26
  35.7 19.6 %collective-permute-start.13 = (bf16[32,4096]{1,0:T(8,128)(2,1)S(1)}, bf16[32,4096]{1,0:T(8,128)(2,1)}, u32[]{:S(2)}, u32[]{:S(2)}) collective-permute-start(bf16[32,4096]{1,0:T(8,128)(2,1)S(1)} %collective-permute-done.5), channel_id=1, source_target_pairs={{0,32},{1,225},{32,64},{33,1},{64,96},{65,33},{96,128},{97,65},{12... | collective-permute-start | bytes 786440 | tf_op jit(solution)/shard_map/ppermute | solution.py:26
  39.4 30.4 %collective-permute-start.18 = (bf16[128,4096]{1,0:T(8,128)(2,1)S(1)}, bf16[128,4096]{1,0:T(8,128)(2,1)S(1)}, u32[]{:S(2)}, u32[]{:S(2)}) collective-permute-start(bf16[128,4096]{1,0:T(8,128)(2,1)S(1)} %constant_dynamic-update-slice_fusion.refs_4_), channel_id=1, source_target_pairs={{0,24},{1,9},{8,0},{9,17},{16,8},{17,25},{24,16},{25,1},{2,26},{3,... | collective-permute-start | bytes 3145736 | tf_op jit(solution)/shard_map/ppermute | solution.py:26
  45.6 9.8 %copy-start.15 = (bf16[32,4096]{1,0:T(8,128)(2,1)S(1)}, bf16[32,4096]{1,0:T(8,128)(2,1)}, u32[]{:S(2)}) copy-start(bf16[32,4096]{1,0:T(8,128)(2,1)} %copy-done.14) | copy-start | bytes 786436
  52.0 16.2 %collective-permute-start.10 = (bf16[128,2560]{1,0:T(8,128)(2,1)}, bf16[128,2560]{1,0:T(8,128)(2,1)}, u32[]{:S(2)}, u32[]{:S(2)}) collective-permute-start(bf16[128,2560]{1,0:T(8,128)(2,1)} %collective-permute-done.9.refs_0_), channel_id=1, source_target_pairs={{0,32},{1,225},{32,64},{33,1},{64,96},{65,33},{96,128},{97,65},{12... | collective-permute-start | bytes 1966088 | tf_op jit(solution)/shard_map/ppermute | solution.py:26
  54.8 15.5 %collective-permute-start.16 = (bf16[128,2560]{1,0:T(8,128)(2,1)}, bf16[128,2560]{1,0:T(8,128)(2,1)}, u32[]{:S(2)}, u32[]{:S(2)}) collective-permute-start(bf16[128,2560]{1,0:T(8,128)(2,1)} %collective-permute-done.15.refs_1_), channel_id=1, source_target_pairs={{0,224},{1,33},{32,0},{33,65},{64,32},{65,97},{96,64},{97,129},{12... | collective-permute-start | bytes 1966088 | tf_op jit(solution)/shard_map/ppermute | solution.py:26
  56.3 25.7 %copy-start = (bf16[96,4096]{1,0:T(8,128)(2,1)}, bf16[96,4096]{1,0:T(8,128)(2,1)S(1)}, u32[]{:S(2)}) copy-start(bf16[96,4096]{1,0:T(8,128)(2,1)S(1)} %pad_maximum_fusion.refs_3_) | copy-start | bytes 2359300
  56.3 25.7 %collective-permute-start.14 = (bf16[96,4096]{1,0:T(8,128)(2,1)S(1)}, bf16[96,4096]{1,0:T(8,128)(2,1)S(1)}, u32[]{:S(2)}, u32[]{:S(2)}) collective-permute-start(bf16[96,4096]{1,0:T(8,128)(2,1)S(1)} %pad_maximum_fusion.refs_3_), channel_id=1, source_target_pairs={{0,8},{1,25},{8,16},{9,1},{16,24},{17,9},{24,0},{25,17},{2,10},{3,... | collective-permute-start | bytes 2359304 | tf_op jit(solution)/shard_map/ppermute | solution.py:26
  68.2 15.6 %collective-permute-start.11 = (bf16[128,2560]{1,0:T(8,128)(2,1)}, bf16[128,2560]{1,0:T(8,128)(2,1)}, u32[]{:S(2)}, u32[]{:S(2)}) collective-permute-start(bf16[128,2560]{1,0:T(8,128)(2,1)} %collective-permute-done.10.refs_2_), channel_id=1, source_target_pairs={{0,32},{1,225},{32,64},{33,1},{64,96},{65,33},{96,128},{97,65},{12... | collective-permute-start | bytes 1966088 | tf_op jit(solution)/shard_map/ppermute | solution.py:26
  68.2 5.3 %copy-start.3 = (bf16[128,4096]{1,0:T(8,128)(2,1)}, bf16[128,4096]{1,0:T(8,128)(2,1)S(1)}, u32[]{:S(2)}) copy-start(bf16[128,4096]{1,0:T(8,128)(2,1)S(1)} %collective-permute-done.17.refs_5_) | copy-start | bytes 3145732
  68.2 22.1 %collective-permute-start.21 = (bf16[128,4096]{1,0:T(8,128)(2,1)S(1)}, bf16[128,4096]{1,0:T(8,128)(2,1)S(1)}, u32[]{:S(2)}, u32[]{:S(2)}) collective-permute-start(bf16[128,4096]{1,0:T(8,128)(2,1)S(1)} %collective-permute-done.17.refs_5_), channel_id=1, source_target_pairs={{0,8},{1,25},{8,16},{9,1},{16,24},{17,9},{24,0},{25,17},{2,10},{3,... | collective-permute-start | bytes 3145736 | tf_op jit(solution)/shard_map/ppermute | solution.py:26
  69.8 3.7 %copy-start.4 = (bf16[128,4096]{1,0:T(8,128)(2,1)}, bf16[128,4096]{1,0:T(8,128)(2,1)S(1)}, u32[]{:S(2)}) copy-start(bf16[128,4096]{1,0:T(8,128)(2,1)S(1)} %collective-permute-done.18.refs_6_) | copy-start | bytes 3145732
  69.8 20.5 %collective-permute-start.22 = (bf16[96,4096]{1,0:T(8,128)(2,1)S(1)}, bf16[96,4096]{1,0:T(8,128)(2,1)S(1)}, u32[]{:S(2)}, u32[]{:S(2)}) collective-permute-start(bf16[96,4096]{1,0:T(8,128)(2,1)S(1)} %pad_maximum_fusion.refs_3_), channel_id=1, source_target_pairs={{0,24},{1,9},{8,0},{9,17},{16,8},{17,25},{24,16},{25,1},{2,26},{3,... | collective-permute-start | bytes 2359304 | tf_op jit(solution)/shard_map/ppermute | solution.py:26
  70.3 20.0 %collective-permute-start.20 = (bf16[128,2560]{1,0:T(8,128)(2,1)}, bf16[128,2560]{1,0:T(8,128)(2,1)S(1)}, u32[]{:S(2)}, u32[]{:S(2)}) collective-permute-start(bf16[128,2560]{1,0:T(8,128)(2,1)} %collective-permute-done.16.refs_3_), channel_id=1, source_target_pairs={{0,224},{1,33},{32,0},{33,65},{64,32},{65,97},{96,64},{97,129},{12... | collective-permute-start | bytes 1966088 | tf_op jit(solution)/shard_map/ppermute | solution.py:26
  82.0 8.3 %copy-start.8 = (bf16[96,4096]{1,0:T(8,128)(2,1)}, bf16[96,4096]{1,0:T(8,128)(2,1)S(1)}, u32[]{:S(2)}) copy-start(bf16[96,4096]{1,0:T(8,128)(2,1)S(1)} %collective-permute-done.14.refs_4_) | copy-start | bytes 2359300
  82.0 19.9 %collective-permute-start.19 = (bf16[96,4096]{1,0:T(8,128)(2,1)S(1)}, bf16[96,4096]{1,0:T(8,128)(2,1)S(1)}, u32[]{:S(2)}, u32[]{:S(2)}) collective-permute-start(bf16[96,4096]{1,0:T(8,128)(2,1)S(1)} %collective-permute-done.14.refs_4_), channel_id=1, source_target_pairs={{0,8},{1,25},{8,16},{9,1},{16,24},{17,9},{24,0},{25,17},{2,10},{3,... | collective-permute-start | bytes 2359304 | tf_op jit(solution)/shard_map/ppermute | solution.py:26
  83.8 18.2 %collective-permute-start.12 = (bf16[128,2560]{1,0:T(8,128)(2,1)}, bf16[128,2560]{1,0:T(8,128)(2,1)S(1)}, u32[]{:S(2)}, u32[]{:S(2)}) collective-permute-start(bf16[128,2560]{1,0:T(8,128)(2,1)} %collective-permute-done.11.refs_0_), channel_id=1, source_target_pairs={{0,32},{1,225},{32,64},{33,1},{64,96},{65,33},{96,128},{97,65},{12... | collective-permute-start | bytes 1966088 | tf_op jit(solution)/shard_map/ppermute | solution.py:26
  90.2 0.9 copy-start.9
  90.2 1.2 copy-start.2
  90.3 1.4 copy-start.12
  102.0 0.9 copy-start.10
  102.0 1.1 copy-start.11
  110.6 24.8 %collective-permute-start.23 = (bf16[128,512]{1,0:T(8,128)(2,1)}, bf16[128,512]{1,0:T(8,128)(2,1)S(1)}, u32[]{:S(2)}, u32[]{:S(2)}) collective-permute-start(bf16[128,512]{1,0:T(8,128)(2,1)} %get-tuple-element.48), channel_id=1, source_target_pairs={{0,1},{1,2},{2,3},{3,4},{4,5},{5,6},{6,7},{7,0},{8,9},{9,10},{10,1... | collective-permute-start | bytes 393224 | tf_op jit(solution)/shard_map/ppermute | solution.py:376
  110.6 27.0 %collective-permute-start.24 = (bf16[128,512]{1,0:T(8,128)(2,1)}, bf16[128,512]{1,0:T(8,128)(2,1)S(1)}, u32[]{:S(2)}, u32[]{:S(2)}) collective-permute-start(bf16[128,512]{1,0:T(8,128)(2,1)} %get-tuple-element.49), channel_id=1, source_target_pairs={{0,2},{1,3},{2,4},{3,5},{4,6},{5,7},{6,0},{7,1},{8,10},{9,11},{10,... | collective-permute-start | bytes 393224 | tf_op jit(solution)/shard_map/ppermute | solution.py:376
  122.5 17.4 %all-to-all-start.1 = ((bf16[32,8,128]{2,1,0:T(8,128)(2,1)}), bf16[32,8,128]{2,1,0:T(8,128)(2,1)S(1)}, u32[]{:S(2)}, u32[]{:S(2)}) async-start(bf16[32,8,128]{2,1,0:T(8,128)(2,1)} %broadcast_in_dim.2), calls=%async_computation.1 | async-start | bytes 131072 | tf_op jit(solution)/shard_map/all_to_all | solution.py:364
  131.2 12.4 %collective-permute-start.25 = (bf16[128,512]{1,0:T(8,128)(2,1)}, bf16[128,512]{1,0:T(8,128)(2,1)S(1)}, u32[]{:S(2)}, u32[]{:S(2)}) collective-permute-start(bf16[128,512]{1,0:T(8,128)(2,1)} %get-tuple-element.50), channel_id=1, source_target_pairs={{0,3},{1,4},{2,5},{3,6},{4,7},{5,0},{6,1},{7,2},{8,11},{9,12},{10,... | collective-permute-start | bytes 393224 | tf_op jit(solution)/shard_map/ppermute | solution.py:376
  131.3 12.3 %collective-permute-start.26 = (bf16[128,512]{1,0:T(8,128)(2,1)}, bf16[128,512]{1,0:T(8,128)(2,1)S(1)}, u32[]{:S(2)}, u32[]{:S(2)}) collective-permute-start(bf16[128,512]{1,0:T(8,128)(2,1)} %get-tuple-element.51), channel_id=1, source_target_pairs={{0,4},{1,5},{2,6},{3,7},{4,0},{5,1},{6,2},{7,3},{8,12},{9,13},{10,... | collective-permute-start | bytes 393224 | tf_op jit(solution)/shard_map/ppermute | solution.py:376
  132.8 10.9 %collective-permute-start.27 = (bf16[128,512]{1,0:T(8,128)(2,1)}, bf16[128,512]{1,0:T(8,128)(2,1)S(1)}, u32[]{:S(2)}, u32[]{:S(2)}) collective-permute-start(bf16[128,512]{1,0:T(8,128)(2,1)} %get-tuple-element.52), channel_id=1, source_target_pairs={{0,5},{1,6},{2,7},{3,0},{4,1},{5,2},{6,3},{7,4},{8,13},{9,14},{10,... | collective-permute-start | bytes 393224 | tf_op jit(solution)/shard_map/ppermute | solution.py:376
  135.4 9.5 %copy-start.16 = (bf16[128,512]{1,0:T(8,128)(2,1)}, bf16[128,512]{1,0:T(8,128)(2,1)S(1)}, u32[]{:S(2)}) copy-start(bf16[128,512]{1,0:T(8,128)(2,1)S(1)} %collective-permute-done.23.refs_1_) | copy-start | bytes 393220
  135.4 8.7 %collective-permute-start.28 = (bf16[128,512]{1,0:T(8,128)(2,1)}, bf16[128,512]{1,0:T(8,128)(2,1)S(1)}, u32[]{:S(2)}, u32[]{:S(2)}) collective-permute-start(bf16[128,512]{1,0:T(8,128)(2,1)} %get-tuple-element.53), channel_id=1, source_target_pairs={{0,6},{1,7},{2,0},{3,1},{4,2},{5,3},{6,4},{7,5},{8,14},{9,15},{10,... | collective-permute-start | bytes 393224 | tf_op jit(solution)/shard_map/ppermute | solution.py:376
  137.5 7.4 %copy-start.17 = (bf16[128,512]{1,0:T(8,128)(2,1)}, bf16[128,512]{1,0:T(8,128)(2,1)S(1)}, u32[]{:S(2)}) copy-start(bf16[128,512]{1,0:T(8,128)(2,1)S(1)} %collective-permute-done.24.refs_2_) | copy-start | bytes 393220
  137.5 7.4 %collective-permute-start.29 = (bf16[128,512]{1,0:T(8,128)(2,1)}, bf16[128,512]{1,0:T(8,128)(2,1)S(1)}, u32[]{:S(2)}, u32[]{:S(2)}) collective-permute-start(bf16[128,512]{1,0:T(8,128)(2,1)} %get-tuple-element.54), channel_id=1, source_target_pairs={{0,7},{1,0},{2,1},{3,2},{4,3},{5,4},{6,5},{7,6},{8,15},{9,8},{10,9... | collective-permute-start | bytes 393224 | tf_op jit(solution)/shard_map/ppermute | solution.py:376
  139.9 0.6 copy-start.13
  143.6 1.3 copy-start.18
  143.6 1.3 copy-start.19
  143.7 1.3 copy-start.20
  144.1 0.8 copy-start.21
  144.9 0.6 copy-start.22

commit v2 on v1

--- a/solution.py
+++ b/solution.py
@@ -13,7 +13,7 @@
 I32 = jnp.int32
 LANES = 128
 NEAR, FAR = (1, 7, 2, 6), (3, 5, 4)
-VMEM_LIMIT = 56 << 20
+VMEM_LIMIT = 16 << 20
 
 
 def turn(value, axis, by):
@@ -103,12 +103,6 @@
             acc[:, :n], acc[:, n:] = base, shrink
 
 
-def weight_copies(cut, weights, dense, w, d):
-    first = [(weights.at[:cut], w.at[:cut]), (dense.at[:, :cut], d.at[:, :cut])]
-    second = [(weights.at[cut:], w.at[cut:]), (dense.at[:, cut:], d.at[:, cut:])]
-    return first, second
-
-
 def both_products(cut, first, second, w, d, rows_a, rows_b, acc_a, acc_b, sems):
     copies = start(first + second, sems)
     wait(copies[: len(first)])
@@ -126,10 +120,10 @@
 
 
 def own_kernel(cut, *refs):
-    own, (weights, dense, fill, base, slots), (w, d, rows_a, rows_b, acc_a, acc_b, sems) = (
+    own, (w, d, fill, base, slots), (rows_a, rows_b, acc_a, acc_b, sems) = (
         refs[:4], refs[4:9], refs[9:],
     )
-    first, second = weight_copies(cut, weights, dense, w, d)
+    first, second = [], []
     rows = own[0].shape[0]
     for j in range(4):
         at = pl.ds(j * rows, rows)
@@ -140,10 +134,10 @@
 
 
 def near_kernel(cut, *refs):
-    a, near, (weights, dense, acc_a, acc_b), (w, d, rows_a, rows_b, sems) = (
+    a, near, (w, d, acc_a, acc_b), (rows_a, rows_b, sems) = (
         refs[:4], refs[4:7], refs[7:11], refs[11:],
     )
-    first, second = weight_copies(cut, weights, dense, w, d)
+    first, second = [], []
     for k in range(4):
         n = a[k].shape[0]
         first.append((a[k], rows_a.at[pl.ds(k * n, n)]))
@@ -153,12 +147,12 @@
 
 
 def far_kernel(cut, *refs):
-    a, b, (weights, dense), (fill, near_a, near_b, earlier) = (
+    a, b, (w, d), (fill, near_a, near_b, earlier) = (
         refs[:2], refs[2:6], refs[6:8], refs[8:12],
     )
     base, acc_a, far_b, slots = refs[12:16]
-    w, d, rows_a, rows_b, acc_b, sems = refs[16:]
-    first, second = weight_copies(cut, weights, dense, w, d)
+    rows_a, rows_b, acc_b, sems = refs[16:]
+    first, second = [], []
     at_b = 0
     for k in range(4):
         n, n_b = a[0].shape[0], b[k].shape[0]
@@ -184,10 +178,10 @@
     slots[...] = total
 
 
-def last_kernel(cut, info, a, far, weights, dense, fill, far_a, far_b, base_own, base_near, earlier, *refs):
-    slots, out, (w, d, acc_a, acc_b, base, sems) = refs[0], refs[1:9], refs[9:]
-    first, second = weight_copies(cut, weights, dense, w, d)
-    both_products(cut, first, second, w, d, a, far, acc_a, acc_b, sems)
+def last_kernel(cut, info, a, far, w, d, fill, far_a, far_b, base_own, base_near, earlier,
+                slots, keep, send, acc_a, acc_b, base, sems):
+    multiply(a, w.at[:cut], d.at[:, :cut], acc_a)
+    multiply(far, w.at[cut:], d.at[:, cut:], acc_b)
     n = a.shape[0]
     rows = n // 4
     total = earlier[...]
@@ -209,41 +203,50 @@
         total += finish(base, i * n, fill, i, parts)
     rank = total.shape[1]
     slots[:, :rank], slots[:, rank:] = total, total
-    z, _, sign, t, _ = (info[k] for k in range(5))
+    z, sign, t = info[0], info[2], info[3]
+    core = t & 1
+    copies = []
+    for by in range(4):
+        for out, of in ((keep, core), (send, 1 - core)):
+            i = (sign * (z - ((t - core + 2 * by) & 7) - of)) & 7
+            copies.append((base.at[pl.ds(pl.multiple_of(i * n, n), n)], out.at[pl.ds(by * n, n)]))
+    wait(start(copies, sems))
+
+
+def swapped(ref, at, rows):
+    return stack(*(ref[at + (-j) % 4 * rows : at + ((-j) % 4 + 1) * rows, :] for j in range(4)))
+
+
+def pair_kernel(keep, got, *out):
+    n = out[0].shape[0]
     for by, ref in enumerate(out):
-        i = (sign * (z - t - by)) & 7
-        ref[...] = base[pl.ds(pl.multiple_of(i * n, n), n), :]
-
-
-def delta_kernel(slots, pick, mask, up, delta):
+        both = keep[by * n : (by + 1) * n, :].astype(F32) + swapped(got, by * n, n // 4).astype(F32)
+        ref[...] = both.astype(ref.dtype)
+
+
+def sum_kernel(info, slots, pick, mask, up, *refs):
+    got, out, total = refs[:4], refs[4], refs[5]
+    x, sign = info[1], info[2]
+    rows = out.shape[0] // 4
+    total[...] = sum(ref[...].astype(F32) for ref in got)
     mine = dot(pick[...], slots[...]).astype(BF16)
     spread = jnp.concatenate([mine] * (mask.shape[1] // LANES), axis=1) * mask[...]
-    delta[...] = dot(spread, up[...])
-
-
-def sum_kernel(info, delta, *refs):
-    got, out, total = refs[:8], refs[8], refs[9]
-    x, sign = info[1], info[2]
-    rows = out.shape[0] // 4
-    for j in range(4):
-        at = slice(j * rows, (j + 1) * rows)
-        other = slice((-j) % 4 * rows, ((-j) % 4 + 1) * rows)
-        total[at, :] = sum(ref[other if by % 2 else at, :].astype(F32) for by, ref in enumerate(got))
+    delta = dot(spread, up[...])
     for k in range(4):
         j = (sign * (x - k)) & 3
+        part = total[pl.ds(pl.multiple_of(j * rows, rows), rows), :]
         at = slice(k * rows, (k + 1) * rows)
-        part = total[pl.ds(pl.multiple_of(j * rows, rows), rows), :]
         out[at, :] = (part + delta[at, :]).astype(BF16)
 
 
-def local(kernel, out_shape, places, scratch=(), flops=1 << 20, name=None):
+def local(kernel, out_shape, places, scratch=(), flops=1 << 20, name=None, out="v"):
     vmem = pl.BlockSpec(memory_space=pltpu.VMEM)
     specs = {"s": pl.BlockSpec(memory_space=pltpu.SMEM), "v": vmem, "h": pl.BlockSpec(memory_space=pl.ANY)}
     return pl.pallas_call(
         kernel,
         out_shape=out_shape,
         in_specs=[specs[place] for place in places],
-        out_specs=jax.tree.map(lambda _: vmem, out_shape),
+        out_specs=tuple(specs[p] for p in out) if len(out) > 1 else jax.tree.map(lambda _: vmem, out_shape),
         scratch_shapes=scratch,
         compiler_params=pltpu.CompilerParams(vmem_limit_bytes=VMEM_LIMIT),
         cost_estimate=pl.CostEstimate(flops=flops, bytes_accessed=4 << 20, transcendentals=0),
@@ -286,8 +289,6 @@
     def scratch(rows_a, rows_b, copies):
         rows_of = [((rows_a * rows, cut), BF16), ((rows_b * rows, width - cut), BF16)]
         return [
-            pltpu.VMEM((width, out_width), BF16),
-            pltpu.VMEM((rank, width), BF16),
             *(pltpu.VMEM(*shape) for shape in rows_of if shape[0][0]),
         ], [pltpu.SemaphoreType.DMA((copies,))]
 
@@ -313,27 +314,27 @@
     base_own, slots = local(
         functools.partial(own_kernel, cut),
         (block, jax.ShapeDtypeStruct((64, rank), F32)),
-        "hhhhhhv",
+        "hhhhvvv",
         [*head, acc(4), acc(4), *tail],
         cost(4),
         "own",
     )(hidden, own_1, own_2, own_3, down_matrix, dense, fill)
-    far_0 = after(stack(*(b[i] for i in FAR)), pick, mask)
+    far_0 = after(stack(*(b[i] for i in FAR)), pick, mask, near_1)
     near_2 = turn(near_1, "x", 1)
     far_1, far_3 = turn(far_0, "x", 1), turn(far_0, "x", -1)
-    a[2], a[6] = turn(after(a[1], base_own), "z", 1), turn(a[7], "z", -1)
+    a[2], a[6] = turn(after(a[1], near_1), "z", 1), turn(after(a[7], near_3), "z", -1)
     head, tail = scratch(16, 12, 11)
     near_a, near_b = local(
         functools.partial(near_kernel, cut),
         (sums(16), sums(12)),
-        "hhhhhhhhh",
+        "hhhhhhhvv",
         [*head, *tail],
         cost(14),
         "near",
     )(*(a[i] for i in NEAR), near_0, near_1, near_3, down_matrix, dense)
-    far_2 = turn(after(far_1, near_a, near_b), "x", 1)
-    a[3], a[5] = turn(a[2], "z", 1), turn(a[6], "z", -1)
-    a[4] = turn(a[3], "z", 1)
+    far_2 = turn(far_1, "x", 1)
+    a[3], a[5] = turn(after(a[2], base_own), "z", 1), turn(a[6], "z", -1)
+    a[4] = turn(after(a[3], near_a, near_b), "z", 1)
     head, tail = scratch(8, 13, 10)
     base_near, far_a, far_b, slots = local(
         functools.partial(far_kernel, cut),
@@ -343,40 +344,42 @@
             sums(9),
             jax.ShapeDtypeStruct((64, rank), F32),
         ),
-        "hhhhhhhhvvvv",
+        "hhhhhhvvvvvv",
         [*head, acc(13), *tail],
         cost(11),
         "far",
     )(a[3], a[5], near_2, far_0, far_1, far_3, down_matrix, dense, fill, near_a, near_b, slots)
-    head, tail = scratch(0, 0, 4)
-    slots, *blocks = local(
+    four = jax.ShapeDtypeStruct((4 * n, out_width), BF16)
+    slots, keep, send = local(
         functools.partial(last_kernel, cut),
-        (jax.ShapeDtypeStruct((64, LANES), F32),) + (block,) * 8,
-        "svvhhvvvvvv",
-        [*head, acc(4), acc(3), pltpu.VMEM((8 * n, out_width), BF16), *tail],
+        (jax.ShapeDtypeStruct((64, LANES), F32), four, four),
+        "svvvvvvvvvv",
+        [acc(4), acc(3), pltpu.VMEM((8 * n, out_width), BF16), pltpu.SemaphoreType.DMA((8,))],
         cost(4),
         "last",
+        "vhh",
     )(info, a[4], far_2, down_matrix, dense, fill, far_a, far_b, base_own, base_near, slots)
 
     slots = lax.all_to_all(slots, ("y", "core"), 0, 0, tiled=True)
     slots = jnp.sum(slots.reshape(8, 8, LANES), axis=0)
     slots = jnp.broadcast_to(slots[None], (adapters, 8, LANES)).reshape(adapters * 8, LANES)
     slots = lax.all_to_all(slots, ("z", "x"), 0, 0, tiled=True).astype(BF16)
-    delta = local(
-        delta_kernel,
-        jax.ShapeDtypeStruct((n, out_width), F32),
-        "vvvv",
-        flops=2 * n * adapters * rank * out_width,
-        name="delta",
-    )(slots, pick, mask, up_factors.reshape(adapters * rank, out_width))
-
-    got = [blocks[0]]
-    for by in range(1, 8):
-        pairs = [(i, (i + by) % 8) for i in range(8)]
-        got.append(lax.ppermute(blocks[by], ("y", "core"), pairs))
+
+    given = lax.ppermute(send, "core", [(0, 1), (1, 0)])
+    pairs = local(
+        pair_kernel, (jax.ShapeDtypeStruct((n, out_width), F32), block, block, block), "vv", name="pair"
+    )(keep, given)
+    got = [pairs[0]]
+    for by in range(1, 4):
+        got.append(lax.ppermute(pairs[by], "y", [(i, (i + by) % 4) for i in range(4)]))
     return local(
-        sum_kernel, block, "s" + "v" * 9, [pltpu.VMEM((n, out_width), F32)], name="sum"
-    )(info, delta, *got)
+        sum_kernel,
+        block,
+        "s" + "v" * 8,
+        [pltpu.VMEM((n, out_width), F32)],
+        2 * n * adapters * rank * out_width,
+        "sum",
+    )(info, slots, pick, mask, up_factors.reshape(adapters * rank, out_width), *got)
 
 
 def solution(mesh):

time: 150 us -> 136 us (0.907); the launches traced: 148 us -> 136 us
  Pallas kernels: 40.9 us -> 21.1 us
  starting transfers between devices: 55.6 us -> 48.1 us
  blocking collectives: 9.62 us -> 16.9 us
  local copies, waits for them, and re-layouts: 9.15 us -> 13.9 us
  waiting for transfers between devices: 29.5 us -> 32.9 us
    all_to_all x1, blocking collectives: 9.62 us -> 16.9 us  [shards(): slots = lax.all_to_all(slots, ('z', 'x'), 0, 0, tiled=True).astype(BF16)]
    ppermute x23, waiting for transfers between devices: 25.9 us -> 32.8 us  [turn(): return lax.ppermute(value, (axis, 'core'), pairs)]
    unnamed x52 -> x36, local copies, waits for them, and re-layouts: 5.2 us -> 11.4 us
    pallas_call x1, Pallas kernels: 10.2 us -> 4.94 us  [shards(): local(functools.partial(far_kernel, cut), (jax.ShapeDtypeStruct((4 * n, o...]
    pallas_call x1, Pallas kernels: 6.42 us -> 2.19 us  [shards(): local(functools.partial(own_kernel, cut), (block, jax.ShapeDtypeStruct((6...]
    all_to_all x1, starting transfers between devices: 8.73 us -> 4.61 us  [shards(): slots = lax.all_to_all(slots, ('y', 'core'), 0, 0, tiled=True)]
    pallas_call x2, Pallas kernels: 5.25 us -> 1.9 us  [the longest x1 1.78 us: shards(): local(sum_kernel, block, 's' + 'v' * 8, [pltpu.VMEM((n, out_width), F32)]...]
    pallas_call x1, Pallas kernels: 7.44 us -> 4.31 us  [shards(): local(functools.partial(last_kernel, cut), (jax.ShapeDtypeStruct((64, LAN...]
  transfers between devices with their start and end apart: 31 -> 28, of which waited for: 11 -> 12; matrix products, arithmetic and copies ran while one was open for 4% -> 5% of each run, Pallas kernels for 21% -> 11%
where the time goes in v2:
time: 136 us
  starting transfers between devices  48.1 us (35%)
  waiting for transfers between devices  32.9 us (24%)
  Pallas kernels  21.1 us (16%)
  blocking collectives  16.9 us (12%)
  local copies, waits for them, and re-layouts  13.9 us (10%)
  other arithmetic  2.66 us (2%)
    ppermute x23, starting transfers between devices, turn(): return lax.ppermute(value, (axis, 'core'), pairs)  37.1 us
    ppermute x23, waiting for transfers between devices, turn(): return lax.ppermute(value, (axis, 'core'), pairs)  32.8 us
    all_to_all x1, blocking collectives, shards(): slots = lax.all_to_all(slots, ('z', 'x'), 0, 0, tiled=True).astype(BF16)  16.9 us
    unnamed x36, local copies, waits for them, and re-layouts  11.4 us
    ppermute x3, starting transfers between devices, shards(): lax.ppermute(pairs[by], 'y', [(i, (i + by) % 4) for i in range(4)])  6.23 us
    pallas_call x1, Pallas kernels, shards(): local(functools.partial(near_kernel, cut), (sums(16), sums(12)), 'hhhhhhh...  6.2 us
    pallas_call x1, Pallas kernels, shards(): local(functools.partial(far_kernel, cut), (jax.ShapeDtypeStruct((4 * n, o...  4.94 us
    all_to_all x1, starting transfers between devices, shards(): slots = lax.all_to_all(slots, ('y', 'core'), 0, 0, tiled=True)  4.61 us
  transfers between devices with their start and end apart: 28, of which 12 were waited for; matrix products, arithmetic and copies ran while one was open for 5% of the time, Pallas kernels for 11%

profile of v2, /device:TPU:2, one launch (start us, length us, event | category | flops | bytes accessed | tf_op | source)
XLA Modules:
  0.0 135.7 jit_solution(11475703286812181785)
XLA Ops:
  0.0 1.0 slice.19
  1.0 2.0 %collective-permute-start.3 = (bf16[32,4096]{1,0:T(8,128)(2,1)S(1)}, bf16[32,4096]{1,0:T(8,128)(2,1)S(1)}, u32[]{:S(2)}, u32[]{:S(2)}) collective-permute-start(bf16[32,4096]{1,0:T(8,128)(2,1)S(1)} %slice.19), channel_id=1, source_target_pairs={{0,32},{1,225},{32,64},{33,1},{64,96},{65,33},{96,128},{97,65},{12... | collective-permute-start | bytes 786440 | tf_op jit(solution)/shard_map/ppermute | solution.py:26
  3.0 1.5 %collective-permute-start = (bf16[32,6656]{1,0:T(8,128)(2,1)}, bf16[32,6656]{1,0:T(8,128)(2,1)S(1)}, u32[]{:S(2)}, u32[]{:S(2)}) collective-permute-start(bf16[32,6656]{1,0:T(8,128)(2,1)} %refs_0_.1), channel_id=1, source_target_pairs={{0,8},{1,25},{8,16},{9,1},{16,24},{17,9},{24,0},{25,17},{2,10},{3,... | collective-permute-start | bytes 1277960 | tf_op jit(solution)/shard_map/ppermute | solution.py:26
  4.5 0.5 collective-permute-start.2
  5.1 4.0 %collective-permute-start.6 = (bf16[32,4096]{1,0:T(8,128)(2,1)S(1)}, bf16[32,4096]{1,0:T(8,128)(2,1)S(1)}, u32[]{:S(2)}, u32[]{:S(2)}) collective-permute-start(bf16[32,4096]{1,0:T(8,128)(2,1)S(1)} %slice.19), channel_id=1, source_target_pairs={{0,224},{1,33},{32,0},{33,65},{64,32},{65,97},{96,64},{97,129},{12... | collective-permute-start | bytes 786440 | tf_op jit(solution)/shard_map/ppermute | solution.py:26
  9.1 2.2 %collective-permute-done.3 = bf16[32,4096]{1,0:T(8,128)(2,1)S(1)} collective-permute-done((bf16[32,4096]{1,0:T(8,128)(2,1)S(1)}, bf16[32,4096]{1,0:T(8,128)(2,1)S(1)}, u32[]{:S(2)}, u32[]{:S(2)}) %collective-permute-start.3) | collective-permute-done | bytes 262176 | tf_op jit(solution)/shard_map/ppermute | solution.py:26
  11.3 0.7 constant_dynamic-update-slice_fusion.3
  12.1 0.9 collective-permute-done.6
  13.0 3.7 %collective-permute-start.7 = (bf16[32,4096]{1,0:T(8,128)(2,1)S(1)}, bf16[32,4096]{1,0:T(8,128)(2,1)S(1)}, u32[]{:S(2)}, u32[]{:S(2)}) collective-permute-start(bf16[32,4096]{1,0:T(8,128)(2,1)S(1)} %collective-permute-done.6), channel_id=1, source_target_pairs={{0,224},{1,33},{32,0},{33,65},{64,32},{65,97},{96,64},{97,129},{12... | collective-permute-start | bytes 786440 | tf_op jit(solution)/shard_map/ppermute | solution.py:26
  16.7 0.7 constant_dynamic-update-slice_fusion.2
  17.4 1.5 %collective-permute-start.1 = (bf16[32,6656]{1,0:T(8,128)(2,1)S(1)}, bf16[32,6656]{1,0:T(8,128)(2,1)S(1)}, u32[]{:S(2)}, u32[]{:S(2)}) collective-permute-start(bf16[32,6656]{1,0:T(8,128)(2,1)S(1)} %collective-permute-done.refs_1_), channel_id=1, source_target_pairs={{0,8},{1,25},{8,16},{9,1},{16,24},{17,9},{24,0},{25,17},{2,10},{3,... | collective-permute-start | bytes 1277960 | tf_op jit(solution)/shard_map/ppermute | solution.py:26
  18.9 1.7 %collective-permute-done.4 = bf16[32,4096]{1,0:T(8,128)(2,1)S(1)} collective-permute-done((bf16[32,4096]{1,0:T(8,128)(2,1)S(1)}, bf16[32,4096]{1,0:T(8,128)(2,1)S(1)}, u32[]{:S(2)}, u32[]{:S(2)}) %collective-permute-start.4) | collective-permute-done | bytes 262176 | tf_op jit(solution)/shard_map/ppermute | solution.py:26
  20.6 0.7 constant_dynamic-update-slice_fusion.1
  21.3 0.7 constant_dynamic-update-slice_fusion.refs_4_
  22.0 1.5 %collective-permute-start.10 = (bf16[128,4096]{1,0:T(8,128)(2,1)}, bf16[128,4096]{1,0:T(8,128)(2,1)}, u32[]{:S(2)}, u32[]{:S(2)}) collective-permute-start(bf16[128,4096]{1,0:T(8,128)(2,1)} %constant_dynamic-update-slice_fusion.refs_4_), channel_id=1, source_target_pairs={{0,8},{1,25},{8,16},{9,1},{16,24},{17,9},{24,0},{25,17},{2,10},{3,... | collective-permute-start | bytes 3145736 | tf_op jit(solution)/shard_map/ppermute | solution.py:26
  23.5 0.0 slice-start
  23.6 0.7 copy-done.4
  24.4 1.7 %collective-permute-start.5 = (bf16[32,4096]{1,0:T(8,128)(2,1)S(1)}, bf16[32,4096]{1,0:T(8,128)(2,1)}, u32[]{:S(2)}, u32[]{:S(2)}) collective-permute-start(bf16[32,4096]{1,0:T(8,128)(2,1)S(1)} %collective-permute-done.4), channel_id=1, source_target_pairs={{0,32},{1,225},{32,64},{33,1},{64,96},{65,33},{96,128},{97,65},{12... | collective-permute-start | bytes 786440 | tf_op jit(solution)/shard_map/ppermute | solution.py:26
  26.0 1.8 %collective-permute-start.8 = (bf16[32,4096]{1,0:T(8,128)(2,1)S(1)}, bf16[32,4096]{1,0:T(8,128)(2,1)}, u32[]{:S(2)}, u32[]{:S(2)}) collective-permute-start(bf16[32,4096]{1,0:T(8,128)(2,1)S(1)} %collective-permute-done.7), channel_id=1, source_target_pairs={{0,224},{1,33},{32,0},{33,65},{64,32},{65,97},{96,64},{97,129},{12... | collective-permute-start | bytes 786440 | tf_op jit(solution)/shard_map/ppermute | solution.py:26
  27.9 0.8 copy-done.6
  28.6 0.9 pad_maximum_fusion.1
  29.5 5.5 %collective-permute-done.5 = bf16[32,4096]{1,0:T(8,128)(2,1)} collective-permute-done((bf16[32,4096]{1,0:T(8,128)(2,1)S(1)}, bf16[32,4096]{1,0:T(8,128)(2,1)}, u32[]{:S(2)}, u32[]{:S(2)}) %collective-permute-start.5) | collective-permute-done | bytes 262176 | tf_op jit(solution)/shard_map/ppermute | solution.py:26
  35.0 3.1 %collective-permute-start.9 = (bf16[128,2560]{1,0:T(8,128)(2,1)}, bf16[128,2560]{1,0:T(8,128)(2,1)}, u32[]{:S(2)}, u32[]{:S(2)}) collective-permute-start(bf16[128,2560]{1,0:T(8,128)(2,1)} %pad_maximum_fusion.1), channel_id=1, source_target_pairs={{0,32},{1,225},{32,64},{33,1},{64,96},{65,33},{96,128},{97,65},{12... | collective-permute-start | bytes 1966088 | tf_op jit(solution)/shard_map/ppermute | solution.py:26
  38.1 3.9 %collective-permute-start.17 = (bf16[32,4096]{1,0:T(8,128)(2,1)}, bf16[32,4096]{1,0:T(8,128)(2,1)}, u32[]{:S(2)}, u32[]{:S(2)}) collective-permute-start(bf16[32,4096]{1,0:T(8,128)(2,1)} %collective-permute-done.5), channel_id=1, source_target_pairs={{0,32},{1,225},{32,64},{33,1},{64,96},{65,33},{96,128},{97,65},{12... | collective-permute-start | bytes 786440 | tf_op jit(solution)/shard_map/ppermute | solution.py:26
  42.0 0.5 broadcast.4
  42.5 0.6 reduce.4
  43.1 0.1 reshape.19.ids_ref
  43.2 0.7 stack.23.info
  43.8 1.2 copy-done.3
  45.0 0.7 copy-done.10
  45.7 0.7 copy-done.11
  46.4 1.6 %plan.1 = (bf16[1024,64]{1,0:T(8,128)(2,1)S(1)}, bf16[128,256]{1,0:T(8,128)(2,1)S(1)}, bf16[128,2048]{1,0:T(8,128)(2,1)S(1)}, bf16[64,6656]{1,0:T(8,128)(2,1)S(1)}) custom-call(s32[5]{0:T(128)S(1)} %copy-done.11, s32[32,32]{1,0:T(8,128)S(1)} %reshape.19.ids_ref, bf16[64,6656]{1,0:T(8,128)(2,1)S(1)} %bitcast.15, f32[1,6656]{1,0:T(1,128)S(1)} %copy-done.10), custom_call_target="tpu_custom_call" | custom-call | flops 1048576 | bytes 4194304 | tf_op jit(solution)/shard_map/plan/pallas_call | solution.py:270
  48.0 4.6 %collective-permute-done.9.refs_0_ = bf16[128,2560]{1,0:T(8,128)(2,1)} collective-permute-done((bf16[128,2560]{1,0:T(8,128)(2,1)}, bf16[128,2560]{1,0:T(8,128)(2,1)}, u32[]{:S(2)}, u32[]{:S(2)}) %collective-permute-start.9) | collective-permute-done | bytes 655392 | tf_op jit(solution)/shard_map/ppermute | solution.py:26
  52.5 2.2 %collective-permute-start.11 = (bf16[128,2560]{1,0:T(8,128)(2,1)}, bf16[128,2560]{1,0:T(8,128)(2,1)S(1)}, u32[]{:S(2)}, u32[]{:S(2)}) collective-permute-start(bf16[128,2560]{1,0:T(8,128)(2,1)} %collective-permute-done.9.refs_0_), channel_id=1, source_target_pairs={{0,32},{1,225},{32,64},{33,1},{64,96},{65,33},{96,128},{97,65},{12... | collective-permute-start | bytes 1966088 | tf_op jit(solution)/shard_map/ppermute | solution.py:26
  54.7 2.2 %collective-permute-done.17 = bf16[32,4096]{1,0:T(8,128)(2,1)} collective-permute-done((bf16[32,4096]{1,0:T(8,128)(2,1)}, bf16[32,4096]{1,0:T(8,128)(2,1)}, u32[]{:S(2)}, u32[]{:S(2)}) %collective-permute-start.17) | collective-permute-done | bytes 262176 | tf_op jit(solution)/shard_map/ppermute | solution.py:26
  56.9 1.2 pad_maximum_fusion.refs_3_
  58.1 0.2 collective-permute-start.18
  58.3 1.6 %collective-permute-done.13.refs_1_ = bf16[128,2560]{1,0:T(8,128)(2,1)} collective-permute-done((bf16[128,2560]{1,0:T(8,128)(2,1)}, bf16[128,2560]{1,0:T(8,128)(2,1)}, u32[]{:S(2)}, u32[]{:S(2)}) %collective-permute-start.13) | collective-permute-done | bytes 655392 | tf_op jit(solution)/shard_map/ppermute | solution.py:26
  60.0 1.2 collective-permute-start.15
  61.2 2.9 %copy-done = bf16[6656,512]{1,0:T(8,128)(2,1)S(1)} copy-done((bf16[6656,512]{1,0:T(8,128)(2,1)S(1)}, bf16[6656,512]{1,0:T(8,128)(2,1)}, u32[]{:S(2)}) %copy-start) | copy-done | bytes 6815768
  64.1 2.2 %own.1 = (bf16[128,512]{1,0:T(8,128)(2,1)S(1)}, f32[64,64]{1,0:T(8,128)S(1)}) custom-call(bf16[32,6656]{1,0:T(8,128)(2,1)S(1)} %copy-done.2, bf16[32,6656]{1,0:T(8,128)(2,1)S(1)} %collective-permute-done.refs_1_, bf16[32,6656]{1,0:T(8,128)(2,1)S(1)} %copy-done.7, bf16[32,6656]{1,0:T(8,128)(2,1)S(1)} %copy-done.5, bf16[6656,512]{1,0:T(8,128)(2,1)S(1)} %copy-done, ...), custom_call_target="tpu_custom_call" | custom-call | flops 981467136 | bytes 4194304 | tf_op jit(solution)/shard_map/own/pallas_call | solution.py:314
  66.3 3.5 %collective-permute-done.11.refs_2_ = bf16[128,2560]{1,0:T(8,128)(2,1)S(1)} collective-permute-done((bf16[128,2560]{1,0:T(8,128)(2,1)}, bf16[128,2560]{1,0:T(8,128)(2,1)S(1)}, u32[]{:S(2)}, u32[]{:S(2)}) %collective-permute-start.11) | collective-permute-done | bytes 655392 | tf_op jit(solution)/shard_map/ppermute | solution.py:26
  69.9 2.4 %collective-permute-start.12 = (bf16[128,2560]{1,0:T(8,128)(2,1)S(1)}, bf16[128,2560]{1,0:T(8,128)(2,1)S(1)}, u32[]{:S(2)}, u32[]{:S(2)}) collective-permute-start(bf16[128,2560]{1,0:T(8,128)(2,1)S(1)} %collective-permute-done.11.refs_2_), channel_id=1, source_target_pairs={{0,32},{1,225},{32,64},{33,1},{64,96},{65,33},{96,128},{97,65},{12... | collective-permute-start | bytes 1966088 | tf_op jit(solution)/shard_map/ppermute | solution.py:26
  72.2 1.4 %collective-permute-start.21 = (bf16[128,4096]{1,0:T(8,128)(2,1)}, bf16[128,4096]{1,0:T(8,128)(2,1)S(1)}, u32[]{:S(2)}, u32[]{:S(2)}) collective-permute-start(bf16[128,4096]{1,0:T(8,128)(2,1)} %collective-permute-done.10.refs_5_), channel_id=1, source_target_pairs={{0,8},{1,25},{8,16},{9,1},{16,24},{17,9},{24,0},{25,17},{2,10},{3,... | collective-permute-start | bytes 3145736 | tf_op jit(solution)/shard_map/ppermute | solution.py:26
  73.6 0.6 collective-permute-start.22
  74.3 2.8 %collective-permute-done.15.refs_3_ = bf16[128,2560]{1,0:T(8,128)(2,1)S(1)} collective-permute-done((bf16[128,2560]{1,0:T(8,128)(2,1)}, bf16[128,2560]{1,0:T(8,128)(2,1)S(1)}, u32[]{:S(2)}, u32[]{:S(2)}) %collective-permute-start.15) | collective-permute-done | bytes 655392 | tf_op jit(solution)/shard_map/ppermute | solution.py:26
  77.1 1.4 %collective-permute-start.20 = (bf16[128,2560]{1,0:T(8,128)(2,1)S(1)}, bf16[128,2560]{1,0:T(8,128)(2,1)S(1)}, u32[]{:S(2)}, u32[]{:S(2)}) collective-permute-start(bf16[128,2560]{1,0:T(8,128)(2,1)S(1)} %collective-permute-done.15.refs_3_), channel_id=1, source_target_pairs={{0,224},{1,33},{32,0},{33,65},{64,32},{65,97},{96,64},{97,129},{12... | collective-permute-start | bytes 1966088 | tf_op jit(solution)/shard_map/ppermute | solution.py:26
  78.5 1.4 collective-permute-start.19
  79.8 6.2 %near.1 = (f32[512,576]{1,0:T(8,128)S(1)}, f32[384,576]{1,0:T(8,128)S(1)}) custom-call(bf16[128,2560]{1,0:T(8,128)(2,1)} %collective-permute-done.9.refs_0_, bf16[128,2560]{1,0:T(8,128)(2,1)} %collective-permute-done.13.refs_1_, bf16[128,2560]{1,0:T(8,128)(2,1)S(1)} %collective-permute-done.11.refs_2_, ...), custom_call_target="tpu_custom_call" | custom-call | flops 3435134976 | bytes 4194304 | tf_op jit(solution)/shard_map/near/pallas_call | solution.py:327
  86.0 2.1 %collective-permute-done.12.refs_0_ = bf16[128,2560]{1,0:T(8,128)(2,1)S(1)} collective-permute-done((bf16[128,2560]{1,0:T(8,128)(2,1)S(1)}, bf16[128,2560]{1,0:T(8,128)(2,1)S(1)}, u32[]{:S(2)}, u32[]{:S(2)}) %collective-permute-start.12) | collective-permute-done | bytes 655392 | tf_op jit(solution)/shard_map/ppermute | solution.py:26
  88.2 1.1 collective-permute-start.16
  89.3 4.8 %collective-permute-done.22.refs_5_ = bf16[96,4096]{1,0:T(8,128)(2,1)S(1)} collective-permute-done((bf16[96,4096]{1,0:T(8,128)(2,1)S(1)}, bf16[96,4096]{1,0:T(8,128)(2,1)S(1)}, u32[]{:S(2)}, u32[]{:S(2)}) %collective-permute-start.22) | collective-permute-done | bytes 786464 | tf_op jit(solution)/shard_map/ppermute | solution.py:26
  94.1 4.9 %far.1 = (bf16[512,512]{1,0:T(8,128)(2,1)S(1)}, f32[256,576]{1,0:T(8,128)S(1)}, f32[288,576]{1,0:T(8,128)S(1)}, f32[64,64]{1,0:T(8,128)S(1)}) custom-call(bf16[128,2560]{1,0:T(8,128)(2,1)S(1)} %collective-permute-done.12.refs_0_, bf16[128,2560]{1,0:T(8,128)(2,1)S(1)} %collective-permute-done.20.refs_1_, ...), custom_call_target="tpu_custom_call" | custom-call | flops 2699034624 | bytes 4194304 | tf_op jit(solution)/shard_map/far/pallas_call | solution.py:339
  99.1 0.9 collective-permute-done.16.a
  100.0 4.3 %last.1 = (f32[64,128]{1,0:T(8,128)}, bf16[512,512]{1,0:T(8,128)(2,1)S(1)}, bf16[512,512]{1,0:T(8,128)(2,1)}) custom-call(s32[5]{0:T(128)S(1)} %copy-done.12, bf16[128,2560]{1,0:T(8,128)(2,1)S(1)} %collective-permute-done.16.a, bf16[96,4096]{1,0:T(8,128)(2,1)S(1)} %collective-permute-done.19.far, bf16[6656,512]{1,0:T(8,128)(2,1)S(1)} %bitcast.13, ...), custom_call_target="tpu_custom_call" | custom-call | flops 981467136 | bytes 4194304 | tf_op jit(solution)/shard_map/last/pallas_call | solution.py:353
  104.3 0.1 collective-permute-start.23
  104.4 4.6 %all-to-all-start = ((f32[8,8,128]{2,1,0:T(8,128)}), f32[8,8,128]{2,1,0:T(8,128)S(1)}, u32[]{:S(2)}, u32[]{:S(2)}) async-start(f32[8,8,128]{2,1,0:T(8,128)} %bitcast.6), calls=%async_computation | async-start | bytes 65536 | tf_op jit(solution)/shard_map/all_to_all | solution.py:363
  109.0 0.1 pair.1
  109.1 2.1 %collective-permute-start.24 = (bf16[128,512]{1,0:T(8,128)(2,1)S(1)}, bf16[128,512]{1,0:T(8,128)(2,1)S(1)}, u32[]{:S(2)}, u32[]{:S(2)}) collective-permute-start(bf16[128,512]{1,0:T(8,128)(2,1)S(1)} %get-tuple-element.52), channel_id=1, source_target_pairs={{0,2},{2,4},{4,6},{6,0},{1,3},{3,5},{5,7},{7,1},{8,10},{10,12},{12... | collective-permute-start | bytes 393224 | tf_op jit(solution)/shard_map/ppermute | solution.py:374
  111.2 2.7 %collective-permute-start.25 = (bf16[128,512]{1,0:T(8,128)(2,1)S(1)}, bf16[128,512]{1,0:T(8,128)(2,1)S(1)}, u32[]{:S(2)}, u32[]{:S(2)}) collective-permute-start(bf16[128,512]{1,0:T(8,128)(2,1)S(1)} %get-tuple-element.53), channel_id=1, source_target_pairs={{0,4},{2,6},{4,0},{6,2},{1,5},{3,7},{5,1},{7,3},{8,12},{10,14},{12... | collective-permute-start | bytes 393224 | tf_op jit(solution)/shard_map/ppermute | solution.py:374
  113.9 1.5 %collective-permute-start.26 = (bf16[128,512]{1,0:T(8,128)(2,1)S(1)}, bf16[128,512]{1,0:T(8,128)(2,1)S(1)}, u32[]{:S(2)}, u32[]{:S(2)}) collective-permute-start(bf16[128,512]{1,0:T(8,128)(2,1)S(1)} %get-tuple-element.54), channel_id=1, source_target_pairs={{0,6},{2,0},{4,2},{6,4},{1,7},{3,1},{5,3},{7,5},{8,14},{10,8},{12,... | collective-permute-start | bytes 393224 | tf_op jit(solution)/shard_map/ppermute | solution.py:374
  115.4 16.9 %all_to_all.15 = bf16[32,8,128]{2,1,0:T(8,128)(2,1)S(1)} all-to-all(bf16[32,8,128]{2,1,0:T(8,128)(2,1)S(1)} %broadcast_in_dim.2), channel_id=1, replica_groups=mesh['z'=8,'x'=4,'y'=4,'core'=2] {'z','x'}, dimensions={0} | all-to-all | bytes 131072 | tf_op jit(solution)/shard_map/all_to_all | solution.py:366
  132.4 1.6 %copy-done.1 = bf16[32,64,512]{2,1,0:T(8,128)(2,1)S(1)} copy-done((bf16[32,64,512]{2,1,0:T(8,128)(2,1)S(1)}, bf16[32,64,512]{2,1,0:T(8,128)(2,1)}, u32[]{:S(2)}) %copy-start.1) | copy-done | bytes 2097176
  133.9 1.8 %sum.1 = bf16[128,512]{1,0:T(8,128)(2,1)} custom-call(s32[5]{0:T(128)S(1)} %copy-done.12, bf16[256,128]{1,0:T(8,128)(2,1)S(1)} %bitcast.16, bf16[128,256]{1,0:T(8,128)(2,1)S(1)} %get-tuple-element.40.pick, bf16[128,2048]{1,0:T(8,128)(2,1)S(1)} %copy-done.9, bf16[2048,512]{1,0:T(8,128)(2,1)S(1)} %bitcast.14, f32[128,512]{1,0:T(8,128)S(1)} %get-tuple-element.51.refs_0_, ...), custom_call_target="tpu_custom_call" | custom-call | flops 268435456 | bytes 4194304 | tf_op jit(solution)/shard_map/sum/pallas_call | solution.py:375
  (50 shorter events, 0.2 us)
Async XLA Ops:
  0.0 23.5 %copy-start.2 = (bf16[32,6656]{1,0:T(8,128)(2,1)S(1)}, bf16[32,6656]{1,0:T(8,128)(2,1)}, u32[]{:S(2)}) copy-start(bf16[32,6656]{1,0:T(8,128)(2,1)} %refs_0_.1) | copy-start | bytes 1277956
  1.0 10.3 %collective-permute-start.3 = (bf16[32,4096]{1,0:T(8,128)(2,1)S(1)}, bf16[32,4096]{1,0:T(8,128)(2,1)S(1)}, u32[]{:S(2)}, u32[]{:S(2)}) collective-permute-start(bf16[32,4096]{1,0:T(8,128)(2,1)S(1)} %slice.19), channel_id=1, source_target_pairs={{0,32},{1,225},{32,64},{33,1},{64,96},{65,33},{96,128},{97,65},{12... | collective-permute-start | bytes 786440 | tf_op jit(solution)/shard_map/ppermute | solution.py:26
  3.0 14.4 %collective-permute-start = (bf16[32,6656]{1,0:T(8,128)(2,1)}, bf16[32,6656]{1,0:T(8,128)(2,1)S(1)}, u32[]{:S(2)}, u32[]{:S(2)}) collective-permute-start(bf16[32,6656]{1,0:T(8,128)(2,1)} %refs_0_.1), channel_id=1, source_target_pairs={{0,8},{1,25},{8,16},{9,1},{16,24},{17,9},{24,0},{25,17},{2,10},{3,... | collective-permute-start | bytes 1277960 | tf_op jit(solution)/shard_map/ppermute | solution.py:26
  4.5 19.0 %collective-permute-start.2 = (bf16[32,6656]{1,0:T(8,128)(2,1)}, bf16[32,6656]{1,0:T(8,128)(2,1)S(1)}, u32[]{:S(2)}, u32[]{:S(2)}) collective-permute-start(bf16[32,6656]{1,0:T(8,128)(2,1)} %refs_0_.1), channel_id=1, source_target_pairs={{0,24},{1,9},{8,0},{9,17},{16,8},{17,25},{24,16},{25,1},{2,26},{3,... | collective-permute-start | bytes 1277960 | tf_op jit(solution)/shard_map/ppermute | solution.py:26
  5.1 7.9 %collective-permute-start.6 = (bf16[32,4096]{1,0:T(8,128)(2,1)S(1)}, bf16[32,4096]{1,0:T(8,128)(2,1)S(1)}, u32[]{:S(2)}, u32[]{:S(2)}) collective-permute-start(bf16[32,4096]{1,0:T(8,128)(2,1)S(1)} %slice.19), channel_id=1, source_target_pairs={{0,224},{1,33},{32,0},{33,65},{64,32},{65,97},{96,64},{97,129},{12... | collective-permute-start | bytes 786440 | tf_op jit(solution)/shard_map/ppermute | solution.py:26
  11.3 9.2 %collective-permute-start.4 = (bf16[32,4096]{1,0:T(8,128)(2,1)S(1)}, bf16[32,4096]{1,0:T(8,128)(2,1)S(1)}, u32[]{:S(2)}, u32[]{:S(2)}) collective-permute-start(bf16[32,4096]{1,0:T(8,128)(2,1)S(1)} %collective-permute-done.3), channel_id=1, source_target_pairs={{0,32},{1,225},{32,64},{33,1},{64,96},{65,33},{96,128},{97,65},{12... | collective-permute-start | bytes 786440 | tf_op jit(solution)/shard_map/ppermute | solution.py:26
  13.0 8.3 %collective-permute-start.7 = (bf16[32,4096]{1,0:T(8,128)(2,1)S(1)}, bf16[32,4096]{1,0:T(8,128)(2,1)S(1)}, u32[]{:S(2)}, u32[]{:S(2)}) collective-permute-start(bf16[32,4096]{1,0:T(8,128)(2,1)S(1)} %collective-permute-done.6), channel_id=1, source_target_pairs={{0,224},{1,33},{32,0},{33,65},{64,32},{65,97},{96,64},{97,129},{12... | collective-permute-start | bytes 786440 | tf_op jit(solution)/shard_map/ppermute | solution.py:26
  17.4 10.4 %collective-permute-start.1 = (bf16[32,6656]{1,0:T(8,128)(2,1)S(1)}, bf16[32,6656]{1,0:T(8,128)(2,1)S(1)}, u32[]{:S(2)}, u32[]{:S(2)}) collective-permute-start(bf16[32,6656]{1,0:T(8,128)(2,1)S(1)} %collective-permute-done.refs_1_), channel_id=1, source_target_pairs={{0,8},{1,25},{8,16},{9,1},{16,24},{17,9},{24,0},{25,17},{2,10},{3,... | collective-permute-start | bytes 1277960 | tf_op jit(solution)/shard_map/ppermute | solution.py:26
  22.0 20.5 %copy-start.13 = (s32[1024,1]{0,1:T(1,128)S(1)}, s32[1024,1]{0,1:T(1,128)}, u32[]{:S(2)}) copy-start(s32[1024,1]{0,1:T(1,128)} %param.11) | copy-start | bytes 12292
  22.0 30.5 %collective-permute-start.10 = (bf16[128,4096]{1,0:T(8,128)(2,1)}, bf16[128,4096]{1,0:T(8,128)(2,1)}, u32[]{:S(2)}, u32[]{:S(2)}) collective-permute-start(bf16[128,4096]{1,0:T(8,128)(2,1)} %constant_dynamic-update-slice_fusion.refs_4_), channel_id=1, source_target_pairs={{0,8},{1,25},{8,16},{9,1},{16,24},{17,9},{24,0},{25,17},{2,10},{3,... | collective-permute-start | bytes 3145736 | tf_op jit(solution)/shard_map/ppermute | solution.py:26
  23.5 56.3 %slice-start = ((s8[6815744]{0:T(1024)(128)(4,1)}), s8[2621440]{0:T(1024)(128)(4,1)S(1)}, s32[]{:S(2)}) async-start(s8[6815744]{0:T(1024)(128)(4,1)} %bitcast.12), calls=%async_computation.2 | async-start | bytes 5242880
  23.6 0.8 copy-start.4
  24.4 10.6 %collective-permute-start.5 = (bf16[32,4096]{1,0:T(8,128)(2,1)S(1)}, bf16[32,4096]{1,0:T(8,128)(2,1)}, u32[]{:S(2)}, u32[]{:S(2)}) collective-permute-start(bf16[32,4096]{1,0:T(8,128)(2,1)S(1)} %collective-permute-done.4), channel_id=1, source_target_pairs={{0,32},{1,225},{32,64},{33,1},{64,96},{65,33},{96,128},{97,65},{12... | collective-permute-start | bytes 786440 | tf_op jit(solution)/shard_map/ppermute | solution.py:26
  26.0 8.9 %collective-permute-start.8 = (bf16[32,4096]{1,0:T(8,128)(2,1)S(1)}, bf16[32,4096]{1,0:T(8,128)(2,1)}, u32[]{:S(2)}, u32[]{:S(2)}) collective-permute-start(bf16[32,4096]{1,0:T(8,128)(2,1)S(1)} %collective-permute-done.7), channel_id=1, source_target_pairs={{0,224},{1,33},{32,0},{33,65},{64,32},{65,97},{96,64},{97,129},{12... | collective-permute-start | bytes 786440 | tf_op jit(solution)/shard_map/ppermute | solution.py:26
  27.9 0.8 copy-start.6
  35.0 17.5 %collective-permute-start.9 = (bf16[128,2560]{1,0:T(8,128)(2,1)}, bf16[128,2560]{1,0:T(8,128)(2,1)}, u32[]{:S(2)}, u32[]{:S(2)}) collective-permute-start(bf16[128,2560]{1,0:T(8,128)(2,1)} %pad_maximum_fusion.1), channel_id=1, source_target_pairs={{0,32},{1,225},{32,64},{33,1},{64,96},{65,33},{96,128},{97,65},{12... | collective-permute-start | bytes 1966088 | tf_op jit(solution)/shard_map/ppermute | solution.py:26
  38.1 21.9 %collective-permute-start.14 = (bf16[128,4096]{1,0:T(8,128)(2,1)}, bf16[128,4096]{1,0:T(8,128)(2,1)}, u32[]{:S(2)}, u32[]{:S(2)}) collective-permute-start(bf16[128,4096]{1,0:T(8,128)(2,1)} %constant_dynamic-update-slice_fusion.refs_4_), channel_id=1, source_target_pairs={{0,24},{1,9},{8,0},{9,17},{16,8},{17,25},{24,16},{25,1},{2,26},{3,... | collective-permute-start | bytes 3145736 | tf_op jit(solution)/shard_map/ppermute | solution.py:26
  38.1 18.9 %collective-permute-start.17 = (bf16[32,4096]{1,0:T(8,128)(2,1)}, bf16[32,4096]{1,0:T(8,128)(2,1)}, u32[]{:S(2)}, u32[]{:S(2)}) collective-permute-start(bf16[32,4096]{1,0:T(8,128)(2,1)} %collective-permute-done.5), channel_id=1, source_target_pairs={{0,32},{1,225},{32,64},{33,1},{64,96},{65,33},{96,128},{97,65},{12... | collective-permute-start | bytes 786440 | tf_op jit(solution)/shard_map/ppermute | solution.py:26
  42.0 18.0 %collective-permute-start.13 = (bf16[128,2560]{1,0:T(8,128)(2,1)}, bf16[128,2560]{1,0:T(8,128)(2,1)}, u32[]{:S(2)}, u32[]{:S(2)}) collective-permute-start(bf16[128,2560]{1,0:T(8,128)(2,1)} %pad_maximum_fusion.1), channel_id=1, source_target_pairs={{0,224},{1,33},{32,0},{33,65},{64,32},{65,97},{96,64},{97,129},{12... | collective-permute-start | bytes 1966088 | tf_op jit(solution)/shard_map/ppermute | solution.py:26
  43.8 1.2 copy-start.3
  45.0 0.7 copy-start.10
  45.7 0.7 copy-start.11
  46.4 14.8 %copy-start.5 = (bf16[32,6656]{1,0:T(8,128)(2,1)S(1)}, bf16[32,6656]{1,0:T(8,128)(2,1)}, u32[]{:S(2)}) copy-start(bf16[32,6656]{1,0:T(8,128)(2,1)} %copy-done.4) | copy-start | bytes 1277956
  46.4 14.8 %copy-start.7 = (bf16[32,6656]{1,0:T(8,128)(2,1)S(1)}, bf16[32,6656]{1,0:T(8,128)(2,1)}, u32[]{:S(2)}) copy-start(bf16[32,6656]{1,0:T(8,128)(2,1)} %copy-done.6) | copy-start | bytes 1277956
  48.0 18.4 %copy-start.8 = (bf16[128,2048]{1,0:T(8,128)(2,1)}, bf16[128,2048]{1,0:T(8,128)(2,1)S(1)}, u32[]{:S(2)}) copy-start(bf16[128,2048]{1,0:T(8,128)(2,1)S(1)} %get-tuple-element.41.mask) | copy-start | bytes 1572868
  52.5 17.3 %collective-permute-start.11 = (bf16[128,2560]{1,0:T(8,128)(2,1)}, bf16[128,2560]{1,0:T(8,128)(2,1)S(1)}, u32[]{:S(2)}, u32[]{:S(2)}) collective-permute-start(bf16[128,2560]{1,0:T(8,128)(2,1)} %collective-permute-done.9.refs_0_), channel_id=1, source_target_pairs={{0,32},{1,225},{32,64},{33,1},{64,96},{65,33},{96,128},{97,65},{12... | collective-permute-start | bytes 1966088 | tf_op jit(solution)/shard_map/ppermute | solution.py:26
  58.1 20.4 %collective-permute-start.18 = (bf16[96,4096]{1,0:T(8,128)(2,1)S(1)}, bf16[96,4096]{1,0:T(8,128)(2,1)S(1)}, u32[]{:S(2)}, u32[]{:S(2)}) collective-permute-start(bf16[96,4096]{1,0:T(8,128)(2,1)S(1)} %pad_maximum_fusion.refs_3_), channel_id=1, source_target_pairs={{0,8},{1,25},{8,16},{9,1},{16,24},{17,9},{24,0},{25,17},{2,10},{3,... | collective-permute-start | bytes 2359304 | tf_op jit(solution)/shard_map/ppermute | solution.py:26
  60.0 17.1 %collective-permute-start.15 = (bf16[128,2560]{1,0:T(8,128)(2,1)}, bf16[128,2560]{1,0:T(8,128)(2,1)S(1)}, u32[]{:S(2)}, u32[]{:S(2)}) collective-permute-start(bf16[128,2560]{1,0:T(8,128)(2,1)} %collective-permute-done.13.refs_1_), channel_id=1, source_target_pairs={{0,224},{1,33},{32,0},{33,65},{64,32},{65,97},{96,64},{97,129},{12... | collective-permute-start | bytes 1966088 | tf_op jit(solution)/shard_map/ppermute | solution.py:26
  61.2 2.9 %copy-start = (bf16[6656,512]{1,0:T(8,128)(2,1)S(1)}, bf16[6656,512]{1,0:T(8,128)(2,1)}, u32[]{:S(2)}) copy-start(bf16[6656,512]{1,0:T(8,128)(2,1)} %w.1) | copy-start | bytes 20447236
  64.1 15.7 %slice-start.1 = ((s8[6815744]{0:T(1024)(128)(4,1)}), s8[4194304]{0:T(1024)(128)(4,1)S(1)}, s32[]{:S(2)}) async-start(s8[6815744]{0:T(1024)(128)(4,1)} %bitcast.12), calls=%async_computation.3 | async-start | bytes 8388608
  69.9 18.3 %collective-permute-start.12 = (bf16[128,2560]{1,0:T(8,128)(2,1)S(1)}, bf16[128,2560]{1,0:T(8,128)(2,1)S(1)}, u32[]{:S(2)}, u32[]{:S(2)}) collective-permute-start(bf16[128,2560]{1,0:T(8,128)(2,1)S(1)} %collective-permute-done.11.refs_2_), channel_id=1, source_target_pairs={{0,32},{1,225},{32,64},{33,1},{64,96},{65,33},{96,128},{97,65},{12... | collective-permute-start | bytes 1966088 | tf_op jit(solution)/shard_map/ppermute | solution.py:26
  72.2 21.9 %collective-permute-start.21 = (bf16[128,4096]{1,0:T(8,128)(2,1)}, bf16[128,4096]{1,0:T(8,128)(2,1)S(1)}, u32[]{:S(2)}, u32[]{:S(2)}) collective-permute-start(bf16[128,4096]{1,0:T(8,128)(2,1)} %collective-permute-done.10.refs_5_), channel_id=1, source_target_pairs={{0,8},{1,25},{8,16},{9,1},{16,24},{17,9},{24,0},{25,17},{2,10},{3,... | collective-permute-start | bytes 3145736 | tf_op jit(solution)/shard_map/ppermute | solution.py:26
  73.6 20.5 %collective-permute-start.22 = (bf16[96,4096]{1,0:T(8,128)(2,1)S(1)}, bf16[96,4096]{1,0:T(8,128)(2,1)S(1)}, u32[]{:S(2)}, u32[]{:S(2)}) collective-permute-start(bf16[96,4096]{1,0:T(8,128)(2,1)S(1)} %pad_maximum_fusion.refs_3_), channel_id=1, source_target_pairs={{0,24},{1,9},{8,0},{9,17},{16,8},{17,25},{24,16},{25,1},{2,26},{3,... | collective-permute-start | bytes 2359304 | tf_op jit(solution)/shard_map/ppermute | solution.py:26
  77.1 17.0 %collective-permute-start.20 = (bf16[128,2560]{1,0:T(8,128)(2,1)S(1)}, bf16[128,2560]{1,0:T(8,128)(2,1)S(1)}, u32[]{:S(2)}, u32[]{:S(2)}) collective-permute-start(bf16[128,2560]{1,0:T(8,128)(2,1)S(1)} %collective-permute-done.15.refs_3_), channel_id=1, source_target_pairs={{0,224},{1,33},{32,0},{33,65},{64,32},{65,97},{96,64},{97,129},{12... | collective-permute-start | bytes 1966088 | tf_op jit(solution)/shard_map/ppermute | solution.py:26
  78.5 20.6 %collective-permute-start.19 = (bf16[96,4096]{1,0:T(8,128)(2,1)S(1)}, bf16[96,4096]{1,0:T(8,128)(2,1)S(1)}, u32[]{:S(2)}, u32[]{:S(2)}) collective-permute-start(bf16[96,4096]{1,0:T(8,128)(2,1)S(1)} %collective-permute-done.18.refs_4_), channel_id=1, source_target_pairs={{0,8},{1,25},{8,16},{9,1},{16,24},{17,9},{24,0},{25,17},{2,10},{3,... | collective-permute-start | bytes 2359304 | tf_op jit(solution)/shard_map/ppermute | solution.py:26
  88.2 11.8 %collective-permute-start.16 = (bf16[128,2560]{1,0:T(8,128)(2,1)S(1)}, bf16[128,2560]{1,0:T(8,128)(2,1)S(1)}, u32[]{:S(2)}, u32[]{:S(2)}) collective-permute-start(bf16[128,2560]{1,0:T(8,128)(2,1)S(1)} %collective-permute-done.12.refs_0_), channel_id=1, source_target_pairs={{0,32},{1,225},{32,64},{33,1},{64,96},{65,33},{96,128},{97,65},{12... | collective-permute-start | bytes 1966088 | tf_op jit(solution)/shard_map/ppermute | solution.py:26
  94.1 5.9 %copy-start.12 = (s32[5]{0:T(128)S(1)}, s32[5]{0:T(128)}, u32[]{:S(2)}) copy-start(s32[5]{0:T(128)} %stack.23.info) | copy-start | bytes 64
  104.3 28.1 %copy-start.9 = (bf16[128,2048]{1,0:T(8,128)(2,1)S(1)}, bf16[128,2048]{1,0:T(8,128)(2,1)}, u32[]{:S(2)}) copy-start(bf16[128,2048]{1,0:T(8,128)(2,1)} %copy-done.8) | copy-start | bytes 1572868
  104.3 4.7 %collective-permute-start.23 = (bf16[512,512]{1,0:T(8,128)(2,1)}, bf16[512,512]{1,0:T(8,128)(2,1)S(1)}, u32[]{:S(2)}, u32[]{:S(2)}) collective-permute-start(bf16[512,512]{1,0:T(8,128)(2,1)} %get-tuple-element.50), channel_id=1, source_target_pairs={{0,1},{1,0},{2,3},{3,2},{4,5},{5,4},{6,7},{7,6},{8,9},{9,8},{10,11... | collective-permute-start | bytes 1572872 | tf_op jit(solution)/shard_map/ppermute | solution.py:368
  104.4 11.0 %all-to-all-start = ((f32[8,8,128]{2,1,0:T(8,128)}), f32[8,8,128]{2,1,0:T(8,128)S(1)}, u32[]{:S(2)}, u32[]{:S(2)}) async-start(f32[8,8,128]{2,1,0:T(8,128)} %bitcast.6), calls=%async_computation | async-start | bytes 65536 | tf_op jit(solution)/shard_map/all_to_all | solution.py:363
  109.1 23.2 %collective-permute-start.24 = (bf16[128,512]{1,0:T(8,128)(2,1)S(1)}, bf16[128,512]{1,0:T(8,128)(2,1)S(1)}, u32[]{:S(2)}, u32[]{:S(2)}) collective-permute-start(bf16[128,512]{1,0:T(8,128)(2,1)S(1)} %get-tuple-element.52), channel_id=1, source_target_pairs={{0,2},{2,4},{4,6},{6,0},{1,3},{3,5},{5,7},{7,1},{8,10},{10,12},{12... | collective-permute-start | bytes 393224 | tf_op jit(solution)/shard_map/ppermute | solution.py:374
  111.2 21.1 %collective-permute-start.25 = (bf16[128,512]{1,0:T(8,128)(2,1)S(1)}, bf16[128,512]{1,0:T(8,128)(2,1)S(1)}, u32[]{:S(2)}, u32[]{:S(2)}) collective-permute-start(bf16[128,512]{1,0:T(8,128)(2,1)S(1)} %get-tuple-element.53), channel_id=1, source_target_pairs={{0,4},{2,6},{4,0},{6,2},{1,5},{3,7},{5,1},{7,3},{8,12},{10,14},{12... | collective-permute-start | bytes 393224 | tf_op jit(solution)/shard_map/ppermute | solution.py:374
  113.9 18.4 %collective-permute-start.26 = (bf16[128,512]{1,0:T(8,128)(2,1)S(1)}, bf16[128,512]{1,0:T(8,128)(2,1)S(1)}, u32[]{:S(2)}, u32[]{:S(2)}) collective-permute-start(bf16[128,512]{1,0:T(8,128)(2,1)S(1)} %get-tuple-element.54), channel_id=1, source_target_pairs={{0,6},{2,0},{4,2},{6,4},{1,7},{3,1},{5,3},{7,5},{8,14},{10,8},{12,... | collective-permute-start | bytes 393224 | tf_op jit(solution)/shard_map/ppermute | solution.py:374
  132.3 1.6 %copy-start.1 = (bf16[32,64,512]{2,1,0:T(8,128)(2,1)S(1)}, bf16[32,64,512]{2,1,0:T(8,128)(2,1)}, u32[]{:S(2)}) copy-start(bf16[32,64,512]{2,1,0:T(8,128)(2,1)} %param.10) | copy-start | bytes 6291460

commit v3 on v2

--- a/solution.py
+++ b/solution.py
@@ -13,6 +13,7 @@
 I32 = jnp.int32
 LANES = 128
 NEAR, FAR = (1, 7, 2, 6), (3, 5, 4)
+DELTA_COST = 8_000_000_000
 VMEM_LIMIT = 16 << 20
 
 
@@ -42,10 +43,9 @@
     return lax.broadcasted_iota(I32, shape, dim)
 
 
-def plan_kernel(info, ids_ref, levels, scale, fill, pick, mask, dense, slot_of, slot_all):
+def plan_kernel(info, ids_ref, levels, scale, fill, mine, dense, slot_of, slot_all):
     z, x, sign, t, me = (info[k] for k in range(5))
     rows = ids_ref.shape[1]
-    rank = levels.shape[0]
     dense[...] = (levels[...].astype(F32) * scale[...]).astype(BF16)
     ids = ids_ref[...]
     lane, sub = iota(ids.shape, 1), iota(ids.shape, 0)
@@ -68,13 +68,10 @@
             col = column(slot_of[pl.ds(source, 1), :])
             at = (i * 4 + j) * rows
             fill[at : at + rows, :] = ones(col == iota((rows, fill.shape[1]), 1))
-    rank_bits = rank.bit_length() - 1
+    lane = iota((rows, LANES), 1)
     for j in range(4):
-        at = slice(j * rows, (j + 1) * rows)
-        col = column(slot_all[pl.ds(t * 4 + j, 1), :])
-        pick[at, :] = ones(col == iota((rows, pick.shape[1]), 1))
-        col = column(ids_ref[pl.ds(t * 4 + j, 1), :])
-        mask[at, :] = ones(col == (iota((rows, mask.shape[1]), 1) >> rank_bits))
+        slot, adapter = (column(ref[pl.ds(t * 4 + j, 1), :]) for ref in (slot_all, ids_ref))
+        mine[j * rows : (j + 1) * rows, :] = jnp.where(lane == 0, slot, adapter)
 
 
 def start(pairs, sems):
@@ -95,12 +92,14 @@
     for at in range(0, depth, half):
         at = slice(at, at + half)
         rows = lhs[:, at]
-        base, shrink = dot(rows, w[at, :]), dot(rows, dense[:, at], ((1,), (1,)))
-        if at.start:
-            acc[:, :n] += base
-            acc[:, n:] += shrink
-        else:
-            acc[:, :n], acc[:, n:] = base, shrink
+        for to, value in ((slice(0, n), w), (slice(n, None), dense)):
+            if value is None:
+                continue
+            if value is w:
+                part = dot(rows, w[at, :])
+            else:
+                part = dot(rows, dense[:, at], ((1,), (1,)))
+            acc[:, to] = acc[:, to] + part if at.start else part
 
 
 def both_products(cut, first, second, w, d, rows_a, rows_b, acc_a, acc_b, sems):
@@ -178,13 +177,34 @@
     slots[...] = total
 
 
-def last_kernel(cut, info, a, far, w, d, fill, far_a, far_b, base_own, base_near, earlier,
-                slots, keep, send, acc_a, acc_b, base, sems):
-    multiply(a, w.at[:cut], d.at[:, :cut], acc_a)
-    multiply(far, w.at[cut:], d.at[:, cut:], acc_b)
+def slots_kernel(cut, a, far, d, fill, far_a, far_b, earlier, slots):
+    over = ((1,), (1,))
+    last_a, last_b = dot(a[...], d[:, :cut], over), dot(far[...], d[:, cut:], over)
+    n, rank = a.shape[0], d.shape[0]
+    rows, width = n // 4, far_a.shape[1] - rank
+    total = earlier[...]
+    for k, i in enumerate(FAR):
+        parts = []
+        for j in range(4):
+            if k == 2:
+                of_a = last_a[j * rows : (j + 1) * rows, :]
+            else:
+                of_a = far_a[k * n + j * rows : k * n + (j + 1) * rows, width:]
+            if j == 2:
+                of_b = last_b[k * rows : (k + 1) * rows, :]
+            else:
+                row_b = ((j if j < 2 else 2) * 3 + k) * rows
+                of_b = far_b[row_b : row_b + rows, width:]
+            parts.append((of_a + of_b).astype(BF16))
+        total += dot(fill[i * n : (i + 1) * n, :], stack(*parts), ((0,), (0,)))
+    slots[:, :rank], slots[:, rank:] = total, total
+
+
+def last_kernel(cut, info, a, far, w, far_a, far_b, base_own, base_near, keep, send, acc_a, acc_b, base, sems):
+    multiply(a, w.at[:cut], None, acc_a)
+    multiply(far, w.at[cut:], None, acc_b)
     n = a.shape[0]
-    rows = n // 4
-    total = earlier[...]
+    rows, width = n // 4, base.shape[1]
     base[:n, :] = base_own[...]
     for k, i in enumerate(NEAR):
         base[i * n : (i + 1) * n, :] = base_near[k * n : (k + 1) * n, :]
@@ -193,16 +213,14 @@
         for j in range(4):
             of_a = acc_a[j * rows : (j + 1) * rows, :] if k == 2 else None
             if k < 2:
-                of_a = far_a[k * n + j * rows : k * n + (j + 1) * rows, :]
+                of_a = far_a[k * n + j * rows : k * n + (j + 1) * rows, :width]
             if j == 2:
                 of_b = acc_b[k * rows : (k + 1) * rows, :]
             else:
                 row_b = ((j if j < 2 else 2) * 3 + k) * rows
-                of_b = far_b[row_b : row_b + rows, :]
+                of_b = far_b[row_b : row_b + rows, :width]
             parts.append(of_a + of_b)
-        total += finish(base, i * n, fill, i, parts)
-    rank = total.shape[1]
-    slots[:, :rank], slots[:, rank:] = total, total
+        base[i * n : (i + 1) * n, :] = stack(*parts).astype(BF16)
     z, sign, t = info[0], info[2], info[3]
     core = t & 1
     copies = []
@@ -224,14 +242,25 @@
         ref[...] = both.astype(ref.dtype)
 
 
-def sum_kernel(info, slots, pick, mask, up, *refs):
+def load_kernel(source, out):
+    out[...] = source[...]
+
+
+def delta_kernel(rank, slots, mine, up, delta):
+    slot, adapter = mine[:, :1], mine[:, 1:2]
+    n = mine.shape[0]
+    pick = jnp.where(slot == iota((n, slots.shape[0]), 1), 1.0, 0.0).astype(BF16)
+    rows = dot(pick, slots[...]).astype(BF16)
+    spread = jnp.concatenate([rows] * (up.shape[0] // LANES), axis=1)
+    chosen = adapter == (iota(spread.shape, 1) >> (rank.bit_length() - 1))
+    delta[...] = dot(jnp.where(chosen, spread, jnp.zeros((), BF16)), up[...])
+
+
+def sum_kernel(info, delta, *refs):
     got, out, total = refs[:4], refs[4], refs[5]
     x, sign = info[1], info[2]
     rows = out.shape[0] // 4
     total[...] = sum(ref[...].astype(F32) for ref in got)
-    mine = dot(pick[...], slots[...]).astype(BF16)
-    spread = jnp.concatenate([mine] * (mask.shape[1] // LANES), axis=1) * mask[...]
-    delta = dot(spread, up[...])
     for k in range(4):
         j = (sign * (x - k)) & 3
         part = total[pl.ds(pl.multiple_of(j * rows, rows), rows), :]
@@ -267,12 +296,11 @@
     levels = levels.reshape(rank, width)
 
     info = jnp.stack([z, x, sign, t, me]).astype(I32)
-    fill, pick, mask, dense = local(
+    fill, mine, dense = local(
         plan_kernel,
         (
             jax.ShapeDtypeStruct((32 * rows, 64), BF16),
-            jax.ShapeDtypeStruct((4 * rows, 8 * adapters), BF16),
-            jax.ShapeDtypeStruct((4 * rows, adapters * rank), BF16),
+            jax.ShapeDtypeStruct((4 * rows, LANES), I32),
             jax.ShapeDtypeStruct((rank, width), BF16),
         ),
         "svvv",
@@ -319,10 +347,10 @@
         cost(4),
         "own",
     )(hidden, own_1, own_2, own_3, down_matrix, dense, fill)
-    far_0 = after(stack(*(b[i] for i in FAR)), pick, mask, near_1)
+    far_0 = after(stack(*(b[i] for i in FAR)), mine, near_1)
     near_2 = turn(near_1, "x", 1)
     far_1, far_3 = turn(far_0, "x", 1), turn(far_0, "x", -1)
-    a[2], a[6] = turn(after(a[1], near_1), "z", 1), turn(after(a[7], near_3), "z", -1)
+    a[2], a[6] = turn(after(a[1], near_1), "z", 1), turn(after(a[7], near_1), "z", -1)
     head, tail = scratch(16, 12, 11)
     near_a, near_b = local(
         functools.partial(near_kernel, cut),
@@ -350,19 +378,32 @@
         "far",
     )(a[3], a[5], near_2, far_0, far_1, far_3, down_matrix, dense, fill, near_a, near_b, slots)
     four = jax.ShapeDtypeStruct((4 * n, out_width), BF16)
-    slots, keep, send = local(
+    slots = local(
+        functools.partial(slots_kernel, cut),
+        jax.ShapeDtypeStruct((64, LANES), F32),
+        "v" * 7,
+        flops=2 * n * width * rank,
+        name="slots",
+    )(a[4], far_2, dense, fill, far_a, far_b, slots)
+    keep, send = local(
         functools.partial(last_kernel, cut),
-        (jax.ShapeDtypeStruct((64, LANES), F32), four, four),
-        "svvvvvvvvvv",
-        [acc(4), acc(3), pltpu.VMEM((8 * n, out_width), BF16), pltpu.SemaphoreType.DMA((8,))],
+        (four, four),
+        "svvvvvvv",
+        [
+            pltpu.VMEM((n, out_width), F32),
+            pltpu.VMEM((3 * rows, out_width), F32),
+            pltpu.VMEM((8 * n, out_width), BF16),
+            pltpu.SemaphoreType.DMA((8,)),
+        ],
         cost(4),
         "last",
-        "vhh",
-    )(info, a[4], far_2, down_matrix, dense, fill, far_a, far_b, base_own, base_near, slots)
+        "hh",
+    )(info, after(a[4], slots), far_2, down_matrix, far_a, far_b, base_own, base_near)
 
     slots = lax.all_to_all(slots, ("y", "core"), 0, 0, tiled=True)
     slots = jnp.sum(slots.reshape(8, 8, LANES), axis=0)
     slots = jnp.broadcast_to(slots[None], (adapters, 8, LANES)).reshape(adapters * 8, LANES)
+    shared = slots
     slots = lax.all_to_all(slots, ("z", "x"), 0, 0, tiled=True).astype(BF16)
 
     given = lax.ppermute(send, "core", [(0, 1), (1, 0)])
@@ -372,14 +413,18 @@
     got = [pairs[0]]
     for by in range(1, 4):
         got.append(lax.ppermute(pairs[by], "y", [(i, (i + by) % 4) for i in range(4)]))
+    up = up_factors.reshape(adapters * rank, out_width)
+    up = local(load_kernel, jax.ShapeDtypeStruct(up.shape, BF16), "v", name="load")(after(up, shared))
+    delta = local(
+        functools.partial(delta_kernel, rank),
+        jax.ShapeDtypeStruct((n, out_width), F32),
+        "vvv",
+        flops=DELTA_COST,
+        name="delta",
+    )(slots, mine, up)
     return local(
-        sum_kernel,
-        block,
-        "s" + "v" * 8,
-        [pltpu.VMEM((n, out_width), F32)],
-        2 * n * adapters * rank * out_width,
-        "sum",
-    )(info, slots, pick, mask, up_factors.reshape(adapters * rank, out_width), *got)
+        sum_kernel, block, "s" + "v" * 5, [pltpu.VMEM((n, out_width), F32)], name="sum"
+    )(info, delta, *got)
 
 
 def solution(mesh):

time: 136 us -> 135 us (level)
  waiting for transfers between devices: 32.9 us -> 46.4 us
  starting transfers between devices: 48.1 us -> 39.6 us
  blocking collectives: 16.9 us -> 9.8 us
    ppermute x23, waiting for transfers between devices: 32.8 us -> 42.1 us  [turn(): return lax.ppermute(value, (axis, 'core'), pairs)]
    all_to_all x1, blocking collectives: 16.9 us -> 9.8 us  [shards(): slots = lax.all_to_all(slots, ('y', 'core'), 0, 0, tiled=True)]
    ppermute x23, starting transfers between devices: 37.1 us -> 31 us  [turn(): return lax.ppermute(value, (axis, 'core'), pairs)]
    ppermute x3, starting transfers between devices: 6.23 us -> 3.71 us  [shards(): lax.ppermute(pairs[by], 'y', [(i, (i + by) % 4) for i in range(4)])]
    all_to_all x1, waiting for transfers between devices: 0.01 us -> 2.43 us  [shards(): slots = lax.all_to_all(slots, ('z', 'x'), 0, 0, tiled=True).astype(BF16)]
    ppermute x3, waiting for transfers between devices: 0.01 us -> 1.87 us  [shards(): lax.ppermute(pairs[by], 'y', [(i, (i + by) % 4) for i in range(4)])]
    unnamed x36 -> x34, local copies, waits for them, and re-layouts: 11.4 us -> 12.2 us
    pallas_call x2 -> x5, Pallas kernels: 6.09 us -> 5.88 us  [the longest x1 3.1 us: shards(): local(functools.partial(last_kernel, cut), (four, four), 'svvvvvvv', [plt...]
  transfers between devices with their start and end apart: 28 -> 28, of which waited for: 12 -> 16; matrix products, arithmetic and copies ran while one was open for 5% -> 5% of each run, Pallas kernels for 11% -> 12%
where the time goes in v3:
time: 135 us
  waiting for transfers between devices  46.4 us (34%)
  starting transfers between devices  39.6 us (29%)
  Pallas kernels  21.5 us (16%)
  local copies, waits for them, and re-layouts  14.8 us (11%)
  blocking collectives  9.8 us (7%)
  other arithmetic  2.71 us (2%)
    ppermute x23, waiting for transfers between devices, turn(): return lax.ppermute(value, (axis, 'core'), pairs)  42.1 us
    ppermute x23, starting transfers between devices, turn(): return lax.ppermute(value, (axis, 'core'), pairs)  31 us
    unnamed x34, local copies, waits for them, and re-layouts  12.2 us
    all_to_all x1, blocking collectives, shards(): slots = lax.all_to_all(slots, ('y', 'core'), 0, 0, tiled=True)  9.8 us
    pallas_call x1, Pallas kernels, shards(): local(functools.partial(near_kernel, cut), (sums(16), sums(12)), 'hhhhhhh...  6.2 us
    pallas_call x1, Pallas kernels, shards(): local(functools.partial(far_kernel, cut), (jax.ShapeDtypeStruct((4 * n, o...  4.93 us
    all_to_all x1, starting transfers between devices, shards(): slots = lax.all_to_all(slots, ('z', 'x'), 0, 0, tiled=True).astype(BF16)  4.73 us
    ppermute x3, starting transfers between devices, shards(): lax.ppermute(pairs[by], 'y', [(i, (i + by) % 4) for i in range(4)])  3.71 us
  transfers between devices with their start and end apart: 28, of which 16 were waited for; matrix products, arithmetic and copies ran while one was open for 5% of the time, Pallas kernels for 12%

profile of v3, /device:TPU:2, one launch (start us, length us, event | category | flops | bytes accessed | tf_op | source)
XLA Modules:
  0.0 135.0 jit_solution(18138591783887445514)
XLA Ops:
  0.0 1.0 slice.19
  1.0 2.0 %collective-permute-start.3 = (bf16[32,4096]{1,0:T(8,128)(2,1)S(1)}, bf16[32,4096]{1,0:T(8,128)(2,1)S(1)}, u32[]{:S(2)}, u32[]{:S(2)}) collective-permute-start(bf16[32,4096]{1,0:T(8,128)(2,1)S(1)} %slice.19), channel_id=1, source_target_pairs={{0,32},{1,225},{32,64},{33,1},{64,96},{65,33},{96,128},{97,65},{12... | collective-permute-start | bytes 786440 | tf_op jit(solution)/shard_map/ppermute | solution.py:27
  3.0 1.5 %collective-permute-start = (bf16[32,6656]{1,0:T(8,128)(2,1)}, bf16[32,6656]{1,0:T(8,128)(2,1)S(1)}, u32[]{:S(2)}, u32[]{:S(2)}) collective-permute-start(bf16[32,6656]{1,0:T(8,128)(2,1)} %refs_0_.1), channel_id=1, source_target_pairs={{0,8},{1,25},{8,16},{9,1},{16,24},{17,9},{24,0},{25,17},{2,10},{3,... | collective-permute-start | bytes 1277960 | tf_op jit(solution)/shard_map/ppermute | solution.py:27
  4.5 0.5 collective-permute-start.2
  5.1 4.0 %collective-permute-start.6 = (bf16[32,4096]{1,0:T(8,128)(2,1)S(1)}, bf16[32,4096]{1,0:T(8,128)(2,1)S(1)}, u32[]{:S(2)}, u32[]{:S(2)}) collective-permute-start(bf16[32,4096]{1,0:T(8,128)(2,1)S(1)} %slice.19), channel_id=1, source_target_pairs={{0,224},{1,33},{32,0},{33,65},{64,32},{65,97},{96,64},{97,129},{12... | collective-permute-start | bytes 786440 | tf_op jit(solution)/shard_map/ppermute | solution.py:27
  9.1 2.2 %collective-permute-done.3 = bf16[32,4096]{1,0:T(8,128)(2,1)S(1)} collective-permute-done((bf16[32,4096]{1,0:T(8,128)(2,1)S(1)}, bf16[32,4096]{1,0:T(8,128)(2,1)S(1)}, u32[]{:S(2)}, u32[]{:S(2)}) %collective-permute-start.3) | collective-permute-done | bytes 262176 | tf_op jit(solution)/shard_map/ppermute | solution.py:27
  11.3 0.7 constant_dynamic-update-slice_fusion.3
  12.1 0.9 collective-permute-done.6
  13.0 3.7 %collective-permute-start.7 = (bf16[32,4096]{1,0:T(8,128)(2,1)S(1)}, bf16[32,4096]{1,0:T(8,128)(2,1)S(1)}, u32[]{:S(2)}, u32[]{:S(2)}) collective-permute-start(bf16[32,4096]{1,0:T(8,128)(2,1)S(1)} %collective-permute-done.6), channel_id=1, source_target_pairs={{0,224},{1,33},{32,0},{33,65},{64,32},{65,97},{96,64},{97,129},{12... | collective-permute-start | bytes 786440 | tf_op jit(solution)/shard_map/ppermute | solution.py:27
  16.7 0.7 constant_dynamic-update-slice_fusion.2
  17.4 1.5 %collective-permute-start.1 = (bf16[32,6656]{1,0:T(8,128)(2,1)S(1)}, bf16[32,6656]{1,0:T(8,128)(2,1)S(1)}, u32[]{:S(2)}, u32[]{:S(2)}) collective-permute-start(bf16[32,6656]{1,0:T(8,128)(2,1)S(1)} %collective-permute-done.refs_1_), channel_id=1, source_target_pairs={{0,8},{1,25},{8,16},{9,1},{16,24},{17,9},{24,0},{25,17},{2,10},{3,... | collective-permute-start | bytes 1277960 | tf_op jit(solution)/shard_map/ppermute | solution.py:27
  18.9 1.7 %collective-permute-done.4 = bf16[32,4096]{1,0:T(8,128)(2,1)S(1)} collective-permute-done((bf16[32,4096]{1,0:T(8,128)(2,1)S(1)}, bf16[32,4096]{1,0:T(8,128)(2,1)S(1)}, u32[]{:S(2)}, u32[]{:S(2)}) %collective-permute-start.4) | collective-permute-done | bytes 262176 | tf_op jit(solution)/shard_map/ppermute | solution.py:27
  20.6 0.7 constant_dynamic-update-slice_fusion.1
  21.3 0.7 constant_dynamic-update-slice_fusion.refs_4_
  22.0 1.5 %collective-permute-start.10 = (bf16[128,4096]{1,0:T(8,128)(2,1)}, bf16[128,4096]{1,0:T(8,128)(2,1)}, u32[]{:S(2)}, u32[]{:S(2)}) collective-permute-start(bf16[128,4096]{1,0:T(8,128)(2,1)} %constant_dynamic-update-slice_fusion.refs_4_), channel_id=1, source_target_pairs={{0,8},{1,25},{8,16},{9,1},{16,24},{17,9},{24,0},{25,17},{2,10},{3,... | collective-permute-start | bytes 3145736 | tf_op jit(solution)/shard_map/ppermute | solution.py:27
  23.6 0.8 copy-done.4
  24.4 1.7 %collective-permute-start.5 = (bf16[32,4096]{1,0:T(8,128)(2,1)S(1)}, bf16[32,4096]{1,0:T(8,128)(2,1)}, u32[]{:S(2)}, u32[]{:S(2)}) collective-permute-start(bf16[32,4096]{1,0:T(8,128)(2,1)S(1)} %collective-permute-done.4), channel_id=1, source_target_pairs={{0,32},{1,225},{32,64},{33,1},{64,96},{65,33},{96,128},{97,65},{12... | collective-permute-start | bytes 786440 | tf_op jit(solution)/shard_map/ppermute | solution.py:27
  26.1 1.8 %collective-permute-start.8 = (bf16[32,4096]{1,0:T(8,128)(2,1)S(1)}, bf16[32,4096]{1,0:T(8,128)(2,1)S(1)}, u32[]{:S(2)}, u32[]{:S(2)}) collective-permute-start(bf16[32,4096]{1,0:T(8,128)(2,1)S(1)} %collective-permute-done.7), channel_id=1, source_target_pairs={{0,224},{1,33},{32,0},{33,65},{64,32},{65,97},{96,64},{97,129},{12... | collective-permute-start | bytes 786440 | tf_op jit(solution)/shard_map/ppermute | solution.py:27
  27.9 0.8 copy-done.6
  28.7 0.9 pad_maximum_fusion.1
  29.6 5.5 %collective-permute-done.5 = bf16[32,4096]{1,0:T(8,128)(2,1)} collective-permute-done((bf16[32,4096]{1,0:T(8,128)(2,1)S(1)}, bf16[32,4096]{1,0:T(8,128)(2,1)}, u32[]{:S(2)}, u32[]{:S(2)}) %collective-permute-start.5) | collective-permute-done | bytes 262176 | tf_op jit(solution)/shard_map/ppermute | solution.py:27
  35.0 0.7 copy-done.11
  35.8 2.3 %collective-permute-start.9 = (bf16[128,2560]{1,0:T(8,128)(2,1)}, bf16[128,2560]{1,0:T(8,128)(2,1)}, u32[]{:S(2)}, u32[]{:S(2)}) collective-permute-start(bf16[128,2560]{1,0:T(8,128)(2,1)} %pad_maximum_fusion.1), channel_id=1, source_target_pairs={{0,32},{1,225},{32,64},{33,1},{64,96},{65,33},{96,128},{97,65},{12... | collective-permute-start | bytes 1966088 | tf_op jit(solution)/shard_map/ppermute | solution.py:27
  38.0 4.7 %collective-permute-start.17 = (bf16[32,4096]{1,0:T(8,128)(2,1)}, bf16[32,4096]{1,0:T(8,128)(2,1)}, u32[]{:S(2)}, u32[]{:S(2)}) collective-permute-start(bf16[32,4096]{1,0:T(8,128)(2,1)} %collective-permute-done.5), channel_id=1, source_target_pairs={{0,32},{1,225},{32,64},{33,1},{64,96},{65,33},{96,128},{97,65},{12... | collective-permute-start | bytes 786440 | tf_op jit(solution)/shard_map/ppermute | solution.py:27
  42.7 0.6 broadcast.4
  43.2 0.6 reduce.4
  44.1 1.2 copy-done.3
  45.2 1.5 %plan.1 = (bf16[1024,64]{1,0:T(8,128)(2,1)S(1)}, s32[128,128]{1,0:T(8,128)S(1)}, bf16[64,6656]{1,0:T(8,128)(2,1)S(1)}) custom-call(s32[5]{0:T(128)S(1)} %stack.23.info, s32[32,32]{1,0:T(8,128)S(1)} %reshape.19.ids_ref, bf16[64,6656]{1,0:T(8,128)(2,1)S(1)} %bitcast.15, f32[1,6656]{1,0:T(1,128)S(1)} %copy-done.8), custom_call_target="tpu_custom_call" | custom-call | flops 1048576 | bytes 4194304 | tf_op jit(solution)/shard_map/plan/pallas_call | solution.py:299
  46.7 0.6 copy-done.9
  47.3 7.4 %collective-permute-done.9.refs_0_ = bf16[128,2560]{1,0:T(8,128)(2,1)} collective-permute-done((bf16[128,2560]{1,0:T(8,128)(2,1)}, bf16[128,2560]{1,0:T(8,128)(2,1)}, u32[]{:S(2)}, u32[]{:S(2)}) %collective-permute-start.9) | collective-permute-done | bytes 655392 | tf_op jit(solution)/shard_map/ppermute | solution.py:27
  54.8 2.8 %collective-permute-done.17 = bf16[32,4096]{1,0:T(8,128)(2,1)} collective-permute-done((bf16[32,4096]{1,0:T(8,128)(2,1)}, bf16[32,4096]{1,0:T(8,128)(2,1)}, u32[]{:S(2)}, u32[]{:S(2)}) %collective-permute-start.17) | collective-permute-done | bytes 262176 | tf_op jit(solution)/shard_map/ppermute | solution.py:27
  57.6 1.2 pad_maximum_fusion.refs_3_
  58.7 0.2 collective-permute-start.18
  59.0 1.7 %collective-permute-done.13.refs_1_ = bf16[128,2560]{1,0:T(8,128)(2,1)} collective-permute-done((bf16[128,2560]{1,0:T(8,128)(2,1)}, bf16[128,2560]{1,0:T(8,128)(2,1)}, u32[]{:S(2)}, u32[]{:S(2)}) %collective-permute-start.13) | collective-permute-done | bytes 655392 | tf_op jit(solution)/shard_map/ppermute | solution.py:27
  60.7 1.2 collective-permute-start.14
  61.9 2.9 %copy-done = bf16[6656,512]{1,0:T(8,128)(2,1)S(1)} copy-done((bf16[6656,512]{1,0:T(8,128)(2,1)S(1)}, bf16[6656,512]{1,0:T(8,128)(2,1)}, u32[]{:S(2)}) %copy-start) | copy-done | bytes 6815768
  64.8 2.2 %own.1 = (bf16[128,512]{1,0:T(8,128)(2,1)S(1)}, f32[64,64]{1,0:T(8,128)S(1)}) custom-call(bf16[32,6656]{1,0:T(8,128)(2,1)S(1)} %copy-done.2, bf16[32,6656]{1,0:T(8,128)(2,1)S(1)} %collective-permute-done.refs_1_, bf16[32,6656]{1,0:T(8,128)(2,1)S(1)} %copy-done.7, bf16[32,6656]{1,0:T(8,128)(2,1)S(1)} %copy-done.5, bf16[6656,512]{1,0:T(8,128)(2,1)S(1)} %copy-done, ...), custom_call_target="tpu_custom_call" | custom-call | flops 981467136 | bytes 4194304 | tf_op jit(solution)/shard_map/own/pallas_call | solution.py:342
  67.0 6.3 %collective-permute-done.11.refs_2_ = bf16[128,2560]{1,0:T(8,128)(2,1)S(1)} collective-permute-done((bf16[128,2560]{1,0:T(8,128)(2,1)}, bf16[128,2560]{1,0:T(8,128)(2,1)S(1)}, u32[]{:S(2)}, u32[]{:S(2)}) %collective-permute-start.11) | collective-permute-done | bytes 655392 | tf_op jit(solution)/shard_map/ppermute | solution.py:27
  73.3 2.0 %collective-permute-start.22 = (bf16[96,4096]{1,0:T(8,128)(2,1)S(1)}, bf16[96,4096]{1,0:T(8,128)(2,1)S(1)}, u32[]{:S(2)}, u32[]{:S(2)}) collective-permute-start(bf16[96,4096]{1,0:T(8,128)(2,1)S(1)} %pad_maximum_fusion.refs_3_), channel_id=1, source_target_pairs={{0,24},{1,9},{8,0},{9,17},{16,8},{17,25},{24,16},{25,1},{2,26},{3,... | collective-permute-start | bytes 2359304 | tf_op jit(solution)/shard_map/ppermute | solution.py:27
  75.3 2.3 %collective-permute-done.14.refs_3_ = bf16[128,2560]{1,0:T(8,128)(2,1)S(1)} collective-permute-done((bf16[128,2560]{1,0:T(8,128)(2,1)}, bf16[128,2560]{1,0:T(8,128)(2,1)S(1)}, u32[]{:S(2)}, u32[]{:S(2)}) %collective-permute-start.14) | collective-permute-done | bytes 655392 | tf_op jit(solution)/shard_map/ppermute | solution.py:27
  77.7 2.4 %collective-permute-start.20 = (bf16[128,2560]{1,0:T(8,128)(2,1)S(1)}, bf16[128,2560]{1,0:T(8,128)(2,1)S(1)}, u32[]{:S(2)}, u32[]{:S(2)}) collective-permute-start(bf16[128,2560]{1,0:T(8,128)(2,1)S(1)} %collective-permute-done.14.refs_3_), channel_id=1, source_target_pairs={{0,224},{1,33},{32,0},{33,65},{64,32},{65,97},{96,64},{97,129},{12... | collective-permute-start | bytes 1966088 | tf_op jit(solution)/shard_map/ppermute | solution.py:27
  80.1 6.2 %near.1 = (f32[512,576]{1,0:T(8,128)S(1)}, f32[384,576]{1,0:T(8,128)S(1)}) custom-call(bf16[128,2560]{1,0:T(8,128)(2,1)} %collective-permute-done.9.refs_0_, bf16[128,2560]{1,0:T(8,128)(2,1)} %collective-permute-done.13.refs_1_, bf16[128,2560]{1,0:T(8,128)(2,1)S(1)} %collective-permute-done.11.refs_2_, ...), custom_call_target="tpu_custom_call" | custom-call | flops 3435134976 | bytes 4194304 | tf_op jit(solution)/shard_map/near/pallas_call | solution.py:355
  86.3 4.5 %collective-permute-done.12.refs_0_ = bf16[128,2560]{1,0:T(8,128)(2,1)S(1)} collective-permute-done((bf16[128,2560]{1,0:T(8,128)(2,1)S(1)}, bf16[128,2560]{1,0:T(8,128)(2,1)S(1)}, u32[]{:S(2)}, u32[]{:S(2)}) %collective-permute-start.12) | collective-permute-done | bytes 655392 | tf_op jit(solution)/shard_map/ppermute | solution.py:27
  90.8 3.0 %collective-permute-done.22.refs_5_ = bf16[96,4096]{1,0:T(8,128)(2,1)S(1)} collective-permute-done((bf16[96,4096]{1,0:T(8,128)(2,1)S(1)}, bf16[96,4096]{1,0:T(8,128)(2,1)S(1)}, u32[]{:S(2)}, u32[]{:S(2)}) %collective-permute-start.22) | collective-permute-done | bytes 786464 | tf_op jit(solution)/shard_map/ppermute | solution.py:27
  93.9 4.9 %far.1 = (bf16[512,512]{1,0:T(8,128)(2,1)S(1)}, f32[256,576]{1,0:T(8,128)S(1)}, f32[288,576]{1,0:T(8,128)S(1)}, f32[64,64]{1,0:T(8,128)S(1)}) custom-call(bf16[128,2560]{1,0:T(8,128)(2,1)S(1)} %collective-permute-done.12.refs_0_, bf16[128,2560]{1,0:T(8,128)(2,1)S(1)} %collective-permute-done.20.refs_1_, ...), custom_call_target="tpu_custom_call" | custom-call | flops 2699034624 | bytes 4194304 | tf_op jit(solution)/shard_map/far/pallas_call | solution.py:367
  98.8 0.1 collective-permute-done.19.far
  98.9 3.7 %collective-permute-done.16.a = bf16[128,2560]{1,0:T(8,128)(2,1)S(1)} collective-permute-done((bf16[128,2560]{1,0:T(8,128)(2,1)S(1)}, bf16[128,2560]{1,0:T(8,128)(2,1)S(1)}, u32[]{:S(2)}, u32[]{:S(2)}) %collective-permute-start.16) | collective-permute-done | bytes 655392 | tf_op jit(solution)/shard_map/ppermute | solution.py:27
  102.6 0.8 slots.1
  103.4 3.1 %last.1 = (bf16[512,512]{1,0:T(8,128)(2,1)S(1)}, bf16[512,512]{1,0:T(8,128)(2,1)}) custom-call(s32[5]{0:T(128)S(1)} %stack.23.info, bf16[128,2560]{1,0:T(8,128)(2,1)S(1)} %collective-permute-done.16.a, bf16[96,4096]{1,0:T(8,128)(2,1)S(1)} %collective-permute-done.19.far, bf16[6656,512]{1,0:T(8,128)(2,1)S(1)} %bitcast.13, ...), custom_call_target="tpu_custom_call" | custom-call | flops 981467136 | bytes 4194304 | tf_op jit(solution)/shard_map/last/pallas_call | solution.py:388
  106.6 9.8 %all_to_all.15 = f32[8,8,128]{2,1,0:T(8,128)S(1)} all-to-all(f32[8,8,128]{2,1,0:T(8,128)S(1)} %bitcast.16), channel_id=1, replica_groups=mesh['z'=8,'x'=4,'y'=4,'core'=2] {'y','core'}, dimensions={0} | all-to-all | bytes 65536 | tf_op jit(solution)/shard_map/all_to_all | solution.py:403
  116.4 0.6 broadcast_in_dim.2
  117.0 4.7 %all-to-all-start.1 = ((bf16[32,8,128]{2,1,0:T(8,128)(2,1)}), bf16[32,8,128]{2,1,0:T(8,128)(2,1)S(1)}, u32[]{:S(2)}, u32[]{:S(2)}) async-start(bf16[32,8,128]{2,1,0:T(8,128)(2,1)} %broadcast_in_dim.2), calls=%async_computation.1 | async-start | bytes 131072 | tf_op jit(solution)/shard_map/all_to_all | solution.py:407
  121.8 1.6 %copy-done.1 = bf16[32,64,512]{2,1,0:T(8,128)(2,1)S(1)} copy-done((bf16[32,64,512]{2,1,0:T(8,128)(2,1)S(1)}, bf16[32,64,512]{2,1,0:T(8,128)(2,1)}, u32[]{:S(2)}) %copy-start.1) | copy-done | bytes 2097176
  123.3 0.1 load.1.up
  123.5 0.8 pair.1
  124.3 0.6 collective-permute-start.24
  124.8 2.1 %collective-permute-start.25 = (bf16[128,512]{1,0:T(8,128)(2,1)}, bf16[128,512]{1,0:T(8,128)(2,1)S(1)}, u32[]{:S(2)}, u32[]{:S(2)}) collective-permute-start(bf16[128,512]{1,0:T(8,128)(2,1)} %get-tuple-element.51), channel_id=1, source_target_pairs={{0,4},{2,6},{4,0},{6,2},{1,5},{3,7},{5,1},{7,3},{8,12},{10,14},{12... | collective-permute-start | bytes 393224 | tf_op jit(solution)/shard_map/ppermute | solution.py:415
  126.9 1.1 collective-permute-start.26
  128.0 2.4 %all-to-all-done.1 = bf16[32,8,128]{2,1,0:T(8,128)(2,1)S(1)} async-done(((bf16[32,8,128]{2,1,0:T(8,128)(2,1)}), bf16[32,8,128]{2,1,0:T(8,128)(2,1)S(1)}, u32[]{:S(2)}, u32[]{:S(2)}) %all-to-all-start.1) | async-done | bytes 65568 | tf_op jit(solution)/shard_map/all_to_all | solution.py:407
  130.4 0.8 copy-done.10
  131.3 0.6 delta.1
  131.9 1.2 collective-permute-done.24.refs_1_
  133.1 0.6 collective-permute-done.26.refs_3_
  133.8 1.3 sum.1
  (51 shorter events, 0.4 us)
Async XLA Ops:
  0.0 23.5 %copy-start.2 = (bf16[32,6656]{1,0:T(8,128)(2,1)S(1)}, bf16[32,6656]{1,0:T(8,128)(2,1)}, u32[]{:S(2)}) copy-start(bf16[32,6656]{1,0:T(8,128)(2,1)} %refs_0_.1) | copy-start | bytes 1277956
  1.0 10.3 %collective-permute-start.3 = (bf16[32,4096]{1,0:T(8,128)(2,1)S(1)}, bf16[32,4096]{1,0:T(8,128)(2,1)S(1)}, u32[]{:S(2)}, u32[]{:S(2)}) collective-permute-start(bf16[32,4096]{1,0:T(8,128)(2,1)S(1)} %slice.19), channel_id=1, source_target_pairs={{0,32},{1,225},{32,64},{33,1},{64,96},{65,33},{96,128},{97,65},{12... | collective-permute-start | bytes 786440 | tf_op jit(solution)/shard_map/ppermute | solution.py:27
  3.0 14.4 %collective-permute-start = (bf16[32,6656]{1,0:T(8,128)(2,1)}, bf16[32,6656]{1,0:T(8,128)(2,1)S(1)}, u32[]{:S(2)}, u32[]{:S(2)}) collective-permute-start(bf16[32,6656]{1,0:T(8,128)(2,1)} %refs_0_.1), channel_id=1, source_target_pairs={{0,8},{1,25},{8,16},{9,1},{16,24},{17,9},{24,0},{25,17},{2,10},{3,... | collective-permute-start | bytes 1277960 | tf_op jit(solution)/shard_map/ppermute | solution.py:27
  4.5 19.1 %collective-permute-start.2 = (bf16[32,6656]{1,0:T(8,128)(2,1)}, bf16[32,6656]{1,0:T(8,128)(2,1)S(1)}, u32[]{:S(2)}, u32[]{:S(2)}) collective-permute-start(bf16[32,6656]{1,0:T(8,128)(2,1)} %refs_0_.1), channel_id=1, source_target_pairs={{0,24},{1,9},{8,0},{9,17},{16,8},{17,25},{24,16},{25,1},{2,26},{3,... | collective-permute-start | bytes 1277960 | tf_op jit(solution)/shard_map/ppermute | solution.py:27
  5.1 7.9 %collective-permute-start.6 = (bf16[32,4096]{1,0:T(8,128)(2,1)S(1)}, bf16[32,4096]{1,0:T(8,128)(2,1)S(1)}, u32[]{:S(2)}, u32[]{:S(2)}) collective-permute-start(bf16[32,4096]{1,0:T(8,128)(2,1)S(1)} %slice.19), channel_id=1, source_target_pairs={{0,224},{1,33},{32,0},{33,65},{64,32},{65,97},{96,64},{97,129},{12... | collective-permute-start | bytes 786440 | tf_op jit(solution)/shard_map/ppermute | solution.py:27
  11.3 9.2 %collective-permute-start.4 = (bf16[32,4096]{1,0:T(8,128)(2,1)S(1)}, bf16[32,4096]{1,0:T(8,128)(2,1)S(1)}, u32[]{:S(2)}, u32[]{:S(2)}) collective-permute-start(bf16[32,4096]{1,0:T(8,128)(2,1)S(1)} %collective-permute-done.3), channel_id=1, source_target_pairs={{0,32},{1,225},{32,64},{33,1},{64,96},{65,33},{96,128},{97,65},{12... | collective-permute-start | bytes 786440 | tf_op jit(solution)/shard_map/ppermute | solution.py:27
  13.0 8.3 %collective-permute-start.7 = (bf16[32,4096]{1,0:T(8,128)(2,1)S(1)}, bf16[32,4096]{1,0:T(8,128)(2,1)S(1)}, u32[]{:S(2)}, u32[]{:S(2)}) collective-permute-start(bf16[32,4096]{1,0:T(8,128)(2,1)S(1)} %collective-permute-done.6), channel_id=1, source_target_pairs={{0,224},{1,33},{32,0},{33,65},{64,32},{65,97},{96,64},{97,129},{12... | collective-permute-start | bytes 786440 | tf_op jit(solution)/shard_map/ppermute | solution.py:27
  17.4 10.5 %collective-permute-start.1 = (bf16[32,6656]{1,0:T(8,128)(2,1)S(1)}, bf16[32,6656]{1,0:T(8,128)(2,1)S(1)}, u32[]{:S(2)}, u32[]{:S(2)}) collective-permute-start(bf16[32,6656]{1,0:T(8,128)(2,1)S(1)} %collective-permute-done.refs_1_), channel_id=1, source_target_pairs={{0,8},{1,25},{8,16},{9,1},{16,24},{17,9},{24,0},{25,17},{2,10},{3,... | collective-permute-start | bytes 1277960 | tf_op jit(solution)/shard_map/ppermute | solution.py:27
  21.3 21.9 %copy-start.12 = (s32[1024,1]{0,1:T(1,128)S(1)}, s32[1024,1]{0,1:T(1,128)}, u32[]{:S(2)}) copy-start(s32[1024,1]{0,1:T(1,128)} %param.11) | copy-start | bytes 12292
  21.3 22.8 %copy-start.8 = (f32[1,6656]{1,0:T(1,128)S(1)}, f32[1,6656]{1,0:T(1,128)}, u32[]{:S(2)}) copy-start(f32[1,6656]{1,0:T(1,128)} %scale.1) | copy-start | bytes 79876
  22.0 32.7 %collective-permute-start.10 = (bf16[128,4096]{1,0:T(8,128)(2,1)}, bf16[128,4096]{1,0:T(8,128)(2,1)}, u32[]{:S(2)}, u32[]{:S(2)}) collective-permute-start(bf16[128,4096]{1,0:T(8,128)(2,1)} %constant_dynamic-update-slice_fusion.refs_4_), channel_id=1, source_target_pairs={{0,8},{1,25},{8,16},{9,1},{16,24},{17,9},{24,0},{25,17},{2,10},{3,... | collective-permute-start | bytes 3145736 | tf_op jit(solution)/shard_map/ppermute | solution.py:27
  23.5 56.6 %slice-start = ((s8[6815744]{0:T(1024)(128)(4,1)}), s8[2621440]{0:T(1024)(128)(4,1)S(1)}, s32[]{:S(2)}) async-start(s8[6815744]{0:T(1024)(128)(4,1)} %bitcast.12), calls=%async_computation.2 | async-start | bytes 5242880
  23.6 0.8 copy-start.4
  24.4 10.6 %collective-permute-start.5 = (bf16[32,4096]{1,0:T(8,128)(2,1)S(1)}, bf16[32,4096]{1,0:T(8,128)(2,1)}, u32[]{:S(2)}, u32[]{:S(2)}) collective-permute-start(bf16[32,4096]{1,0:T(8,128)(2,1)S(1)} %collective-permute-done.4), channel_id=1, source_target_pairs={{0,32},{1,225},{32,64},{33,1},{64,96},{65,33},{96,128},{97,65},{12... | collective-permute-start | bytes 786440 | tf_op jit(solution)/shard_map/ppermute | solution.py:27
  26.1 9.0 %collective-permute-start.8 = (bf16[32,4096]{1,0:T(8,128)(2,1)S(1)}, bf16[32,4096]{1,0:T(8,128)(2,1)S(1)}, u32[]{:S(2)}, u32[]{:S(2)}) collective-permute-start(bf16[32,4096]{1,0:T(8,128)(2,1)S(1)} %collective-permute-done.7), channel_id=1, source_target_pairs={{0,224},{1,33},{32,0},{33,65},{64,32},{65,97},{96,64},{97,129},{12... | collective-permute-start | bytes 786440 | tf_op jit(solution)/shard_map/ppermute | solution.py:27
  27.9 0.8 copy-start.6
  35.0 0.7 copy-start.11
  35.8 19.0 %collective-permute-start.9 = (bf16[128,2560]{1,0:T(8,128)(2,1)}, bf16[128,2560]{1,0:T(8,128)(2,1)}, u32[]{:S(2)}, u32[]{:S(2)}) collective-permute-start(bf16[128,2560]{1,0:T(8,128)(2,1)} %pad_maximum_fusion.1), channel_id=1, source_target_pairs={{0,32},{1,225},{32,64},{33,1},{64,96},{65,33},{96,128},{97,65},{12... | collective-permute-start | bytes 1966088 | tf_op jit(solution)/shard_map/ppermute | solution.py:27
  38.0 19.6 %collective-permute-start.17 = (bf16[32,4096]{1,0:T(8,128)(2,1)}, bf16[32,4096]{1,0:T(8,128)(2,1)}, u32[]{:S(2)}, u32[]{:S(2)}) collective-permute-start(bf16[32,4096]{1,0:T(8,128)(2,1)} %collective-permute-done.5), channel_id=1, source_target_pairs={{0,32},{1,225},{32,64},{33,1},{64,96},{65,33},{96,128},{97,65},{12... | collective-permute-start | bytes 786440 | tf_op jit(solution)/shard_map/ppermute | solution.py:27
  42.7 18.0 %collective-permute-start.13 = (bf16[128,2560]{1,0:T(8,128)(2,1)}, bf16[128,2560]{1,0:T(8,128)(2,1)}, u32[]{:S(2)}, u32[]{:S(2)}) collective-permute-start(bf16[128,2560]{1,0:T(8,128)(2,1)} %pad_maximum_fusion.1), channel_id=1, source_target_pairs={{0,224},{1,33},{32,0},{33,65},{64,32},{65,97},{96,64},{97,129},{12... | collective-permute-start | bytes 1966088 | tf_op jit(solution)/shard_map/ppermute | solution.py:27
  44.1 1.2 copy-start.3
  45.2 16.6 %copy-start.5 = (bf16[32,6656]{1,0:T(8,128)(2,1)S(1)}, bf16[32,6656]{1,0:T(8,128)(2,1)}, u32[]{:S(2)}) copy-start(bf16[32,6656]{1,0:T(8,128)(2,1)} %copy-done.4) | copy-start | bytes 1277956
  45.2 16.6 %copy-start.7 = (bf16[32,6656]{1,0:T(8,128)(2,1)S(1)}, bf16[32,6656]{1,0:T(8,128)(2,1)}, u32[]{:S(2)}) copy-start(bf16[32,6656]{1,0:T(8,128)(2,1)} %copy-done.6) | copy-start | bytes 1277956
  46.7 0.6 copy-start.9
  47.3 26.0 %collective-permute-start.15 = (bf16[128,4096]{1,0:T(8,128)(2,1)}, bf16[128,4096]{1,0:T(8,128)(2,1)S(1)}, u32[]{:S(2)}, u32[]{:S(2)}) collective-permute-start(bf16[128,4096]{1,0:T(8,128)(2,1)} %constant_dynamic-update-slice_fusion.refs_4_), channel_id=1, source_target_pairs={{0,24},{1,9},{8,0},{9,17},{16,8},{17,25},{24,16},{25,1},{2,26},{3,... | collective-permute-start | bytes 3145736 | tf_op jit(solution)/shard_map/ppermute | solution.py:27
  54.8 18.5 %collective-permute-start.11 = (bf16[128,2560]{1,0:T(8,128)(2,1)}, bf16[128,2560]{1,0:T(8,128)(2,1)S(1)}, u32[]{:S(2)}, u32[]{:S(2)}) collective-permute-start(bf16[128,2560]{1,0:T(8,128)(2,1)} %collective-permute-done.9.refs_0_), channel_id=1, source_target_pairs={{0,32},{1,225},{32,64},{33,1},{64,96},{65,33},{96,128},{97,65},{12... | collective-permute-start | bytes 1966088 | tf_op jit(solution)/shard_map/ppermute | solution.py:27
  58.7 21.4 %collective-permute-start.18 = (bf16[96,4096]{1,0:T(8,128)(2,1)S(1)}, bf16[96,4096]{1,0:T(8,128)(2,1)S(1)}, u32[]{:S(2)}, u32[]{:S(2)}) collective-permute-start(bf16[96,4096]{1,0:T(8,128)(2,1)S(1)} %pad_maximum_fusion.refs_3_), channel_id=1, source_target_pairs={{0,8},{1,25},{8,16},{9,1},{16,24},{17,9},{24,0},{25,17},{2,10},{3,... | collective-permute-start | bytes 2359304 | tf_op jit(solution)/shard_map/ppermute | solution.py:27
  60.7 17.0 %collective-permute-start.14 = (bf16[128,2560]{1,0:T(8,128)(2,1)}, bf16[128,2560]{1,0:T(8,128)(2,1)S(1)}, u32[]{:S(2)}, u32[]{:S(2)}) collective-permute-start(bf16[128,2560]{1,0:T(8,128)(2,1)} %collective-permute-done.13.refs_1_), channel_id=1, source_target_pairs={{0,224},{1,33},{32,0},{33,65},{64,32},{65,97},{96,64},{97,129},{12... | collective-permute-start | bytes 1966088 | tf_op jit(solution)/shard_map/ppermute | solution.py:27
  61.9 2.9 %copy-start = (bf16[6656,512]{1,0:T(8,128)(2,1)S(1)}, bf16[6656,512]{1,0:T(8,128)(2,1)}, u32[]{:S(2)}) copy-start(bf16[6656,512]{1,0:T(8,128)(2,1)} %w.1) | copy-start | bytes 20447236
  64.8 15.3 %slice-start.1 = ((s8[6815744]{0:T(1024)(128)(4,1)}), s8[4194304]{0:T(1024)(128)(4,1)S(1)}, s32[]{:S(2)}) async-start(s8[6815744]{0:T(1024)(128)(4,1)} %bitcast.12), calls=%async_computation.3 | async-start | bytes 8388608
  73.3 17.5 %collective-permute-start.12 = (bf16[128,2560]{1,0:T(8,128)(2,1)S(1)}, bf16[128,2560]{1,0:T(8,128)(2,1)S(1)}, u32[]{:S(2)}, u32[]{:S(2)}) collective-permute-start(bf16[128,2560]{1,0:T(8,128)(2,1)S(1)} %collective-permute-done.11.refs_2_), channel_id=1, source_target_pairs={{0,32},{1,225},{32,64},{33,1},{64,96},{65,33},{96,128},{97,65},{12... | collective-permute-start | bytes 1966088 | tf_op jit(solution)/shard_map/ppermute | solution.py:27
  73.3 20.6 %collective-permute-start.21 = (bf16[128,4096]{1,0:T(8,128)(2,1)}, bf16[128,4096]{1,0:T(8,128)(2,1)S(1)}, u32[]{:S(2)}, u32[]{:S(2)}) collective-permute-start(bf16[128,4096]{1,0:T(8,128)(2,1)} %collective-permute-done.10.refs_5_), channel_id=1, source_target_pairs={{0,8},{1,25},{8,16},{9,1},{16,24},{17,9},{24,0},{25,17},{2,10},{3,... | collective-permute-start | bytes 3145736 | tf_op jit(solution)/shard_map/ppermute | solution.py:27
  73.3 20.6 %collective-permute-start.22 = (bf16[96,4096]{1,0:T(8,128)(2,1)S(1)}, bf16[96,4096]{1,0:T(8,128)(2,1)S(1)}, u32[]{:S(2)}, u32[]{:S(2)}) collective-permute-start(bf16[96,4096]{1,0:T(8,128)(2,1)S(1)} %pad_maximum_fusion.refs_3_), channel_id=1, source_target_pairs={{0,24},{1,9},{8,0},{9,17},{16,8},{17,25},{24,16},{25,1},{2,26},{3,... | collective-permute-start | bytes 2359304 | tf_op jit(solution)/shard_map/ppermute | solution.py:27
  77.7 16.2 %collective-permute-start.20 = (bf16[128,2560]{1,0:T(8,128)(2,1)S(1)}, bf16[128,2560]{1,0:T(8,128)(2,1)S(1)}, u32[]{:S(2)}, u32[]{:S(2)}) collective-permute-start(bf16[128,2560]{1,0:T(8,128)(2,1)S(1)} %collective-permute-done.14.refs_3_), channel_id=1, source_target_pairs={{0,224},{1,33},{32,0},{33,65},{64,32},{65,97},{96,64},{97,129},{12... | collective-permute-start | bytes 1966088 | tf_op jit(solution)/shard_map/ppermute | solution.py:27
  80.1 18.8 %collective-permute-start.19 = (bf16[96,4096]{1,0:T(8,128)(2,1)S(1)}, bf16[96,4096]{1,0:T(8,128)(2,1)S(1)}, u32[]{:S(2)}, u32[]{:S(2)}) collective-permute-start(bf16[96,4096]{1,0:T(8,128)(2,1)S(1)} %collective-permute-done.18.refs_4_), channel_id=1, source_target_pairs={{0,8},{1,25},{8,16},{9,1},{16,24},{17,9},{24,0},{25,17},{2,10},{3,... | collective-permute-start | bytes 2359304 | tf_op jit(solution)/shard_map/ppermute | solution.py:27
  90.8 11.8 %collective-permute-start.16 = (bf16[128,2560]{1,0:T(8,128)(2,1)S(1)}, bf16[128,2560]{1,0:T(8,128)(2,1)S(1)}, u32[]{:S(2)}, u32[]{:S(2)}) collective-permute-start(bf16[128,2560]{1,0:T(8,128)(2,1)S(1)} %collective-permute-done.12.refs_0_), channel_id=1, source_target_pairs={{0,32},{1,225},{32,64},{33,1},{64,96},{65,33},{96,128},{97,65},{12... | collective-permute-start | bytes 1966088 | tf_op jit(solution)/shard_map/ppermute | solution.py:27
  106.5 17.0 %collective-permute-start.23 = (bf16[512,512]{1,0:T(8,128)(2,1)}, bf16[512,512]{1,0:T(8,128)(2,1)S(1)}, u32[]{:S(2)}, u32[]{:S(2)}) collective-permute-start(bf16[512,512]{1,0:T(8,128)(2,1)} %get-tuple-element.48), channel_id=1, source_target_pairs={{0,1},{1,0},{2,3},{3,2},{4,5},{5,4},{6,7},{7,6},{8,9},{9,8},{10,11... | collective-permute-start | bytes 1572872 | tf_op jit(solution)/shard_map/ppermute | solution.py:409
  117.0 13.4 %all-to-all-start.1 = ((bf16[32,8,128]{2,1,0:T(8,128)(2,1)}), bf16[32,8,128]{2,1,0:T(8,128)(2,1)S(1)}, u32[]{:S(2)}, u32[]{:S(2)}) async-start(bf16[32,8,128]{2,1,0:T(8,128)(2,1)} %broadcast_in_dim.2), calls=%async_computation.1 | async-start | bytes 131072 | tf_op jit(solution)/shard_map/all_to_all | solution.py:407
  121.7 1.6 %copy-start.1 = (bf16[32,64,512]{2,1,0:T(8,128)(2,1)S(1)}, bf16[32,64,512]{2,1,0:T(8,128)(2,1)}, u32[]{:S(2)}) copy-start(bf16[32,64,512]{2,1,0:T(8,128)(2,1)} %param.10) | copy-start | bytes 6291460
  124.3 8.8 %collective-permute-start.24 = (bf16[128,512]{1,0:T(8,128)(2,1)}, bf16[128,512]{1,0:T(8,128)(2,1)S(1)}, u32[]{:S(2)}, u32[]{:S(2)}) collective-permute-start(bf16[128,512]{1,0:T(8,128)(2,1)} %get-tuple-element.50), channel_id=1, source_target_pairs={{0,2},{2,4},{4,6},{6,0},{1,3},{3,5},{5,7},{7,1},{8,10},{10,12},{12... | collective-permute-start | bytes 393224 | tf_op jit(solution)/shard_map/ppermute | solution.py:415
  124.8 8.3 %collective-permute-start.25 = (bf16[128,512]{1,0:T(8,128)(2,1)}, bf16[128,512]{1,0:T(8,128)(2,1)S(1)}, u32[]{:S(2)}, u32[]{:S(2)}) collective-permute-start(bf16[128,512]{1,0:T(8,128)(2,1)} %get-tuple-element.51), channel_id=1, source_target_pairs={{0,4},{2,6},{4,0},{6,2},{1,5},{3,7},{5,1},{7,3},{8,12},{10,14},{12... | collective-permute-start | bytes 393224 | tf_op jit(solution)/shard_map/ppermute | solution.py:415
  126.9 6.8 %collective-permute-start.26 = (bf16[128,512]{1,0:T(8,128)(2,1)}, bf16[128,512]{1,0:T(8,128)(2,1)S(1)}, u32[]{:S(2)}, u32[]{:S(2)}) collective-permute-start(bf16[128,512]{1,0:T(8,128)(2,1)} %get-tuple-element.52), channel_id=1, source_target_pairs={{0,6},{2,0},{4,2},{6,4},{1,7},{3,1},{5,3},{7,5},{8,14},{10,8},{12,... | collective-permute-start | bytes 393224 | tf_op jit(solution)/shard_map/ppermute | solution.py:415
  130.4 0.8 copy-start.10

commit v4 on v3

--- a/solution.py
+++ b/solution.py
@@ -200,8 +200,14 @@
     slots[:, :rank], slots[:, rank:] = total, total
 
 
-def last_kernel(cut, info, a, far, w, far_a, far_b, base_own, base_near, keep, send, acc_a, acc_b, base, sems):
+def last_kernel(cut, info, a, far, weights, far_a, far_b, base_own, base_near, keep, send,
+                acc_a, acc_b, base, w, sems, sems_w):
+    edges = [cut * k // 4 for k in range(4)] + [cut + (w.shape[0] - cut) * k // 4 for k in range(5)]
+    parts = [pl.ds(at, to - at) for at, to in zip(edges, edges[1:])]
+    loads = start([(weights.at[at], w.at[at]) for at in parts], sems_w)
+    wait(loads[:4])
     multiply(a, w.at[:cut], None, acc_a)
+    wait(loads[4:])
     multiply(far, w.at[cut:], None, acc_b)
     n = a.shape[0]
     rows, width = n // 4, base.shape[1]
@@ -242,10 +248,6 @@
         ref[...] = both.astype(ref.dtype)
 
 
-def load_kernel(source, out):
-    out[...] = source[...]
-
-
 def delta_kernel(rank, slots, mine, up, delta):
     slot, adapter = mine[:, :1], mine[:, 1:2]
     n = mine.shape[0]
@@ -268,7 +270,7 @@
         out[at, :] = (part + delta[at, :]).astype(BF16)
 
 
-def local(kernel, out_shape, places, scratch=(), flops=1 << 20, name=None, out="v"):
+def local(kernel, out_shape, places, scratch=(), flops=1 << 20, name=None, out="v", limit=VMEM_LIMIT):
     vmem = pl.BlockSpec(memory_space=pltpu.VMEM)
     specs = {"s": pl.BlockSpec(memory_space=pltpu.SMEM), "v": vmem, "h": pl.BlockSpec(memory_space=pl.ANY)}
     return pl.pallas_call(
@@ -277,7 +279,7 @@
         in_specs=[specs[place] for place in places],
         out_specs=tuple(specs[p] for p in out) if len(out) > 1 else jax.tree.map(lambda _: vmem, out_shape),
         scratch_shapes=scratch,
-        compiler_params=pltpu.CompilerParams(vmem_limit_bytes=VMEM_LIMIT),
+        compiler_params=pltpu.CompilerParams(vmem_limit_bytes=limit),
         cost_estimate=pl.CostEstimate(flops=flops, bytes_accessed=4 << 20, transcendentals=0),
         name=name,
     )
@@ -388,25 +390,28 @@
     keep, send = local(
         functools.partial(last_kernel, cut),
         (four, four),
-        "svvvvvvv",
+        "svvhvvvv",
         [
             pltpu.VMEM((n, out_width), F32),
             pltpu.VMEM((3 * rows, out_width), F32),
             pltpu.VMEM((8 * n, out_width), BF16),
+            pltpu.VMEM((width, out_width), BF16),
+            pltpu.SemaphoreType.DMA((8,)),
             pltpu.SemaphoreType.DMA((8,)),
         ],
         cost(4),
         "last",
         "hh",
+        56 << 20,
     )(info, after(a[4], slots), far_2, down_matrix, far_a, far_b, base_own, base_near)
 
     slots = lax.all_to_all(slots, ("y", "core"), 0, 0, tiled=True)
-    slots = jnp.sum(slots.reshape(8, 8, LANES), axis=0)
+    parts = slots
+    slots = jnp.sum(after(parts, send).reshape(8, 8, LANES), axis=0)
     slots = jnp.broadcast_to(slots[None], (adapters, 8, LANES)).reshape(adapters * 8, LANES)
-    shared = slots
     slots = lax.all_to_all(slots, ("z", "x"), 0, 0, tiled=True).astype(BF16)
 
-    given = lax.ppermute(send, "core", [(0, 1), (1, 0)])
+    given = lax.ppermute(after(send, parts), "core", [(0, 1), (1, 0)])
     pairs = local(
         pair_kernel, (jax.ShapeDtypeStruct((n, out_width), F32), block, block, block), "vv", name="pair"
     )(keep, given)
@@ -414,7 +419,6 @@
     for by in range(1, 4):
         got.append(lax.ppermute(pairs[by], "y", [(i, (i + by) % 4) for i in range(4)]))
     up = up_factors.reshape(adapters * rank, out_width)
-    up = local(load_kernel, jax.ShapeDtypeStruct(up.shape, BF16), "v", name="load")(after(up, shared))
     delta = local(
         functools.partial(delta_kernel, rank),
         jax.ShapeDtypeStruct((n, out_width), F32),

time: 135 us -> 134 us (level)
  blocking collectives: 9.8 us -> 0 us
  starting transfers between devices: 39.6 us -> 47.9 us
  Pallas kernels: 21.5 us -> 25.2 us
  local copies, waits for them, and re-layouts: 14.8 us -> 12.1 us
    all_to_all x1 -> x0, blocking collectives: 9.8 us -> none  [shards(): slots = lax.all_to_all(slots, ('y', 'core'), 0, 0, tiled=True)]
    all_to_all x0 -> x1, starting transfers between devices: none -> 4.48 us  [shards(): slots = lax.all_to_all(slots, ('y', 'core'), 0, 0, tiled=True)]
    pallas_call x2 -> x1, Pallas kernels: 3.24 us -> 6.99 us  [shards(): local(functools.partial(last_kernel, cut), (four, four), 'svvhvvvv', [plt...]
    unnamed x34 -> x50, local copies, waits for them, and re-layouts: 12.2 us -> 9.5 us
    ppermute x3, starting transfers between devices: 3.71 us -> 5.88 us  [shards(): lax.ppermute(pairs[by], 'y', [(i, (i + by) % 4) for i in range(4)])]
  transfers between devices with their start and end apart: 28 -> 29, of which waited for: 16 -> 15; matrix products, arithmetic and copies ran while one was open for 5% -> 5% of each run, Pallas kernels for 12% -> 17%
where the time goes in v4:
time: 134 us
  starting transfers between devices  47.9 us (36%)
  waiting for transfers between devices  45.4 us (34%)
  Pallas kernels  25.2 us (19%)
  local copies, waits for them, and re-layouts  12.1 us (9%)
  other arithmetic  2.75 us (2%)
    ppermute x23, waiting for transfers between devices, turn(): return lax.ppermute(value, (axis, 'core'), pairs)  41.5 us
    ppermute x23, starting transfers between devices, turn(): return lax.ppermute(value, (axis, 'core'), pairs)  31.3 us
    unnamed x50, local copies, waits for them, and re-layouts  9.5 us
    pallas_call x1, Pallas kernels, shards(): local(functools.partial(last_kernel, cut), (four, four), 'svvhvvvv', [plt...  6.99 us
    pallas_call x1, Pallas kernels, shards(): local(functools.partial(near_kernel, cut), (sums(16), sums(12)), 'hhhhhhh...  6.2 us
    ppermute x3, starting transfers between devices, shards(): lax.ppermute(pairs[by], 'y', [(i, (i + by) % 4) for i in range(4)])  5.88 us
    all_to_all x1, starting transfers between devices, shards(): slots = lax.all_to_all(slots, ('z', 'x'), 0, 0, tiled=True).astype(BF16)  5.67 us
    pallas_call x1, Pallas kernels, shards(): local(functools.partial(far_kernel, cut), (jax.ShapeDtypeStruct((4 * n, o...  4.93 us
  transfers between devices with their start and end apart: 29, of which 15 were waited for; matrix products, arithmetic and copies ran while one was open for 5% of the time, Pallas kernels for 17%

profile of v4, /device:TPU:2, one launch (start us, length us, event | category | flops | bytes accessed | tf_op | source)
XLA Modules:
  0.0 133.7 jit_solution(6727942719076103759)
XLA Ops:
  0.0 1.0 slice.19
  1.0 2.0 %collective-permute-start.3 = (bf16[32,4096]{1,0:T(8,128)(2,1)S(1)}, bf16[32,4096]{1,0:T(8,128)(2,1)S(1)}, u32[]{:S(2)}, u32[]{:S(2)}) collective-permute-start(bf16[32,4096]{1,0:T(8,128)(2,1)S(1)} %slice.19), channel_id=1, source_target_pairs={{0,32},{1,225},{32,64},{33,1},{64,96},{65,33},{96,128},{97,65},{12... | collective-permute-start | bytes 786440 | tf_op jit(solution)/shard_map/ppermute | solution.py:27
  3.0 1.5 %collective-permute-start = (bf16[32,6656]{1,0:T(8,128)(2,1)}, bf16[32,6656]{1,0:T(8,128)(2,1)S(1)}, u32[]{:S(2)}, u32[]{:S(2)}) collective-permute-start(bf16[32,6656]{1,0:T(8,128)(2,1)} %refs_0_.1), channel_id=1, source_target_pairs={{0,8},{1,25},{8,16},{9,1},{16,24},{17,9},{24,0},{25,17},{2,10},{3,... | collective-permute-start | bytes 1277960 | tf_op jit(solution)/shard_map/ppermute | solution.py:27
  4.5 0.5 collective-permute-start.2
  5.1 4.0 %collective-permute-start.6 = (bf16[32,4096]{1,0:T(8,128)(2,1)S(1)}, bf16[32,4096]{1,0:T(8,128)(2,1)S(1)}, u32[]{:S(2)}, u32[]{:S(2)}) collective-permute-start(bf16[32,4096]{1,0:T(8,128)(2,1)S(1)} %slice.19), channel_id=1, source_target_pairs={{0,224},{1,33},{32,0},{33,65},{64,32},{65,97},{96,64},{97,129},{12... | collective-permute-start | bytes 786440 | tf_op jit(solution)/shard_map/ppermute | solution.py:27
  9.1 2.2 %collective-permute-done.3 = bf16[32,4096]{1,0:T(8,128)(2,1)S(1)} collective-permute-done((bf16[32,4096]{1,0:T(8,128)(2,1)S(1)}, bf16[32,4096]{1,0:T(8,128)(2,1)S(1)}, u32[]{:S(2)}, u32[]{:S(2)}) %collective-permute-start.3) | collective-permute-done | bytes 262176 | tf_op jit(solution)/shard_map/ppermute | solution.py:27
  11.3 0.7 constant_dynamic-update-slice_fusion.3
  12.1 0.9 collective-permute-done.6
  13.0 3.7 %collective-permute-start.7 = (bf16[32,4096]{1,0:T(8,128)(2,1)S(1)}, bf16[32,4096]{1,0:T(8,128)(2,1)S(1)}, u32[]{:S(2)}, u32[]{:S(2)}) collective-permute-start(bf16[32,4096]{1,0:T(8,128)(2,1)S(1)} %collective-permute-done.6), channel_id=1, source_target_pairs={{0,224},{1,33},{32,0},{33,65},{64,32},{65,97},{96,64},{97,129},{12... | collective-permute-start | bytes 786440 | tf_op jit(solution)/shard_map/ppermute | solution.py:27
  16.7 0.7 constant_dynamic-update-slice_fusion.2
  17.4 1.5 %collective-permute-start.1 = (bf16[32,6656]{1,0:T(8,128)(2,1)S(1)}, bf16[32,6656]{1,0:T(8,128)(2,1)S(1)}, u32[]{:S(2)}, u32[]{:S(2)}) collective-permute-start(bf16[32,6656]{1,0:T(8,128)(2,1)S(1)} %collective-permute-done.refs_1_), channel_id=1, source_target_pairs={{0,8},{1,25},{8,16},{9,1},{16,24},{17,9},{24,0},{25,17},{2,10},{3,... | collective-permute-start | bytes 1277960 | tf_op jit(solution)/shard_map/ppermute | solution.py:27
  18.9 1.7 %collective-permute-done.4 = bf16[32,4096]{1,0:T(8,128)(2,1)S(1)} collective-permute-done((bf16[32,4096]{1,0:T(8,128)(2,1)S(1)}, bf16[32,4096]{1,0:T(8,128)(2,1)S(1)}, u32[]{:S(2)}, u32[]{:S(2)}) %collective-permute-start.4) | collective-permute-done | bytes 262176 | tf_op jit(solution)/shard_map/ppermute | solution.py:27
  20.6 0.7 constant_dynamic-update-slice_fusion.1
  21.3 0.7 constant_dynamic-update-slice_fusion.refs_4_
  22.0 1.5 %collective-permute-start.10 = (bf16[128,4096]{1,0:T(8,128)(2,1)}, bf16[128,4096]{1,0:T(8,128)(2,1)}, u32[]{:S(2)}, u32[]{:S(2)}) collective-permute-start(bf16[128,4096]{1,0:T(8,128)(2,1)} %constant_dynamic-update-slice_fusion.refs_4_), channel_id=1, source_target_pairs={{0,8},{1,25},{8,16},{9,1},{16,24},{17,9},{24,0},{25,17},{2,10},{3,... | collective-permute-start | bytes 3145736 | tf_op jit(solution)/shard_map/ppermute | solution.py:27
  23.6 0.8 copy-done.7
  24.4 1.7 %collective-permute-start.5 = (bf16[32,4096]{1,0:T(8,128)(2,1)S(1)}, bf16[32,4096]{1,0:T(8,128)(2,1)}, u32[]{:S(2)}, u32[]{:S(2)}) collective-permute-start(bf16[32,4096]{1,0:T(8,128)(2,1)S(1)} %collective-permute-done.4), channel_id=1, source_target_pairs={{0,32},{1,225},{32,64},{33,1},{64,96},{65,33},{96,128},{97,65},{12... | collective-permute-start | bytes 786440 | tf_op jit(solution)/shard_map/ppermute | solution.py:27
  26.1 1.8 %collective-permute-start.8 = (bf16[32,4096]{1,0:T(8,128)(2,1)S(1)}, bf16[32,4096]{1,0:T(8,128)(2,1)}, u32[]{:S(2)}, u32[]{:S(2)}) collective-permute-start(bf16[32,4096]{1,0:T(8,128)(2,1)S(1)} %collective-permute-done.7), channel_id=1, source_target_pairs={{0,224},{1,33},{32,0},{33,65},{64,32},{65,97},{96,64},{97,129},{12... | collective-permute-start | bytes 786440 | tf_op jit(solution)/shard_map/ppermute | solution.py:27
  27.9 0.8 copy-done.9
  28.6 0.9 pad_maximum_fusion.1
  29.5 5.4 %collective-permute-done.5 = bf16[32,4096]{1,0:T(8,128)(2,1)} collective-permute-done((bf16[32,4096]{1,0:T(8,128)(2,1)S(1)}, bf16[32,4096]{1,0:T(8,128)(2,1)}, u32[]{:S(2)}, u32[]{:S(2)}) %collective-permute-start.5) | collective-permute-done | bytes 262176 | tf_op jit(solution)/shard_map/ppermute | solution.py:27
  35.0 3.1 %collective-permute-start.9 = (bf16[128,2560]{1,0:T(8,128)(2,1)}, bf16[128,2560]{1,0:T(8,128)(2,1)}, u32[]{:S(2)}, u32[]{:S(2)}) collective-permute-start(bf16[128,2560]{1,0:T(8,128)(2,1)} %pad_maximum_fusion.1), channel_id=1, source_target_pairs={{0,32},{1,225},{32,64},{33,1},{64,96},{65,33},{96,128},{97,65},{12... | collective-permute-start | bytes 1966088 | tf_op jit(solution)/shard_map/ppermute | solution.py:27
  38.1 3.9 %collective-permute-start.17 = (bf16[32,4096]{1,0:T(8,128)(2,1)}, bf16[32,4096]{1,0:T(8,128)(2,1)}, u32[]{:S(2)}, u32[]{:S(2)}) collective-permute-start(bf16[32,4096]{1,0:T(8,128)(2,1)} %collective-permute-done.5), channel_id=1, source_target_pairs={{0,32},{1,225},{32,64},{33,1},{64,96},{65,33},{96,128},{97,65},{12... | collective-permute-start | bytes 786440 | tf_op jit(solution)/shard_map/ppermute | solution.py:27
  42.0 0.6 broadcast.4
  42.6 0.7 reduce.3
  43.3 0.1 reshape.20.ids_ref
  43.3 0.1 stack.23.info
  43.4 1.2 copy-done.6
  44.6 1.5 %plan.1 = (bf16[1024,64]{1,0:T(8,128)(2,1)S(1)}, s32[128,128]{1,0:T(8,128)S(1)}, bf16[64,6656]{1,0:T(8,128)(2,1)S(1)}) custom-call(s32[5]{0:T(128)S(1)} %stack.23.info, s32[32,32]{1,0:T(8,128)S(1)} %reshape.20.ids_ref, bf16[64,6656]{1,0:T(8,128)(2,1)S(1)} %bitcast.17, f32[1,6656]{1,0:T(1,128)S(1)} %copy-done.14), custom_call_target="tpu_custom_call" | custom-call | flops 1048576 | bytes 4194304 | tf_op jit(solution)/shard_map/plan/pallas_call | solution.py:301
  46.1 0.1 collective-permute-start.15
  46.2 7.9 %collective-permute-done.9.refs_0_ = bf16[128,2560]{1,0:T(8,128)(2,1)} collective-permute-done((bf16[128,2560]{1,0:T(8,128)(2,1)}, bf16[128,2560]{1,0:T(8,128)(2,1)}, u32[]{:S(2)}, u32[]{:S(2)}) %collective-permute-start.9) | collective-permute-done | bytes 655392 | tf_op jit(solution)/shard_map/ppermute | solution.py:27
  54.1 2.8 %collective-permute-done.17 = bf16[32,4096]{1,0:T(8,128)(2,1)} collective-permute-done((bf16[32,4096]{1,0:T(8,128)(2,1)}, bf16[32,4096]{1,0:T(8,128)(2,1)}, u32[]{:S(2)}, u32[]{:S(2)}) %collective-permute-start.17) | collective-permute-done | bytes 262176 | tf_op jit(solution)/shard_map/ppermute | solution.py:27
  56.9 1.2 pad_maximum_fusion.refs_3_
  58.0 0.3 collective-permute-start.18
  58.3 1.6 %collective-permute-done.13.refs_1_ = bf16[128,2560]{1,0:T(8,128)(2,1)} collective-permute-done((bf16[128,2560]{1,0:T(8,128)(2,1)}, bf16[128,2560]{1,0:T(8,128)(2,1)}, u32[]{:S(2)}, u32[]{:S(2)}) %collective-permute-start.13) | collective-permute-done | bytes 655392 | tf_op jit(solution)/shard_map/ppermute | solution.py:27
  60.0 1.2 collective-permute-start.14
  61.2 2.9 %copy-done = bf16[6656,512]{1,0:T(8,128)(2,1)S(1)} copy-done((bf16[6656,512]{1,0:T(8,128)(2,1)S(1)}, bf16[6656,512]{1,0:T(8,128)(2,1)}, u32[]{:S(2)}) %copy-start) | copy-done | bytes 6815768
  64.1 2.2 %own.1 = (bf16[128,512]{1,0:T(8,128)(2,1)S(1)}, f32[64,64]{1,0:T(8,128)S(1)}) custom-call(bf16[32,6656]{1,0:T(8,128)(2,1)S(1)} %copy-done.5, bf16[32,6656]{1,0:T(8,128)(2,1)S(1)} %collective-permute-done.refs_1_, bf16[32,6656]{1,0:T(8,128)(2,1)S(1)} %copy-done.10, bf16[32,6656]{1,0:T(8,128)(2,1)S(1)} %copy-done.8, bf16[6656,512]{1,0:T(8,128)(2,1)S(1)} %copy-done, ...), custom_call_target="tpu_custom_call" | custom-call | flops 981467136 | bytes 4194304 | tf_op jit(solution)/shard_map/own/pallas_call | solution.py:344
  66.4 5.8 %collective-permute-done.11.refs_2_ = bf16[128,2560]{1,0:T(8,128)(2,1)S(1)} collective-permute-done((bf16[128,2560]{1,0:T(8,128)(2,1)}, bf16[128,2560]{1,0:T(8,128)(2,1)S(1)}, u32[]{:S(2)}, u32[]{:S(2)}) %collective-permute-start.11) | collective-permute-done | bytes 655392 | tf_op jit(solution)/shard_map/ppermute | solution.py:27
  72.2 0.4 collective-permute-start.21
  72.5 1.7 %collective-permute-start.22 = (bf16[96,4096]{1,0:T(8,128)(2,1)S(1)}, bf16[96,4096]{1,0:T(8,128)(2,1)S(1)}, u32[]{:S(2)}, u32[]{:S(2)}) collective-permute-start(bf16[96,4096]{1,0:T(8,128)(2,1)S(1)} %pad_maximum_fusion.refs_3_), channel_id=1, source_target_pairs={{0,24},{1,9},{8,0},{9,17},{16,8},{17,25},{24,16},{25,1},{2,26},{3,... | collective-permute-start | bytes 2359304 | tf_op jit(solution)/shard_map/ppermute | solution.py:27
  74.2 2.9 %collective-permute-done.14.refs_3_ = bf16[128,2560]{1,0:T(8,128)(2,1)S(1)} collective-permute-done((bf16[128,2560]{1,0:T(8,128)(2,1)}, bf16[128,2560]{1,0:T(8,128)(2,1)S(1)}, u32[]{:S(2)}, u32[]{:S(2)}) %collective-permute-start.14) | collective-permute-done | bytes 655392 | tf_op jit(solution)/shard_map/ppermute | solution.py:27
  77.1 2.4 %collective-permute-start.20 = (bf16[128,2560]{1,0:T(8,128)(2,1)S(1)}, bf16[128,2560]{1,0:T(8,128)(2,1)S(1)}, u32[]{:S(2)}, u32[]{:S(2)}) collective-permute-start(bf16[128,2560]{1,0:T(8,128)(2,1)S(1)} %collective-permute-done.14.refs_3_), channel_id=1, source_target_pairs={{0,224},{1,33},{32,0},{33,65},{64,32},{65,97},{96,64},{97,129},{12... | collective-permute-start | bytes 1966088 | tf_op jit(solution)/shard_map/ppermute | solution.py:27
  79.6 6.2 %near.1 = (f32[512,576]{1,0:T(8,128)S(1)}, f32[384,576]{1,0:T(8,128)S(1)}) custom-call(bf16[128,2560]{1,0:T(8,128)(2,1)} %collective-permute-done.9.refs_0_, bf16[128,2560]{1,0:T(8,128)(2,1)} %collective-permute-done.13.refs_1_, bf16[128,2560]{1,0:T(8,128)(2,1)S(1)} %collective-permute-done.11.refs_2_, ...), custom_call_target="tpu_custom_call" | custom-call | flops 3435134976 | bytes 4194304 | tf_op jit(solution)/shard_map/near/pallas_call | solution.py:357
  85.8 3.4 %collective-permute-done.12.refs_0_ = bf16[128,2560]{1,0:T(8,128)(2,1)S(1)} collective-permute-done((bf16[128,2560]{1,0:T(8,128)(2,1)S(1)}, bf16[128,2560]{1,0:T(8,128)(2,1)S(1)}, u32[]{:S(2)}, u32[]{:S(2)}) %collective-permute-start.12) | collective-permute-done | bytes 655392 | tf_op jit(solution)/shard_map/ppermute | solution.py:27
  89.2 3.9 %collective-permute-done.22.refs_5_ = bf16[96,4096]{1,0:T(8,128)(2,1)S(1)} collective-permute-done((bf16[96,4096]{1,0:T(8,128)(2,1)S(1)}, bf16[96,4096]{1,0:T(8,128)(2,1)S(1)}, u32[]{:S(2)}, u32[]{:S(2)}) %collective-permute-start.22) | collective-permute-done | bytes 786464 | tf_op jit(solution)/shard_map/ppermute | solution.py:27
  93.1 0.8 collective-permute-done.20.refs_1_
  93.9 4.9 %far.1 = (bf16[512,512]{1,0:T(8,128)(2,1)S(1)}, f32[256,576]{1,0:T(8,128)S(1)}, f32[288,576]{1,0:T(8,128)S(1)}, f32[64,64]{1,0:T(8,128)S(1)}) custom-call(bf16[128,2560]{1,0:T(8,128)(2,1)S(1)} %collective-permute-done.12.refs_0_, bf16[128,2560]{1,0:T(8,128)(2,1)S(1)} %collective-permute-done.20.refs_1_, ...), custom_call_target="tpu_custom_call" | custom-call | flops 2699034624 | bytes 4194304 | tf_op jit(solution)/shard_map/far/pallas_call | solution.py:369
  98.9 2.1 %collective-permute-done.16.a = bf16[128,2560]{1,0:T(8,128)(2,1)S(1)} collective-permute-done((bf16[128,2560]{1,0:T(8,128)(2,1)S(1)}, bf16[128,2560]{1,0:T(8,128)(2,1)S(1)}, u32[]{:S(2)}, u32[]{:S(2)}) %collective-permute-start.16) | collective-permute-done | bytes 655392 | tf_op jit(solution)/shard_map/ppermute | solution.py:27
  101.0 1.4 %slots.1 = f32[64,128]{1,0:T(8,128)} custom-call(bf16[128,2560]{1,0:T(8,128)(2,1)S(1)} %collective-permute-done.16.a, bf16[96,4096]{1,0:T(8,128)(2,1)S(1)} %collective-permute-done.19.far, bf16[64,6656]{1,0:T(8,128)(2,1)S(1)} %get-tuple-element.33.refs_5_.refs_8_.refs_7_.d, bf16[1024,64]{1,0:T(8,128)(2,1)S(1)} %get-tuple-element.34.refs_6_.refs_8_.fill, ...), custom_call_target="tpu_custom_call" | custom-call | flops 109051904 | bytes 4194304 | tf_op jit(solution)/shard_map/slots/pallas_call | solution.py:383
  102.4 4.5 %all-to-all-start = ((f32[8,8,128]{2,1,0:T(8,128)}), f32[8,8,128]{2,1,0:T(8,128)S(1)}, u32[]{:S(2)}, u32[]{:S(2)}) async-start(f32[8,8,128]{2,1,0:T(8,128)} %bitcast.6), calls=%async_computation | async-start | bytes 65536 | tf_op jit(solution)/shard_map/all_to_all | solution.py:408
  106.9 7.0 %last.1 = (bf16[512,512]{1,0:T(8,128)(2,1)}, bf16[512,512]{1,0:T(8,128)(2,1)}) custom-call(s32[5]{0:T(128)} %copy-done.15, bf16[128,2560]{1,0:T(8,128)(2,1)} %copy-done.3, bf16[96,4096]{1,0:T(8,128)(2,1)} %copy-done.1, bf16[6656,512]{1,0:T(8,128)(2,1)} %weights.1, f32[256,576]{1,0:T(8,128)} %copy-done.4, f32[288,576]{1,0:T(8,128)} %copy-done.2, ...), custom_call_target="tpu_custom_call" | custom-call | flops 981467136 | bytes 4194304 | tf_op jit(solution)/shard_map/last/pallas_call | solution.py:390
  113.9 0.6 collective-permute-start.23
  114.5 0.6 broadcast_in_dim.2
  115.1 5.7 %all-to-all-start.1 = ((bf16[32,8,128]{2,1,0:T(8,128)(2,1)}), bf16[32,8,128]{2,1,0:T(8,128)(2,1)S(1)}, u32[]{:S(2)}, u32[]{:S(2)}) async-start(bf16[32,8,128]{2,1,0:T(8,128)(2,1)} %broadcast_in_dim.2), calls=%async_computation.1 | async-start | bytes 131072 | tf_op jit(solution)/shard_map/all_to_all | solution.py:412
  120.8 1.0 copy-done.11
  121.9 0.1 pair.1
  122.0 1.7 %collective-permute-start.24 = (bf16[128,512]{1,0:T(8,128)(2,1)S(1)}, bf16[128,512]{1,0:T(8,128)(2,1)S(1)}, u32[]{:S(2)}, u32[]{:S(2)}) collective-permute-start(bf16[128,512]{1,0:T(8,128)(2,1)S(1)} %get-tuple-element.54), channel_id=1, source_target_pairs={{0,2},{2,4},{4,6},{6,0},{1,3},{3,5},{5,7},{7,1},{8,10},{10,12},{12... | collective-permute-start | bytes 393224 | tf_op jit(solution)/shard_map/ppermute | solution.py:420
  123.7 2.7 %collective-permute-start.25 = (bf16[128,512]{1,0:T(8,128)(2,1)S(1)}, bf16[128,512]{1,0:T(8,128)(2,1)S(1)}, u32[]{:S(2)}, u32[]{:S(2)}) collective-permute-start(bf16[128,512]{1,0:T(8,128)(2,1)S(1)} %get-tuple-element.55), channel_id=1, source_target_pairs={{0,4},{2,6},{4,0},{6,2},{1,5},{3,7},{5,1},{7,3},{8,12},{10,14},{12... | collective-permute-start | bytes 393224 | tf_op jit(solution)/shard_map/ppermute | solution.py:420
  126.4 1.5 %collective-permute-start.26 = (bf16[128,512]{1,0:T(8,128)(2,1)S(1)}, bf16[128,512]{1,0:T(8,128)(2,1)S(1)}, u32[]{:S(2)}, u32[]{:S(2)}) collective-permute-start(bf16[128,512]{1,0:T(8,128)(2,1)S(1)} %get-tuple-element.56), channel_id=1, source_target_pairs={{0,6},{2,0},{4,2},{6,4},{1,7},{3,1},{5,3},{7,5},{8,14},{10,8},{12,... | collective-permute-start | bytes 393224 | tf_op jit(solution)/shard_map/ppermute | solution.py:420
  127.9 1.6 %all-to-all-done.1 = bf16[32,8,128]{2,1,0:T(8,128)(2,1)S(1)} async-done(((bf16[32,8,128]{2,1,0:T(8,128)(2,1)}), bf16[32,8,128]{2,1,0:T(8,128)(2,1)S(1)}, u32[]{:S(2)}, u32[]{:S(2)}) %all-to-all-start.1) | async-done | bytes 65568 | tf_op jit(solution)/shard_map/all_to_all | solution.py:412
  129.5 0.6 delta.1
  130.1 2.2 %collective-permute-done.25.refs_2_ = bf16[128,512]{1,0:T(8,128)(2,1)S(1)} collective-permute-done((bf16[128,512]{1,0:T(8,128)(2,1)S(1)}, bf16[128,512]{1,0:T(8,128)(2,1)S(1)}, u32[]{:S(2)}, u32[]{:S(2)}) %collective-permute-start.25) | collective-permute-done | bytes 131104 | tf_op jit(solution)/shard_map/ppermute | solution.py:420
  132.4 1.3 sum.1
  (67 shorter events, 0.2 us)
Async XLA Ops:
  0.0 23.5 %copy-start.5 = (bf16[32,6656]{1,0:T(8,128)(2,1)S(1)}, bf16[32,6656]{1,0:T(8,128)(2,1)}, u32[]{:S(2)}) copy-start(bf16[32,6656]{1,0:T(8,128)(2,1)} %refs_0_.1) | copy-start | bytes 1277956
  1.0 10.3 %collective-permute-start.3 = (bf16[32,4096]{1,0:T(8,128)(2,1)S(1)}, bf16[32,4096]{1,0:T(8,128)(2,1)S(1)}, u32[]{:S(2)}, u32[]{:S(2)}) collective-permute-start(bf16[32,4096]{1,0:T(8,128)(2,1)S(1)} %slice.19), channel_id=1, source_target_pairs={{0,32},{1,225},{32,64},{33,1},{64,96},{65,33},{96,128},{97,65},{12... | collective-permute-start | bytes 786440 | tf_op jit(solution)/shard_map/ppermute | solution.py:27
  3.0 14.4 %collective-permute-start = (bf16[32,6656]{1,0:T(8,128)(2,1)}, bf16[32,6656]{1,0:T(8,128)(2,1)S(1)}, u32[]{:S(2)}, u32[]{:S(2)}) collective-permute-start(bf16[32,6656]{1,0:T(8,128)(2,1)} %refs_0_.1), channel_id=1, source_target_pairs={{0,8},{1,25},{8,16},{9,1},{16,24},{17,9},{24,0},{25,17},{2,10},{3,... | collective-permute-start | bytes 1277960 | tf_op jit(solution)/shard_map/ppermute | solution.py:27
  4.5 19.0 %collective-permute-start.2 = (bf16[32,6656]{1,0:T(8,128)(2,1)}, bf16[32,6656]{1,0:T(8,128)(2,1)S(1)}, u32[]{:S(2)}, u32[]{:S(2)}) collective-permute-start(bf16[32,6656]{1,0:T(8,128)(2,1)} %refs_0_.1), channel_id=1, source_target_pairs={{0,24},{1,9},{8,0},{9,17},{16,8},{17,25},{24,16},{25,1},{2,26},{3,... | collective-permute-start | bytes 1277960 | tf_op jit(solution)/shard_map/ppermute | solution.py:27
  5.1 7.9 %collective-permute-start.6 = (bf16[32,4096]{1,0:T(8,128)(2,1)S(1)}, bf16[32,4096]{1,0:T(8,128)(2,1)S(1)}, u32[]{:S(2)}, u32[]{:S(2)}) collective-permute-start(bf16[32,4096]{1,0:T(8,128)(2,1)S(1)} %slice.19), channel_id=1, source_target_pairs={{0,224},{1,33},{32,0},{33,65},{64,32},{65,97},{96,64},{97,129},{12... | collective-permute-start | bytes 786440 | tf_op jit(solution)/shard_map/ppermute | solution.py:27
  11.3 9.2 %collective-permute-start.4 = (bf16[32,4096]{1,0:T(8,128)(2,1)S(1)}, bf16[32,4096]{1,0:T(8,128)(2,1)S(1)}, u32[]{:S(2)}, u32[]{:S(2)}) collective-permute-start(bf16[32,4096]{1,0:T(8,128)(2,1)S(1)} %collective-permute-done.3), channel_id=1, source_target_pairs={{0,32},{1,225},{32,64},{33,1},{64,96},{65,33},{96,128},{97,65},{12... | collective-permute-start | bytes 786440 | tf_op jit(solution)/shard_map/ppermute | solution.py:27
  13.0 8.3 %collective-permute-start.7 = (bf16[32,4096]{1,0:T(8,128)(2,1)S(1)}, bf16[32,4096]{1,0:T(8,128)(2,1)S(1)}, u32[]{:S(2)}, u32[]{:S(2)}) collective-permute-start(bf16[32,4096]{1,0:T(8,128)(2,1)S(1)} %collective-permute-done.6), channel_id=1, source_target_pairs={{0,224},{1,33},{32,0},{33,65},{64,32},{65,97},{96,64},{97,129},{12... | collective-permute-start | bytes 786440 | tf_op jit(solution)/shard_map/ppermute | solution.py:27
  17.4 10.4 %collective-permute-start.1 = (bf16[32,6656]{1,0:T(8,128)(2,1)S(1)}, bf16[32,6656]{1,0:T(8,128)(2,1)S(1)}, u32[]{:S(2)}, u32[]{:S(2)}) collective-permute-start(bf16[32,6656]{1,0:T(8,128)(2,1)S(1)} %collective-permute-done.refs_1_), channel_id=1, source_target_pairs={{0,8},{1,25},{8,16},{9,1},{16,24},{17,9},{24,0},{25,17},{2,10},{3,... | collective-permute-start | bytes 1277960 | tf_op jit(solution)/shard_map/ppermute | solution.py:27
  22.0 20.6 %copy-start.20 = (s32[1024,1]{0,1:T(1,128)S(1)}, s32[1024,1]{0,1:T(1,128)}, u32[]{:S(2)}) copy-start(s32[1024,1]{0,1:T(1,128)} %param.11) | copy-start | bytes 12292
  22.0 21.4 %copy-start.14 = (f32[1,6656]{1,0:T(1,128)S(1)}, f32[1,6656]{1,0:T(1,128)}, u32[]{:S(2)}) copy-start(f32[1,6656]{1,0:T(1,128)} %scale.1) | copy-start | bytes 79876
  22.0 32.0 %collective-permute-start.10 = (bf16[128,4096]{1,0:T(8,128)(2,1)}, bf16[128,4096]{1,0:T(8,128)(2,1)}, u32[]{:S(2)}, u32[]{:S(2)}) collective-permute-start(bf16[128,4096]{1,0:T(8,128)(2,1)} %constant_dynamic-update-slice_fusion.refs_4_), channel_id=1, source_target_pairs={{0,8},{1,25},{8,16},{9,1},{16,24},{17,9},{24,0},{25,17},{2,10},{3,... | collective-permute-start | bytes 3145736 | tf_op jit(solution)/shard_map/ppermute | solution.py:27
  23.5 56.0 %slice-start = ((s8[6815744]{0:T(1024)(128)(4,1)}), s8[2621440]{0:T(1024)(128)(4,1)S(1)}, s32[]{:S(2)}) async-start(s8[6815744]{0:T(1024)(128)(4,1)} %bitcast.15), calls=%async_computation.2 | async-start | bytes 5242880
  23.6 0.8 copy-start.7
  24.4 10.6 %collective-permute-start.5 = (bf16[32,4096]{1,0:T(8,128)(2,1)S(1)}, bf16[32,4096]{1,0:T(8,128)(2,1)}, u32[]{:S(2)}, u32[]{:S(2)}) collective-permute-start(bf16[32,4096]{1,0:T(8,128)(2,1)S(1)} %collective-permute-done.4), channel_id=1, source_target_pairs={{0,32},{1,225},{32,64},{33,1},{64,96},{65,33},{96,128},{97,65},{12... | collective-permute-start | bytes 786440 | tf_op jit(solution)/shard_map/ppermute | solution.py:27
  26.1 8.9 %collective-permute-start.8 = (bf16[32,4096]{1,0:T(8,128)(2,1)S(1)}, bf16[32,4096]{1,0:T(8,128)(2,1)}, u32[]{:S(2)}, u32[]{:S(2)}) collective-permute-start(bf16[32,4096]{1,0:T(8,128)(2,1)S(1)} %collective-permute-done.7), channel_id=1, source_target_pairs={{0,224},{1,33},{32,0},{33,65},{64,32},{65,97},{96,64},{97,129},{12... | collective-permute-start | bytes 786440 | tf_op jit(solution)/shard_map/ppermute | solution.py:27
  27.9 0.8 copy-start.9
  35.0 19.1 %collective-permute-start.9 = (bf16[128,2560]{1,0:T(8,128)(2,1)}, bf16[128,2560]{1,0:T(8,128)(2,1)}, u32[]{:S(2)}, u32[]{:S(2)}) collective-permute-start(bf16[128,2560]{1,0:T(8,128)(2,1)} %pad_maximum_fusion.1), channel_id=1, source_target_pairs={{0,32},{1,225},{32,64},{33,1},{64,96},{65,33},{96,128},{97,65},{12... | collective-permute-start | bytes 1966088 | tf_op jit(solution)/shard_map/ppermute | solution.py:27
  38.1 18.8 %collective-permute-start.17 = (bf16[32,4096]{1,0:T(8,128)(2,1)}, bf16[32,4096]{1,0:T(8,128)(2,1)}, u32[]{:S(2)}, u32[]{:S(2)}) collective-permute-start(bf16[32,4096]{1,0:T(8,128)(2,1)} %collective-permute-done.5), channel_id=1, source_target_pairs={{0,32},{1,225},{32,64},{33,1},{64,96},{65,33},{96,128},{97,65},{12... | collective-permute-start | bytes 786440 | tf_op jit(solution)/shard_map/ppermute | solution.py:27
  42.0 18.0 %collective-permute-start.13 = (bf16[128,2560]{1,0:T(8,128)(2,1)}, bf16[128,2560]{1,0:T(8,128)(2,1)}, u32[]{:S(2)}, u32[]{:S(2)}) collective-permute-start(bf16[128,2560]{1,0:T(8,128)(2,1)} %pad_maximum_fusion.1), channel_id=1, source_target_pairs={{0,224},{1,33},{32,0},{33,65},{64,32},{65,97},{96,64},{97,129},{12... | collective-permute-start | bytes 1966088 | tf_op jit(solution)/shard_map/ppermute | solution.py:27
  43.4 22.9 %copy-start.15 = (s32[5]{0:T(128)}, s32[5]{0:T(128)S(1)}, u32[]{:S(2)}) copy-start(s32[5]{0:T(128)S(1)} %stack.23.info) | copy-start | bytes 64
  43.4 1.2 copy-start.6
  44.6 16.6 %copy-start.8 = (bf16[32,6656]{1,0:T(8,128)(2,1)S(1)}, bf16[32,6656]{1,0:T(8,128)(2,1)}, u32[]{:S(2)}) copy-start(bf16[32,6656]{1,0:T(8,128)(2,1)} %copy-done.7) | copy-start | bytes 1277956
  44.6 16.6 %copy-start.10 = (bf16[32,6656]{1,0:T(8,128)(2,1)S(1)}, bf16[32,6656]{1,0:T(8,128)(2,1)}, u32[]{:S(2)}) copy-start(bf16[32,6656]{1,0:T(8,128)(2,1)} %copy-done.9) | copy-start | bytes 1277956
  46.1 20.3 %copy-start.18 = (s32[128,128]{1,0:T(8,128)}, s32[128,128]{1,0:T(8,128)S(1)}, u32[]{:S(2)}) copy-start(s32[128,128]{1,0:T(8,128)S(1)} %get-tuple-element.41.mine) | copy-start | bytes 196612
  46.1 26.4 %collective-permute-start.15 = (bf16[128,4096]{1,0:T(8,128)(2,1)}, bf16[128,4096]{1,0:T(8,128)(2,1)S(1)}, u32[]{:S(2)}, u32[]{:S(2)}) collective-permute-start(bf16[128,4096]{1,0:T(8,128)(2,1)} %constant_dynamic-update-slice_fusion.refs_4_), channel_id=1, source_target_pairs={{0,24},{1,9},{8,0},{9,17},{16,8},{17,25},{24,16},{25,1},{2,26},{3,... | collective-permute-start | bytes 3145736 | tf_op jit(solution)/shard_map/ppermute | solution.py:27
  54.1 18.1 %collective-permute-start.11 = (bf16[128,2560]{1,0:T(8,128)(2,1)}, bf16[128,2560]{1,0:T(8,128)(2,1)S(1)}, u32[]{:S(2)}, u32[]{:S(2)}) collective-permute-start(bf16[128,2560]{1,0:T(8,128)(2,1)} %collective-permute-done.9.refs_0_), channel_id=1, source_target_pairs={{0,32},{1,225},{32,64},{33,1},{64,96},{65,33},{96,128},{97,65},{12... | collective-permute-start | bytes 1966088 | tf_op jit(solution)/shard_map/ppermute | solution.py:27
  58.0 21.5 %collective-permute-start.18 = (bf16[96,4096]{1,0:T(8,128)(2,1)S(1)}, bf16[96,4096]{1,0:T(8,128)(2,1)S(1)}, u32[]{:S(2)}, u32[]{:S(2)}) collective-permute-start(bf16[96,4096]{1,0:T(8,128)(2,1)S(1)} %pad_maximum_fusion.refs_3_), channel_id=1, source_target_pairs={{0,8},{1,25},{8,16},{9,1},{16,24},{17,9},{24,0},{25,17},{2,10},{3,... | collective-permute-start | bytes 2359304 | tf_op jit(solution)/shard_map/ppermute | solution.py:27
  60.0 17.1 %collective-permute-start.14 = (bf16[128,2560]{1,0:T(8,128)(2,1)}, bf16[128,2560]{1,0:T(8,128)(2,1)S(1)}, u32[]{:S(2)}, u32[]{:S(2)}) collective-permute-start(bf16[128,2560]{1,0:T(8,128)(2,1)} %collective-permute-done.13.refs_1_), channel_id=1, source_target_pairs={{0,224},{1,33},{32,0},{33,65},{64,32},{65,97},{96,64},{97,129},{12... | collective-permute-start | bytes 1966088 | tf_op jit(solution)/shard_map/ppermute | solution.py:27
  61.2 2.9 %copy-start = (bf16[6656,512]{1,0:T(8,128)(2,1)S(1)}, bf16[6656,512]{1,0:T(8,128)(2,1)}, u32[]{:S(2)}) copy-start(bf16[6656,512]{1,0:T(8,128)(2,1)} %weights.1) | copy-start | bytes 20447236
  64.1 15.4 %slice-start.1 = ((s8[6815744]{0:T(1024)(128)(4,1)}), s8[4194304]{0:T(1024)(128)(4,1)S(1)}, s32[]{:S(2)}) async-start(s8[6815744]{0:T(1024)(128)(4,1)} %bitcast.15), calls=%async_computation.3 | async-start | bytes 8388608
  66.4 19.4 %copy-start.13 = (bf16[128,512]{1,0:T(8,128)(2,1)}, bf16[128,512]{1,0:T(8,128)(2,1)S(1)}, u32[]{:S(2)}) copy-start(bf16[128,512]{1,0:T(8,128)(2,1)S(1)} %get-tuple-element.35.base_own) | copy-start | bytes 393220
  72.2 17.0 %collective-permute-start.12 = (bf16[128,2560]{1,0:T(8,128)(2,1)S(1)}, bf16[128,2560]{1,0:T(8,128)(2,1)S(1)}, u32[]{:S(2)}, u32[]{:S(2)}) collective-permute-start(bf16[128,2560]{1,0:T(8,128)(2,1)S(1)} %collective-permute-done.11.refs_2_), channel_id=1, source_target_pairs={{0,32},{1,225},{32,64},{33,1},{64,96},{65,33},{96,128},{97,65},{12... | collective-permute-start | bytes 1966088 | tf_op jit(solution)/shard_map/ppermute | solution.py:27
  72.2 20.9 %collective-permute-start.21 = (bf16[128,4096]{1,0:T(8,128)(2,1)}, bf16[128,4096]{1,0:T(8,128)(2,1)S(1)}, u32[]{:S(2)}, u32[]{:S(2)}) collective-permute-start(bf16[128,4096]{1,0:T(8,128)(2,1)} %collective-permute-done.10.refs_5_), channel_id=1, source_target_pairs={{0,8},{1,25},{8,16},{9,1},{16,24},{17,9},{24,0},{25,17},{2,10},{3,... | collective-permute-start | bytes 3145736 | tf_op jit(solution)/shard_map/ppermute | solution.py:27
  72.5 20.6 %collective-permute-start.22 = (bf16[96,4096]{1,0:T(8,128)(2,1)S(1)}, bf16[96,4096]{1,0:T(8,128)(2,1)S(1)}, u32[]{:S(2)}, u32[]{:S(2)}) collective-permute-start(bf16[96,4096]{1,0:T(8,128)(2,1)S(1)} %pad_maximum_fusion.refs_3_), channel_id=1, source_target_pairs={{0,24},{1,9},{8,0},{9,17},{16,8},{17,25},{24,16},{25,1},{2,26},{3,... | collective-permute-start | bytes 2359304 | tf_op jit(solution)/shard_map/ppermute | solution.py:27
  77.1 16.8 %collective-permute-start.20 = (bf16[128,2560]{1,0:T(8,128)(2,1)S(1)}, bf16[128,2560]{1,0:T(8,128)(2,1)S(1)}, u32[]{:S(2)}, u32[]{:S(2)}) collective-permute-start(bf16[128,2560]{1,0:T(8,128)(2,1)S(1)} %collective-permute-done.14.refs_3_), channel_id=1, source_target_pairs={{0,224},{1,33},{32,0},{33,65},{64,32},{65,97},{96,64},{97,129},{12... | collective-permute-start | bytes 1966088 | tf_op jit(solution)/shard_map/ppermute | solution.py:27
  79.5 19.3 %collective-permute-start.19 = (bf16[96,4096]{1,0:T(8,128)(2,1)S(1)}, bf16[96,4096]{1,0:T(8,128)(2,1)S(1)}, u32[]{:S(2)}, u32[]{:S(2)}) collective-permute-start(bf16[96,4096]{1,0:T(8,128)(2,1)S(1)} %collective-permute-done.18.refs_4_), channel_id=1, source_target_pairs={{0,8},{1,25},{8,16},{9,1},{16,24},{17,9},{24,0},{25,17},{2,10},{3,... | collective-permute-start | bytes 2359304 | tf_op jit(solution)/shard_map/ppermute | solution.py:27
  89.2 11.8 %collective-permute-start.16 = (bf16[128,2560]{1,0:T(8,128)(2,1)S(1)}, bf16[128,2560]{1,0:T(8,128)(2,1)S(1)}, u32[]{:S(2)}, u32[]{:S(2)}) collective-permute-start(bf16[128,2560]{1,0:T(8,128)(2,1)S(1)} %collective-permute-done.12.refs_0_), channel_id=1, source_target_pairs={{0,32},{1,225},{32,64},{33,1},{64,96},{65,33},{96,128},{97,65},{12... | collective-permute-start | bytes 1966088 | tf_op jit(solution)/shard_map/ppermute | solution.py:27
  98.8 3.6 %copy-start.2 = (f32[288,576]{1,0:T(8,128)}, f32[288,576]{1,0:T(8,128)S(1)}, u32[]{:S(2)}) copy-start(f32[288,576]{1,0:T(8,128)S(1)} %get-tuple-element.45.far_b) | copy-start | bytes 1990660
  98.8 3.6 %copy-start.4 = (f32[256,576]{1,0:T(8,128)}, f32[256,576]{1,0:T(8,128)S(1)}, u32[]{:S(2)}) copy-start(f32[256,576]{1,0:T(8,128)S(1)} %get-tuple-element.44.far_a) | copy-start | bytes 1769476
  98.8 3.5 %copy-start.12 = (bf16[512,512]{1,0:T(8,128)(2,1)}, bf16[512,512]{1,0:T(8,128)(2,1)S(1)}, u32[]{:S(2)}) copy-start(bf16[512,512]{1,0:T(8,128)(2,1)S(1)} %get-tuple-element.48.base_near) | copy-start | bytes 1572868
  98.8 3.5 %copy-start.1 = (bf16[96,4096]{1,0:T(8,128)(2,1)}, bf16[96,4096]{1,0:T(8,128)(2,1)S(1)}, u32[]{:S(2)}) copy-start(bf16[96,4096]{1,0:T(8,128)(2,1)S(1)} %collective-permute-done.19.far) | copy-start | bytes 2359300
  101.0 1.4 %copy-start.3 = (bf16[128,2560]{1,0:T(8,128)(2,1)}, bf16[128,2560]{1,0:T(8,128)(2,1)S(1)}, u32[]{:S(2)}) copy-start(bf16[128,2560]{1,0:T(8,128)(2,1)S(1)} %collective-permute-done.16.a) | copy-start | bytes 1966084
  102.4 11.5 %all-to-all-start = ((f32[8,8,128]{2,1,0:T(8,128)}), f32[8,8,128]{2,1,0:T(8,128)S(1)}, u32[]{:S(2)}, u32[]{:S(2)}) async-start(f32[8,8,128]{2,1,0:T(8,128)} %bitcast.6), calls=%async_computation | async-start | bytes 65536 | tf_op jit(solution)/shard_map/all_to_all | solution.py:408
  106.9 22.6 %copy-start.17 = (bf16[32,64,512]{2,1,0:T(8,128)(2,1)S(1)}, bf16[32,64,512]{2,1,0:T(8,128)(2,1)}, u32[]{:S(2)}) copy-start(bf16[32,64,512]{2,1,0:T(8,128)(2,1)} %param.10) | copy-start | bytes 6291460
  106.9 22.6 %copy-start.19 = (s32[128,128]{1,0:T(8,128)S(1)}, s32[128,128]{1,0:T(8,128)}, u32[]{:S(2)}) copy-start(s32[128,128]{1,0:T(8,128)} %copy-done.18) | copy-start | bytes 196612
  113.9 6.9 %collective-permute-start.23 = (bf16[512,512]{1,0:T(8,128)(2,1)}, bf16[512,512]{1,0:T(8,128)(2,1)S(1)}, u32[]{:S(2)}, u32[]{:S(2)}) collective-permute-start(bf16[512,512]{1,0:T(8,128)(2,1)} %get-tuple-element.52), channel_id=1, source_target_pairs={{0,1},{1,0},{2,3},{3,2},{4,5},{5,4},{6,7},{7,6},{8,9},{9,8},{10,11... | collective-permute-start | bytes 1572872 | tf_op jit(solution)/shard_map/ppermute | solution.py:414
  115.1 14.4 %all-to-all-start.1 = ((bf16[32,8,128]{2,1,0:T(8,128)(2,1)}), bf16[32,8,128]{2,1,0:T(8,128)(2,1)S(1)}, u32[]{:S(2)}, u32[]{:S(2)}) async-start(bf16[32,8,128]{2,1,0:T(8,128)(2,1)} %broadcast_in_dim.2), calls=%async_computation.1 | async-start | bytes 131072 | tf_op jit(solution)/shard_map/all_to_all | solution.py:412
  120.8 1.0 copy-start.11
  122.0 8.1 %collective-permute-start.24 = (bf16[128,512]{1,0:T(8,128)(2,1)S(1)}, bf16[128,512]{1,0:T(8,128)(2,1)S(1)}, u32[]{:S(2)}, u32[]{:S(2)}) collective-permute-start(bf16[128,512]{1,0:T(8,128)(2,1)S(1)} %get-tuple-element.54), channel_id=1, source_target_pairs={{0,2},{2,4},{4,6},{6,0},{1,3},{3,5},{5,7},{7,1},{8,10},{10,12},{12... | collective-permute-start | bytes 393224 | tf_op jit(solution)/shard_map/ppermute | solution.py:420
  123.7 8.6 %collective-permute-start.25 = (bf16[128,512]{1,0:T(8,128)(2,1)S(1)}, bf16[128,512]{1,0:T(8,128)(2,1)S(1)}, u32[]{:S(2)}, u32[]{:S(2)}) collective-permute-start(bf16[128,512]{1,0:T(8,128)(2,1)S(1)} %get-tuple-element.55), channel_id=1, source_target_pairs={{0,4},{2,6},{4,0},{6,2},{1,5},{3,7},{5,1},{7,3},{8,12},{10,14},{12... | collective-permute-start | bytes 393224 | tf_op jit(solution)/shard_map/ppermute | solution.py:420
  126.4 6.0 %collective-permute-start.26 = (bf16[128,512]{1,0:T(8,128)(2,1)S(1)}, bf16[128,512]{1,0:T(8,128)(2,1)S(1)}, u32[]{:S(2)}, u32[]{:S(2)}) collective-permute-start(bf16[128,512]{1,0:T(8,128)(2,1)S(1)} %get-tuple-element.56), channel_id=1, source_target_pairs={{0,6},{2,0},{4,2},{6,4},{1,7},{3,1},{5,3},{7,5},{8,14},{10,8},{12,... | collective-permute-start | bytes 393224 | tf_op jit(solution)/shard_map/ppermute | solution.py:420
  129.5 2.9 %copy-start.16 = (s32[5]{0:T(128)S(1)}, s32[5]{0:T(128)}, u32[]{:S(2)}) copy-start(s32[5]{0:T(128)} %copy-done.15) | copy-start | bytes 64
